TPU v7x, 32 devices: a whole 2x2x4 slice. The times are simulated.
32 devices in a mesh: dp: 2 (over y), row: 4 (over z), col: 4 (over x, core).
Axes of the slice: x: 2, y: 2, z: 4, core: 2. Of those that a mesh axis runs over, the one named last changes fastest.
Arguments:
- act_in: bfloat16 [2048, 1024], P(('dp', 'col'), 'row'), may hold values from -8 to 8
- act_cot: bfloat16 [2048, 1024], P(('dp', 'col'), 'row'), may hold values from -6 to 6
- segments: int32 [2048], P(('dp', 'col')), may hold values from 0 to 7, as said below
- positions: int32 [2048], P(('dp', 'col')), may hold values from 0 to 382, as said below
- gains: float32 [2304], replicated, may hold values from 0.5 to 1.5
- gains_first: float32 [2304], replicated, may hold values from -32 to 32
- gains_second: float32 [2304], replicated, may hold values from 53.8624 to 861.7984
- query_weight: float32 [1024, 2048], P(('dp', 'col'), 'row'), may hold values from -0.1875 to 0.1875
- query_first: float32 [1024, 2048], P(('dp', 'col'), 'row'), may hold values from -4 to 4
- query_second: float32 [1024, 2048], P(('dp', 'col'), 'row'), may hold values from 4.847616 to 77.56186
- key_weight: float32 [1024, 1024], P(('dp', 'col'), 'row'), may hold values from -0.1875 to 0.1875
- key_first: float32 [1024, 1024], P(('dp', 'col'), 'row'), may hold values from -4 to 4
- key_second: float32 [1024, 1024], P(('dp', 'col'), 'row'), may hold values from 4.847616 to 77.56186
- value_weight: float32 [1024, 1024], P(('dp', 'col'), 'row'), may hold values from -0.1875 to 0.1875
- value_first: float32 [1024, 1024], P(('dp', 'col'), 'row'), may hold values from -32 to 32
- value_second: float32 [1024, 1024], P(('dp', 'col'), 'row'), may hold values from 53.8624 to 861.7984
- output_weight: float32 [1024, 2048], P(('dp', 'col'), 'row'), may hold values from -0.5 to 0.5
- output_first: float32 [1024, 2048], P(('dp', 'col'), 'row'), may hold values from -4 to 4
- output_second: float32 [1024, 2048], P(('dp', 'col'), 'row'), may hold values from 4.847616 to 77.56186
- gate_weight: float32 [1024, 3072], P('row', ('dp', 'col')), may hold values from -0.1875 to 0.1875
- gate_first: float32 [1024, 3072], P('row', ('dp', 'col')), may hold values from -10 to 10
- gate_second: float32 [1024, 3072], P('row', ('dp', 'col')), may hold values from 6.598144 to 105.570305
- up_weight: float32 [1024, 3072], P('row', ('dp', 'col')), may hold values from -0.1875 to 0.1875
- up_first: float32 [1024, 3072], P('row', ('dp', 'col')), may hold values from -10 to 10
- up_second: float32 [1024, 3072], P('row', ('dp', 'col')), may hold values from 6.598144 to 105.570305
- down_weight: float32 [1024, 3072], P('row', ('dp', 'col')), may hold values from -0.109375 to 0.109375
- down_first: float32 [1024, 3072], P('row', ('dp', 'col')), may hold values from -16 to 16
- down_second: float32 [1024, 3072], P('row', ('dp', 'col')), may hold values from 19.390465 to 310.24744
Outputs:
- act_out: bfloat16 [2048, 1024], P(('dp', 'col'), 'row')
- act_grad: float32 [2048, 1024], P(('dp', 'col'), 'row')
- gains_new: float32 [2304], replicated
- gains_first_new: float32 [2304], replicated
- gains_second_new: float32 [2304], replicated
- query_new: float32 [1024, 2048], P(('dp', 'col'), 'row')
- query_first_new: float32 [1024, 2048], P(('dp', 'col'), 'row')
- query_second_new: float32 [1024, 2048], P(('dp', 'col'), 'row')
- key_new: float32 [1024, 1024], P(('dp', 'col'), 'row')
- key_first_new: float32 [1024, 1024], P(('dp', 'col'), 'row')
- key_second_new: float32 [1024, 1024], P(('dp', 'col'), 'row')
- value_new: float32 [1024, 1024], P(('dp', 'col'), 'row')
- value_first_new: float32 [1024, 1024], P(('dp', 'col'), 'row')
- value_second_new: float32 [1024, 1024], P(('dp', 'col'), 'row')
- output_new: float32 [1024, 2048], P(('dp', 'col'), 'row')
- output_first_new: float32 [1024, 2048], P(('dp', 'col'), 'row')
- output_second_new: float32 [1024, 2048], P(('dp', 'col'), 'row')
- gate_new: float32 [1024, 3072], P('row', ('dp', 'col'))
- gate_first_new: float32 [1024, 3072], P('row', ('dp', 'col'))
- gate_second_new: float32 [1024, 3072], P('row', ('dp', 'col'))
- up_new: float32 [1024, 3072], P('row', ('dp', 'col'))
- up_first_new: float32 [1024, 3072], P('row', ('dp', 'col'))
- up_second_new: float32 [1024, 3072], P('row', ('dp', 'col'))
- down_new: float32 [1024, 3072], P('row', ('dp', 'col'))
- down_first_new: float32 [1024, 3072], P('row', ('dp', 'col'))
- down_second_new: float32 [1024, 3072], P('row', ('dp', 'col'))
Inputs may be any that keep to these rules, and one draw needn't show every extreme that they name: `segments`: within each sequence of 256 tokens the segment numbers start at 0, never fall, and a document holds at least 32 tokens (the last of a sequence may be cut). Within a segment the positions rise by one from token to token.
All inputs are finite; a program needn't handle non-finite values.
Results may differ from a plain program's by a relative error of at most 0.013.
The roundings to bfloat16 on the way count: a program that leaves them out, or rounds other values in their place, can miss the bound.
Values may be sent and summed in bfloat16 or wider, within the bound.
No kernel may reach another device: no remote copies, remote signals or barrier semaphores. Data moves between devices by JAX's collectives and lax.ppermute only.
A program may use at most 128 MiB of HBM per device.

v0:
```python
import jax
import jax.numpy as jnp
from jax import lax
from jax.sharding import PartitionSpec as P

D = 1024
HD = 128
STEP = 10


EPSILON = 1e-06
THETA_BASE = 1000000.0
BETA_FIRST = 0.9
BETA_SECOND = 0.95
ADAM_EPSILON = 1e-08
MATRIX_RATE = 0.04
MATRIX_DECAY = 0.1
GAIN_RATE = 0.5
MASK_VALUE = -1e30


def matmul(left, right):
    return jnp.dot(left, right, preferred_element_type=jnp.float32)


def matmul_nt(left, right):
    return lax.dot_general(
        left, right, (((1,), (1,)), ((), ())), preferred_element_type=jnp.float32
    )


def matmul_tn(left, right):
    return lax.dot_general(
        left, right, (((0,), (0,)), ((), ())), preferred_element_type=jnp.float32
    )


def rotary_tables(positions):
    half = HD // 2
    inverse = THETA_BASE ** (-(jnp.arange(half, dtype=jnp.float32) * 2.0 / HD))
    angle = positions.astype(jnp.float32)[..., None] * inverse
    return (jnp.cos(angle), jnp.sin(angle))


def rotate(values, cosine, sine):
    half = values.shape[-1] // 2
    first = values[..., :half]
    second = values[..., half:]
    cosine = cosine[..., None, :]
    sine = sine[..., None, :]
    return jnp.concatenate(
        [first * cosine - second * sine, second * cosine + first * sine], axis=-1
    )


def rotate_back(grads, cosine, sine):
    half = grads.shape[-1] // 2
    first = grads[..., :half]
    second = grads[..., half:]
    cosine = cosine[..., None, :]
    sine = sine[..., None, :]
    return jnp.concatenate(
        [first * cosine + second * sine, second * cosine - first * sine], axis=-1
    )


def head_norm(values, gain):
    factor = lax.rsqrt(jnp.mean(values * values, axis=-1, keepdims=True) + EPSILON)
    return (values * factor * gain, factor)


def head_norm_back(grads, values, factor, gain):
    inner = jnp.sum(grads * gain * values, axis=-1, keepdims=True)
    value_grad = (
        factor * gain * grads - values * (factor * factor * factor) * inner / values.shape[-1]
    )
    gain_grad = jnp.sum(grads * values * factor, axis=(0, 1))
    return (value_grad, gain_grad)


def masked_scores(queries, keys, allowed):
    length = queries.shape[0]
    grouped = queries.reshape(length, keys.shape[1], queries.shape[1] // keys.shape[1], HD)
    scores = jnp.einsum(
        "qgmd,kgd->gmqk", grouped, keys, preferred_element_type=jnp.float32
    ) * HD ** (-0.5)
    return jnp.where(allowed, scores, MASK_VALUE)


def adamw(weight, first, second, grad, rate, decay):
    first_new = BETA_FIRST * first + (1.0 - BETA_FIRST) * grad
    second_new = BETA_SECOND * second + (1.0 - BETA_SECOND) * grad * grad
    first_hat = first_new / (1.0 - BETA_FIRST**STEP)
    second_hat = second_new / (1.0 - BETA_SECOND**STEP)
    weight_new = weight - rate * (
        first_hat / (jnp.sqrt(second_hat) + ADAM_EPSILON) + decay * weight
    )
    return (weight_new, first_new, second_new)


def gather_width(values):
    return lax.all_gather(values, "row", axis=1, tiled=True)


def sum_width(terms):
    return lax.psum_scatter(terms, "row", scatter_dimension=1, tiled=True)


def stat_width(terms):
    return lax.psum(terms, "row")


def gather_tokens(values):
    return lax.all_gather(values, "col", axis=0, tiled=True)


def sum_tokens(terms):
    return lax.psum_scatter(terms, "col", scatter_dimension=0, tiled=True)


def sum_units(terms):
    return lax.psum_scatter(terms, "row", scatter_dimension=0, tiled=True)


def gather_units(values):
    return lax.all_gather(values, "row", axis=0, tiled=True)


def body(
    act_in,
    act_cot,
    segments,
    positions,
    gains,
    gains_first,
    gains_second,
    query_weight,
    query_first,
    query_second,
    key_weight,
    key_first,
    key_second,
    value_weight,
    value_first,
    value_second,
    output_weight,
    output_first,
    output_second,
    gate_weight,
    gate_first,
    gate_second,
    up_weight,
    up_first,
    up_second,
    down_weight,
    down_first,
    down_second,
):
    query_cols, key_cols, value_cols, output_cols = (
        lax.all_gather(query_weight.astype(jnp.bfloat16), ("dp", "col"), axis=0, tiled=True),
        lax.all_gather(key_weight.astype(jnp.bfloat16), ("dp", "col"), axis=0, tiled=True),
        lax.all_gather(value_weight.astype(jnp.bfloat16), ("dp", "col"), axis=0, tiled=True),
        lax.all_gather(output_weight.astype(jnp.bfloat16), ("dp", "col"), axis=0, tiled=True),
    )
    gate_cols, up_cols, down_cols = (
        lax.all_gather(gate_weight.astype(jnp.bfloat16), "dp", axis=1, tiled=True),
        lax.all_gather(up_weight.astype(jnp.bfloat16), "dp", axis=1, tiled=True),
        lax.all_gather(down_weight.astype(jnp.bfloat16), "dp", axis=1, tiled=True),
    )
    row_index = lax.axis_index("row")
    width_part = act_in.shape[1]
    unit_part = gate_cols.shape[1]
    gain_in = gains[:D]
    gain_mid = lax.dynamic_slice_in_dim(gains, D + row_index * width_part, width_part)
    gain_query = gains[2 * D : 2 * D + HD]
    gain_key = gains[2 * D + HD :]
    inputs = gather_width(act_in).astype(jnp.float32)
    length = inputs.shape[0]
    scale_in = lax.rsqrt(jnp.mean(inputs * inputs, axis=-1, keepdims=True) + EPSILON)
    normed = (inputs * scale_in * gain_in).astype(jnp.bfloat16)
    query_heads = matmul(normed, query_cols).reshape(length, -1, HD)
    key_heads = matmul(normed, key_cols).reshape(length, -1, HD)
    values = matmul(normed, value_cols).astype(jnp.bfloat16).reshape(length, -1, HD)
    heads_here = query_heads.shape[1]
    groups_here = key_heads.shape[1]
    group_size = heads_here // groups_here
    query_normed, query_factor = head_norm(query_heads, gain_query)
    key_normed, key_factor = head_norm(key_heads, gain_key)
    cosine, sine = rotary_tables(positions)
    queries = rotate(query_normed, cosine, sine).astype(jnp.bfloat16)
    keys = rotate(key_normed, cosine, sine).astype(jnp.bfloat16)
    index = jnp.arange(length)
    allowed = (segments[:, None] == segments[None, :]) & (index[None, :] <= index[:, None])
    scores = masked_scores(queries, keys, allowed)
    peak = jnp.max(scores, axis=-1, keepdims=True)
    log_total = peak + jnp.log(jnp.sum(jnp.exp(scores - peak), axis=-1, keepdims=True))
    probs = jnp.exp(scores - log_total).astype(jnp.bfloat16)
    context = jnp.einsum("gmqk,kgd->qgmd", probs, values, preferred_element_type=jnp.float32)
    context = context.reshape(length, heads_here * HD).astype(jnp.bfloat16)
    resid = act_in.astype(jnp.float32) + sum_width(matmul_nt(context, output_cols))
    square_sum = stat_width(jnp.sum(resid * resid, axis=-1))
    scale_mid = lax.rsqrt(square_sum / D + EPSILON)[:, None]
    mid_in = (resid * scale_mid * gain_mid).astype(jnp.bfloat16)
    mid_all = gather_tokens(mid_in)
    joined = jnp.concatenate([gate_cols, up_cols], axis=1)
    gate_up = sum_units(matmul(mid_all, joined))
    gate = gate_up[:, :unit_part]
    upward = gate_up[:, unit_part:]
    sigmoid = jax.nn.sigmoid(gate)
    hidden = (gate * sigmoid * upward).astype(jnp.bfloat16)
    hidden_all = gather_units(hidden)
    act_out = (resid + sum_tokens(matmul_nt(hidden_all, down_cols))).astype(jnp.bfloat16)
    cot_all = gather_tokens(act_cot)
    down_total = matmul_tn(cot_all, hidden_all)
    hidden_grad = sum_units(matmul(cot_all, down_cols))
    gate_grad = hidden_grad * upward * sigmoid * (1.0 + gate * (1.0 - sigmoid))
    upward_grad = hidden_grad * gate * sigmoid
    pre_grad = jnp.concatenate([gate_grad, upward_grad], axis=1).astype(jnp.bfloat16)
    pre_all = gather_units(pre_grad)
    joined_grad = matmul_tn(mid_all, pre_all)
    mid_grad = sum_tokens(matmul_nt(pre_all, joined))
    inner_mid = stat_width(jnp.sum(mid_grad * gain_mid * resid, axis=-1))[:, None]
    resid_grad = (
        act_cot.astype(jnp.float32)
        + scale_mid * gain_mid * mid_grad
        - resid * (scale_mid * scale_mid * scale_mid) * inner_mid / D
    )
    gain_mid_grad = jnp.sum(mid_grad * resid * scale_mid, axis=0)
    branch_grad = gather_width(resid_grad.astype(jnp.bfloat16))
    output_total = matmul_tn(branch_grad, context)
    context_grad = (
        matmul(branch_grad, output_cols)
        .astype(jnp.bfloat16)
        .reshape(length, groups_here, group_size, HD)
    )
    scores = masked_scores(queries, keys, allowed)
    weights_full = jnp.exp(scores - log_total)
    prob_grad = jnp.einsum(
        "qgmd,kgd->gmqk", context_grad, values, preferred_element_type=jnp.float32
    )
    delta = jnp.sum(weights_full * prob_grad, axis=-1, keepdims=True)
    score_grad = (weights_full * (prob_grad - delta)).astype(jnp.bfloat16)
    grouped = queries.reshape(length, groups_here, group_size, HD)
    query_grad = jnp.einsum("gmqk,kgd->qgmd", score_grad, keys, preferred_element_type=jnp.float32)
    query_grad = query_grad.reshape(length, heads_here, HD) * HD ** (-0.5)
    key_grad = jnp.einsum(
        "gmqk,qgmd->kgd", score_grad, grouped, preferred_element_type=jnp.float32
    ) * HD ** (-0.5)
    value_grad = jnp.einsum(
        "gmqk,qgmd->kgd",
        weights_full.astype(jnp.bfloat16),
        context_grad,
        preferred_element_type=jnp.float32,
    )
    query_grad, query_gain_grad = head_norm_back(
        rotate_back(query_grad, cosine, sine), query_heads, query_factor, gain_query
    )
    key_grad, key_gain_grad = head_norm_back(
        rotate_back(key_grad, cosine, sine), key_heads, key_factor, gain_key
    )
    query_grad = query_grad.reshape(length, -1).astype(jnp.bfloat16)
    key_grad = key_grad.reshape(length, -1).astype(jnp.bfloat16)
    value_grad = value_grad.reshape(length, -1).astype(jnp.bfloat16)
    query_total = matmul_tn(normed, query_grad)
    key_total = matmul_tn(normed, key_grad)
    value_total = matmul_tn(normed, value_grad)
    normed_grad = (
        matmul_nt(query_grad, query_cols)
        + matmul_nt(key_grad, key_cols)
        + matmul_nt(value_grad, value_cols)
    )
    inner_in = jnp.sum(normed_grad * gain_in * inputs, axis=-1, keepdims=True)
    input_terms = (
        scale_in * gain_in * normed_grad - inputs * (scale_in * scale_in * scale_in) * inner_in / D
    )
    gain_in_grad = jnp.sum(normed_grad * inputs * scale_in, axis=0)
    act_grad = resid_grad + sum_width(input_terms)
    mid_place = lax.dynamic_update_slice_in_dim(
        jnp.zeros((D,), jnp.float32), gain_mid_grad, row_index * width_part, 0
    )
    gains_grad = lax.psum(
        jnp.concatenate([gain_in_grad, mid_place, query_gain_grad, key_gain_grad]),
        ("dp", "row", "col"),
    )
    query_sum, key_sum, value_sum, output_sum = (
        lax.psum_scatter(query_total, ("dp", "col"), scatter_dimension=0, tiled=True),
        lax.psum_scatter(key_total, ("dp", "col"), scatter_dimension=0, tiled=True),
        lax.psum_scatter(value_total, ("dp", "col"), scatter_dimension=0, tiled=True),
        lax.psum_scatter(output_total, ("dp", "col"), scatter_dimension=0, tiled=True),
    )
    gate_sum, up_sum, down_sum = (
        lax.psum_scatter(joined_grad[:, :unit_part], "dp", scatter_dimension=1, tiled=True),
        lax.psum_scatter(joined_grad[:, unit_part:], "dp", scatter_dimension=1, tiled=True),
        lax.psum_scatter(down_total, "dp", scatter_dimension=1, tiled=True),
    )
    gains_new, gains_first_new, gains_second_new = adamw(
        gains, gains_first, gains_second, gains_grad, GAIN_RATE, 0.0
    )
    query_new, query_first_new, query_second_new = adamw(
        query_weight, query_first, query_second, query_sum, MATRIX_RATE, MATRIX_DECAY
    )
    key_new, key_first_new, key_second_new = adamw(
        key_weight, key_first, key_second, key_sum, MATRIX_RATE, MATRIX_DECAY
    )
    value_new, value_first_new, value_second_new = adamw(
        value_weight, value_first, value_second, value_sum, MATRIX_RATE, MATRIX_DECAY
    )
    output_new, output_first_new, output_second_new = adamw(
        output_weight, output_first, output_second, output_sum, MATRIX_RATE, MATRIX_DECAY
    )
    gate_new, gate_first_new, gate_second_new = adamw(
        gate_weight, gate_first, gate_second, gate_sum, MATRIX_RATE, MATRIX_DECAY
    )
    up_new, up_first_new, up_second_new = adamw(
        up_weight, up_first, up_second, up_sum, MATRIX_RATE, MATRIX_DECAY
    )
    down_new, down_first_new, down_second_new = adamw(
        down_weight, down_first, down_second, down_sum, MATRIX_RATE, MATRIX_DECAY
    )
    return (
        act_out,
        act_grad,
        gains_new,
        gains_first_new,
        gains_second_new,
        query_new,
        query_first_new,
        query_second_new,
        key_new,
        key_first_new,
        key_second_new,
        value_new,
        value_first_new,
        value_second_new,
        output_new,
        output_first_new,
        output_second_new,
        gate_new,
        gate_first_new,
        gate_second_new,
        up_new,
        up_first_new,
        up_second_new,
        down_new,
        down_first_new,
        down_second_new,
    )


def solution(mesh):
    return jax.shard_map(
        body,
        mesh=mesh,
        in_specs=(
            P(("dp", "col"), "row"),
            P(("dp", "col"), "row"),
            P(("dp", "col")),
            P(("dp", "col")),
            P(),
            P(),
            P(),
            P(("dp", "col"), "row"),
            P(("dp", "col"), "row"),
            P(("dp", "col"), "row"),
            P(("dp", "col"), "row"),
            P(("dp", "col"), "row"),
            P(("dp", "col"), "row"),
            P(("dp", "col"), "row"),
            P(("dp", "col"), "row"),
            P(("dp", "col"), "row"),
            P(("dp", "col"), "row"),
            P(("dp", "col"), "row"),
            P(("dp", "col"), "row"),
            P("row", ("dp", "col")),
            P("row", ("dp", "col")),
            P("row", ("dp", "col")),
            P("row", ("dp", "col")),
            P("row", ("dp", "col")),
            P("row", ("dp", "col")),
            P("row", ("dp", "col")),
            P("row", ("dp", "col")),
            P("row", ("dp", "col")),
        ),
        out_specs=(
            P(("dp", "col"), "row"),
            P(("dp", "col"), "row"),
            P(),
            P(),
            P(),
            P(("dp", "col"), "row"),
            P(("dp", "col"), "row"),
            P(("dp", "col"), "row"),
            P(("dp", "col"), "row"),
            P(("dp", "col"), "row"),
            P(("dp", "col"), "row"),
            P(("dp", "col"), "row"),
            P(("dp", "col"), "row"),
            P(("dp", "col"), "row"),
            P(("dp", "col"), "row"),
            P(("dp", "col"), "row"),
            P(("dp", "col"), "row"),
            P("row", ("dp", "col")),
            P("row", ("dp", "col")),
            P("row", ("dp", "col")),
            P("row", ("dp", "col")),
            P("row", ("dp", "col")),
            P("row", ("dp", "col")),
            P("row", ("dp", "col")),
            P("row", ("dp", "col")),
            P("row", ("dp", "col")),
        ),
        check_vma=False,
    )
```

profile of v0, /device:TPU:0, one launch (start us, length us, event | category | flops | bytes accessed | tf_op | source)
XLA Modules:
  0.0 691.3 jit_solution(16555361321953669372)
XLA Ops:
  12.2 17.6 %all_gather.39 = bf16[256,1024]{1,0:T(8,128)(2,1)S(1)} all-gather(bf16[256,256]{1,0:T(8,128)(2,1)} %param.28), channel_id=1, replica_groups=mesh['dp'=2,'row'=4,'col'=4] {'row'}, dimensions={1}, use_global_device_ids=true | all-gather | bytes 655360 | tf_op jit(solution)/shard_map/all_gather | solution.py:102
  30.6 9.9 %all_gather.41 = bf16[1024,256]{1,0:T(8,128)(2,1)S(1)} all-gather(bf16[128,256]{1,0:T(8,128)(2,1)S(1)} %convert_element_type.94), channel_id=1, replica_groups=mesh['dp'=2,'row'=4,'col'=4] {'dp','col'}, dimensions={0}, use_global_device_ids=true | all-gather | bytes 589824 | tf_op jit(solution)/shard_map/all_gather | solution.py:161
  42.2 10.4 %all_gather.40 = bf16[1024,256]{1,0:T(8,128)(2,1)S(1)} all-gather(bf16[128,256]{1,0:T(8,128)(2,1)S(1)} %convert_element_type.92), channel_id=1, replica_groups=mesh['dp'=2,'row'=4,'col'=4] {'dp','col'}, dimensions={0}, use_global_device_ids=true | all-gather | bytes 589824 | tf_op jit(solution)/shard_map/all_gather | solution.py:162
  59.2 4.6 all-gather.7.cloned.1.call-done
  66.6 7.8 %all_gather.48 = bf16[256,768]{1,0:T(8,128)(2,1)S(1)} all-gather(bf16[256,384]{1,0:T(8,128)(2,1)S(1)} %convert_element_type.106), channel_id=1, replica_groups=mesh['dp'=2,'row'=4,'col'=4] {'dp'}, dimensions={1}, use_global_device_ids=true | all-gather | bytes 589824 | tf_op jit(solution)/shard_map/all_gather | solution.py:168
  74.4 7.1 %all_gather.49 = bf16[1024,256]{1,0:T(8,128)(2,1)S(1)} all-gather(bf16[256,256]{1,0:T(8,128)(2,1)S(1)} %copy-done.47), channel_id=1, replica_groups=mesh['dp'=2,'row'=4,'col'=4] {'col'}, dimensions={0}, use_global_device_ids=true | all-gather | bytes 655360 | tf_op jit(solution)/shard_map/all_gather | solution.py:114
  86.2 7.8 %all_gather.45 = bf16[256,768]{1,0:T(8,128)(2,1)S(1)} all-gather(bf16[256,384]{1,0:T(8,128)(2,1)S(1)} %convert_element_type.103), channel_id=1, replica_groups=mesh['dp'=2,'row'=4,'col'=4] {'dp'}, dimensions={1}, use_global_device_ids=true | all-gather | bytes 589824 | tf_op jit(solution)/shard_map/all_gather | solution.py:166
  94.0 7.0 %all_gather.46 = bf16[256,768]{1,0:T(8,128)(2,1)S(1)} all-gather(bf16[256,384]{1,0:T(8,128)(2,1)S(1)} %convert_element_type.104), channel_id=1, replica_groups=mesh['dp'=2,'row'=4,'col'=4] {'dp'}, dimensions={1}, use_global_device_ids=true | all-gather | bytes 589824 | tf_op jit(solution)/shard_map/all_gather | solution.py:167
  102.2 12.2 %psum.21 = f32[256]{0:T(256)S(1)} all-reduce(f32[256]{0:T(256)S(1)} %get-tuple-element.58), channel_id=1, replica_groups=mesh['dp'=2,'row'=4,'col'=4] {'row'}, use_global_device_ids=true, to_apply=%region_7.8 | all-reduce | flops 256 | bytes 2048 | tf_op jit(solution)/shard_map/psum | solution.py:110
  115.8 6.6 all_gather.44
  126.9 28.4 %reduce-scatter.20.cloned.1.call-done = f32[256,768]{1,0:T(8,128)} async-done(((f32[1024,768]{1,0:T(8,128)}), f32[256,768]{1,0:T(8,128)}) %reduce-scatter.20.cloned.1.call-update) | async-done | bytes 786448 | tf_op jit(solution)/shard_map/reduce_scatter | solution.py:122
  155.3 113.1 %reduce-scatter.16.cloned.1.call-done = f32[256,1536]{1,0:T(8,128)} async-done(((f32[1024,1536]{1,0:T(8,128)}), f32[256,1536]{1,0:T(8,128)}) %reduce-scatter.16.cloned.1.call-update) | async-done | bytes 1572880 | tf_op jit(solution)/shard_map/reduce_scatter | solution.py:122
  272.9 63.4 %all-gather.11.cloned.1.call-done = bf16[1024,1536]{1,0:T(8,128)(2,1)} async-done(((bf16[256,1536]{1,0:T(8,128)(2,1)}), bf16[1024,1536]{1,0:T(8,128)(2,1)}) %all-gather.11.cloned.1.call-update) | async-done | bytes 3145744 | tf_op jit(solution)/shard_map/all_gather | solution.py:126
  340.3 34.0 %all-gather.9.cloned.1.call-done = bf16[1024,768]{1,0:T(8,128)(2,1)} async-done(((bf16[256,768]{1,0:T(8,128)(2,1)}), bf16[1024,768]{1,0:T(8,128)(2,1)}) %all-gather.9.cloned.1.call-update) | async-done | bytes 1572880 | tf_op jit(solution)/shard_map/all_gather | solution.py:126
  387.1 13.7 %reduce-scatter.22.cloned.1.call-done = f32[256,256]{1,0:T(8,128)} async-done(((f32[1024,256]{1,0:T(8,128)}), f32[256,256]{1,0:T(8,128)}) %reduce-scatter.22.cloned.1.call-update) | async-done | bytes 262160 | tf_op jit(solution)/shard_map/reduce_scatter | solution.py:118
  402.4 11.7 %psum.22 = f32[256]{0:T(256)S(1)} all-reduce(f32[256]{0:T(256)S(1)} %get-tuple-element.29), channel_id=1, replica_groups=mesh['dp'=2,'row'=4,'col'=4] {'row'}, use_global_device_ids=true, to_apply=%region_13.14 | all-reduce | flops 256 | bytes 2048 | tf_op jit(solution)/shard_map/psum | solution.py:110
  414.1 14.1 %reduce-scatter.18.cloned.1.call-done = f32[256,256]{1,0:T(8,128)} async-done(((f32[1024,256]{1,0:T(8,128)}), f32[256,256]{1,0:T(8,128)}) %reduce-scatter.18.cloned.1.call-update) | async-done | bytes 262160 | tf_op jit(solution)/shard_map/reduce_scatter | solution.py:118
  430.2 15.7 %all_gather.51 = bf16[256,1024]{1,0:T(8,128)(2,1)S(1)} all-gather(bf16[256,256]{1,0:T(8,128)(2,1)S(1)} %get-tuple-element.56), channel_id=1, replica_groups=mesh['dp'=2,'row'=4,'col'=4] {'row'}, dimensions={1}, use_global_device_ids=true | all-gather | bytes 655360 | tf_op jit(solution)/shard_map/all_gather | solution.py:102
  471.5 15.7 %reduce-scatter.34.cloned.1.call-done = f32[256,384]{1,0:T(8,128)} async-done(((f32[256,768]{1,0:T(8,128)}), f32[256,384]{1,0:T(8,128)}) %reduce-scatter.34.cloned.1.call-update) | async-done | bytes 393232 | tf_op jit(solution)/shard_map/reduce_scatter | solution.py:292
  489.8 39.5 %psum.23 = f32[2304]{0:T(1024)S(1)} all-reduce(f32[2304]{0:T(1024)S(1)} %pad_maximum_fusion.6), channel_id=1, replica_groups=mesh['dp'=2,'row'=4,'col'=4] {'dp','row','col'}, use_global_device_ids=true, to_apply=%region_25.26 | all-reduce | flops 2304 | bytes 18432 | tf_op jit(solution)/shard_map/psum | solution.py:281
  531.8 34.0 %reduce-scatter.28.cloned.1.call-done = f32[128,256]{1,0:T(8,128)} async-done(((f32[1024,256]{1,0:T(8,128)}), f32[128,256]{1,0:T(8,128)}) %reduce-scatter.28.cloned.1.call-update) | async-done | bytes 131088 | tf_op jit(solution)/shard_map/reduce_scatter | solution.py:287
  567.5 27.6 %reduce-scatter.24.cloned.1.call-done = f32[256,256]{1,0:T(8,128)} async-done(((f32[256,1024]{1,0:T(8,128)}), f32[256,256]{1,0:T(8,128)}) %reduce-scatter.24.cloned.1.call-update) | async-done | bytes 262160 | tf_op jit(solution)/shard_map/reduce_scatter | solution.py:106
  596.7 41.7 %reduce-scatter.32.cloned.1.call-done = f32[128,512]{1,0:T(8,128)} async-done(((f32[1024,512]{1,0:T(8,128)}), f32[128,512]{1,0:T(8,128)}) %reduce-scatter.32.cloned.1.call-update) | async-done | bytes 262160 | tf_op jit(solution)/shard_map/reduce_scatter | solution.py:289
  640.4 42.4 %reduce-scatter.26.cloned.1.call-done = f32[128,512]{1,0:T(8,128)} async-done(((f32[1024,512]{1,0:T(8,128)}), f32[128,512]{1,0:T(8,128)}) %reduce-scatter.26.cloned.1.call-update) | async-done | bytes 262160 | tf_op jit(solution)/shard_map/reduce_scatter | solution.py:286
  (303 shorter events, 90.4 us)
Async XLA Ops:
  7.2 46.8 %all-gather.5.cloned.1.call-start = ((), (), s32[]{:S(2)}) async-start(), calls=%async_computation.13 | async-start | bytes 1179648 | tf_op jit(solution)/shard_map/all_gather | solution.py:160
  8.9 54.9 %all-gather.7.cloned.1.call-start = ((), (), s32[]{:S(2)}) async-start(), calls=%async_computation.14 | async-start | bytes 1179648 | tf_op jit(solution)/shard_map/all_gather | solution.py:163
  10.7 90.5 %reduce-scatter.14.cloned.1.call-start = ((), (), s32[]{:S(2)}) async-start(), calls=%async_computation.15 | async-start | bytes 1310720 | tf_op jit(solution)/shard_map/reduce_scatter | solution.py:106
  66.6 88.7 %reduce-scatter.20.cloned.1.call-start = ((), (), s32[]{:S(2)}) async-start(), calls=%async_computation.19 | async-start | bytes 3932160 | tf_op jit(solution)/shard_map/reduce_scatter | solution.py:122
  84.7 183.7 %reduce-scatter.16.cloned.1.call-start = ((), (), s32[]{:S(2)}) async-start(), calls=%async_computation.16 | async-start | bytes 7864320 | tf_op jit(solution)/shard_map/reduce_scatter | solution.py:122
  126.8 209.5 %all-gather.11.cloned.1.call-start = ((), (), s32[]{:S(2)}) async-start(), calls=%async_computation.20 | async-start | bytes 3932160 | tf_op jit(solution)/shard_map/all_gather | solution.py:126
  272.1 102.2 %all-gather.9.cloned.1.call-start = ((), (), s32[]{:S(2)}) async-start(), calls=%async_computation.17 | async-start | bytes 1966080 | tf_op jit(solution)/shard_map/all_gather | solution.py:126
  272.9 127.9 %reduce-scatter.22.cloned.1.call-start = ((), (), s32[]{:S(2)}) async-start(), calls=%async_computation.21 | async-start | bytes 1310720 | tf_op jit(solution)/shard_map/reduce_scatter | solution.py:118
  340.2 88.0 %reduce-scatter.18.cloned.1.call-start = ((), (), s32[]{:S(2)}) async-start(), calls=%async_computation.18 | async-start | bytes 1310720 | tf_op jit(solution)/shard_map/reduce_scatter | solution.py:118
  377.5 89.4 %reduce-scatter.38.cloned.1.call-start = ((), (), s32[]{:S(2)}) async-start(), calls=%async_computation.29 | async-start | bytes 1179648 | tf_op jit(solution)/shard_map/reduce_scatter | solution.py:294
  380.3 88.9 %reduce-scatter.36.cloned.1.call-start = ((), (), s32[]{:S(2)}) async-start(), calls=%async_computation.28 | async-start | bytes 1179648 | tf_op jit(solution)/shard_map/reduce_scatter | solution.py:293
  385.0 102.3 %reduce-scatter.34.cloned.1.call-start = ((), (), s32[]{:S(2)}) async-start(), calls=%async_computation.27 | async-start | bytes 1179648 | tf_op jit(solution)/shard_map/reduce_scatter | solution.py:292
  387.0 143.0 %reduce-scatter.30.cloned.1.call-start = ((), (), s32[]{:S(2)}) async-start(), calls=%async_computation.25 | async-start | bytes 1179648 | tf_op jit(solution)/shard_map/reduce_scatter | solution.py:288
  451.3 114.5 %reduce-scatter.28.cloned.1.call-start = ((), (), s32[]{:S(2)}) async-start(), calls=%async_computation.24 | async-start | bytes 1179648 | tf_op jit(solution)/shard_map/reduce_scatter | solution.py:287
  458.1 137.0 %reduce-scatter.24.cloned.1.call-start = ((), (), s32[]{:S(2)}) async-start(), calls=%async_computation.22 | async-start | bytes 1310720 | tf_op jit(solution)/shard_map/reduce_scatter | solution.py:106
  462.9 175.6 %reduce-scatter.32.cloned.1.call-start = ((), (), s32[]{:S(2)}) async-start(), calls=%async_computation.26 | async-start | bytes 2359296 | tf_op jit(solution)/shard_map/reduce_scatter | solution.py:289
  464.8 218.0 %reduce-scatter.26.cloned.1.call-start = ((), (), s32[]{:S(2)}) async-start(), calls=%async_computation.23 | async-start | bytes 2359296 | tf_op jit(solution)/shard_map/reduce_scatter | solution.py:286
  471.5 123.5 %copy-start.40 = (f32[256,256]{1,0:T(8,128)S(1)}, f32[256,256]{1,0:T(8,128)}, u32[]{:S(2)}) copy-start(f32[256,256]{1,0:T(8,128)} %get-tuple-element.57) | copy-start | bytes 786436
  471.5 167.0 %copy-start.37 = (f32[128,512]{1,0:T(8,128)S(1)}, f32[128,512]{1,0:T(8,128)}, u32[]{:S(2)}) copy-start(f32[128,512]{1,0:T(8,128)} %param.44) | copy-start | bytes 786436
  471.5 167.0 %copy-start.56 = (f32[128,512]{1,0:T(8,128)S(1)}, f32[128,512]{1,0:T(8,128)}, u32[]{:S(2)}) copy-start(f32[128,512]{1,0:T(8,128)} %param.45) | copy-start | bytes 786436
  471.5 166.9 %copy-start.57 = (f32[128,512]{1,0:T(8,128)S(1)}, f32[128,512]{1,0:T(8,128)}, u32[]{:S(2)}) copy-start(f32[128,512]{1,0:T(8,128)} %param.46) | copy-start | bytes 786436
  529.9 152.9 %copy-start.38 = (f32[128,512]{1,0:T(8,128)S(1)}, f32[128,512]{1,0:T(8,128)}, u32[]{:S(2)}) copy-start(f32[128,512]{1,0:T(8,128)} %param.35) | copy-start | bytes 786436
  529.9 152.9 %copy-start.58 = (f32[128,512]{1,0:T(8,128)S(1)}, f32[128,512]{1,0:T(8,128)}, u32[]{:S(2)}) copy-start(f32[128,512]{1,0:T(8,128)} %param.36) | copy-start | bytes 786436
  529.9 152.9 %copy-start.59 = (f32[128,512]{1,0:T(8,128)S(1)}, f32[128,512]{1,0:T(8,128)}, u32[]{:S(2)}) copy-start(f32[128,512]{1,0:T(8,128)} %param.37) | copy-start | bytes 786436
  (76 other events, 1274.4 us)
Sparse Core Ops, SparseCore 0:
  10.5 26.5 all-gather.4
  39.6 24.2 all-gather.6
  66.7 27.1 reduce-scatter.13
  96.1 59.1 reduce-scatter.19
  157.5 110.7 reduce-scatter.15
  272.3 64.0 all-gather.10
  338.5 35.7 all-gather.8
  377.0 23.7 reduce-scatter.21
  403.3 24.8 reduce-scatter.17
  430.4 17.4 reduce-scatter.37
  450.1 17.4 reduce-scatter.35
  469.8 17.4 reduce-scatter.33
  490.4 36.0 reduce-scatter.29
  529.6 36.1 reduce-scatter.27
  567.9 27.1 reduce-scatter.23
  598.5 39.8 reduce-scatter.31
  641.6 41.1 reduce-scatter.25
where the time goes:
time: 692 us; the launch traced here: 691 us
  waiting for transfers between devices  434 us (63%)
  blocking collectives  153 us (22%)
  other arithmetic  39.7 us (6%)
  matrix products  35.4 us (5%)
  between operations  15.1 us (2%)
  local copies, waits for them, and re-layouts  13.3 us (2%)
    reduce_scatter x2, waiting for transfers between devices, sum_units(): return lax.psum_scatter(terms, 'row', scatter_dimension=0, tiled=True)  141 us
    all_gather x2, waiting for transfers between devices, gather_units(): return lax.all_gather(values, 'row', axis=0, tiled=True)  97.4 us
    reduce_scatter x1, waiting for transfers between devices, body(): lax.psum_scatter(query_total, ('dp', 'col'), scatter_dimension=0, tiled=T...  42.4 us
    reduce_scatter x1, waiting for transfers between devices, body(): lax.psum_scatter(output_total, ('dp', 'col'), scatter_dimension=0, tiled=...  41.7 us
    psum x1, blocking collectives, body(): lax.psum(jnp.concatenate([gain_in_grad, mid_place, query_gain_grad, key_g...  39.5 us
    reduce_scatter x1, waiting for transfers between devices, body(): lax.psum_scatter(key_total, ('dp', 'col'), scatter_dimension=0, tiled=True)  34 us
    all_gather x2, blocking collectives, gather_width(): return lax.all_gather(values, 'row', axis=1, tiled=True)  33.2 us
    reduce_scatter x2, waiting for transfers between devices, sum_tokens(): return lax.psum_scatter(terms, 'col', scatter_dimension=0, tiled=True)  27.8 us
  transfers between devices with their start and end apart: 17, of which 12 were waited for; matrix products, arithmetic and copies ran while one was open for 11% of the time, Pallas kernels for 0%

commit v1 on v0

v1 whole, which is shorter than its diff:
```python
import functools

import jax
import jax.numpy as jnp
from jax import lax
from jax.experimental import pallas as pl
from jax.experimental.pallas import tpu as pltpu
from jax.sharding import PartitionSpec as P

D = 1024
HD = 128
STEP = 10

EPSILON = 1e-06
THETA_BASE = 1000000.0
BETA_FIRST = 0.9
BETA_SECOND = 0.95
ADAM_EPSILON = 1e-08
MATRIX_RATE = 0.04
MATRIX_DECAY = 0.1
GAIN_RATE = 0.5
MASK_VALUE = -1e30
LANE = 128
BLOCKS = D // LANE
PLANE = ("dp", "col")
F32 = jnp.float32
BF16 = jnp.bfloat16


def mm(left, right):
    return jnp.dot(left, right, preferred_element_type=F32)


def mm_nt(left, right):
    return lax.dot_general(left, right, (((1,), (1,)), ((), ())), preferred_element_type=F32)


def mm_tn(left, right):
    return lax.dot_general(left, right, (((0,), (0,)), ((), ())), preferred_element_type=F32)


def lanes(block):
    return pl.ds(pl.multiple_of(block * LANE, LANE), LANE)


def rows_of(block, size):
    return pl.ds(pl.multiple_of(block * size, size), size)


def call(kernel, outs, *args, scalars=0, scratch=(), flops=1e8, limit=32):
    vmem = pl.BlockSpec(memory_space=pltpu.VMEM)
    smem = pl.BlockSpec(memory_space=pltpu.SMEM)
    moved = sum(a.size * a.dtype.itemsize for a in list(args) + list(outs))
    return pl.pallas_call(
        kernel,
        out_shape=list(outs),
        in_specs=[smem] * scalars + [vmem] * (len(args) - scalars),
        out_specs=[vmem] * len(outs),
        scratch_shapes=list(scratch),
        compiler_params=pltpu.CompilerParams(vmem_limit_bytes=limit << 20),
        cost_estimate=pl.CostEstimate(flops=int(flops), bytes_accessed=int(moved), transcendentals=0),
    )(*args)


def shape(dims, dtype):
    return jax.ShapeDtypeStruct(tuple(dims), dtype)


def attend_kernel(place, x_ref, wz_ref, wo_ref, g1_ref, gq_ref, gk_ref, cos_ref, sin_ref, segc_ref, segr_ref,
                  ctx_ref, prob_ref, q_ref, k_ref, v_ref, raw_ref, norm_ref):
    z = place[0]
    x = x_ref[...].astype(F32)
    r1 = lax.rsqrt(jnp.mean(x * x, axis=-1, keepdims=True) + EPSILON)
    for j in range(BLOCKS):
        b = place[1 + j]
        block = x_ref[:, lanes(b ^ (2 * z))].astype(F32)
        norm_ref[:, j * LANE:(j + 1) * LANE] = (block * r1 * g1_ref[:, lanes(b)]).astype(BF16)
    half = D // 2
    qkv = mm(norm_ref[:, :half], wz_ref[...]) + mm(norm_ref[:, half:], wo_ref[...])
    qw, kw = q_ref.shape[1], k_ref.shape[1]
    raw_ref[...] = qkv[:, :qw + kw]
    v_ref[...] = qkv[:, qw + kw:].astype(BF16)
    cosine, sine = cos_ref[...], sin_ref[...]
    for h in range((qw + kw) // HD):
        part = qkv[:, h * HD:(h + 1) * HD]
        is_q = h * HD < qw
        gain = gq_ref[...] if is_q else gk_ref[...]
        part = part * lax.rsqrt(jnp.mean(part * part, axis=-1, keepdims=True) + EPSILON) * gain
        part = (part * cosine + pltpu.roll(part, HD // 2, 1) * sine).astype(BF16)
        if is_q:
            q_ref[:, h * HD:(h + 1) * HD] = part
        else:
            at = h * HD - qw
            k_ref[:, at:at + HD] = part
    length = x.shape[0]
    i = lax.broadcasted_iota(jnp.int32, (length, length), 0)
    j = lax.broadcasted_iota(jnp.int32, (length, length), 1)
    allowed = (segc_ref[...] == segr_ref[...]) & (j <= i)
    heads, groups = qw // HD, kw // HD
    for h in range(heads):
        g = h * groups // heads
        s = mm_nt(q_ref[:, h * HD:(h + 1) * HD], k_ref[:, g * HD:(g + 1) * HD]) * HD ** (-0.5)
        s = jnp.where(allowed, s, MASK_VALUE)
        peak = jnp.max(s, axis=-1, keepdims=True)
        total = peak + jnp.log(jnp.sum(jnp.exp(s - peak), axis=-1, keepdims=True))
        p = jnp.exp(s - total)
        prob_ref[h * length:(h + 1) * length, :] = p
        ctx_ref[:, h * HD:(h + 1) * HD] = mm(p.astype(BF16), v_ref[:, g * HD:(g + 1) * HD]).astype(BF16)


def branch_kernel(place, ctx_ref, oz_ref, oo_ref, own_ref, *rest):
    sends, scratch = rest[:-1], rest[-1]
    z = place[0]
    half = D // 2
    ctx = ctx_ref[...]
    scratch[:, :half] = mm_nt(ctx, oz_ref[...])
    scratch[:, half:] = mm_nt(ctx, oo_ref[...])
    size = own_ref.shape[0]
    for k, out in enumerate((own_ref,) + sends):
        to = z ^ k
        for j in range(BLOCKS):
            b = place[1 + j]
            out[:, lanes(b ^ (2 * to))] = scratch[rows_of(to, size), j * LANE:(j + 1) * LANE].astype(out.dtype)


def mid_kernel(n, place, x_ref, g2_ref, *rest):
    terms, (resid_ref, mid_ref) = rest[:n], rest[n:]
    z = place[0]
    size = resid_ref.shape[0]
    resid = x_ref[rows_of(z, size), :].astype(F32)
    total = terms[0][...].astype(F32)
    for term in terms[1:]:
        total = total + term[...].astype(F32)
    resid = resid + total
    resid_ref[...] = resid
    scale = lax.rsqrt(jnp.mean(resid * resid, axis=-1, keepdims=True) + EPSILON)
    for j in range(BLOCKS):
        at = slice(j * LANE, (j + 1) * LANE)
        mid_ref[:, at] = (resid[:, at] * scale * g2_ref[:, lanes(j ^ (2 * z))]).astype(BF16)


def units_math(gate, up, dhidden):
    sigmoid = jax.nn.sigmoid(gate)
    hidden = (gate * sigmoid * up).astype(BF16)
    dgate = (dhidden * up * sigmoid * (1.0 + gate * (1.0 - sigmoid))).astype(BF16)
    dup = (dhidden * gate * sigmoid).astype(BF16)
    return hidden, dgate, dup


def units_kernel(n, mz_ref, mo_ref, cz_ref, co_ref, *rest):
    w = rest[:n]
    dz_ref, do_ref, az_ref, ao_ref, hid_ref, dgu_ref = rest[n:]
    units = w[0].shape[1] // 3
    part = w[0].shape[0]
    tokens = mz_ref.shape[0]
    for t, (m_ref, c_ref, d_ref, a_ref) in enumerate(
            ((mz_ref, cz_ref, dz_ref, az_ref), (mo_ref, co_ref, do_ref, ao_ref))):
        at = slice(t * tokens, (t + 1) * tokens)
        gu = dh = None
        for k in range(n):
            fs = slice(k * part, (k + 1) * part)
            g_k = mm(m_ref[:, fs], w[k][:, :2 * units])
            h_k = mm(c_ref[:, fs], w[k][:, 2 * units:])
            gu = g_k if gu is None else gu + g_k
            dh = h_k if dh is None else dh + h_k
        hidden, dgate, dup = units_math(gu[:, :units], gu[:, units:], dh)
        hid_ref[at, :] = hidden
        dgu_ref[at, :units] = dgate
        dgu_ref[at, units:] = dup
    for t, (d_ref, a_ref) in enumerate(((dz_ref, az_ref), (do_ref, ao_ref))):
        at = slice(t * tokens, (t + 1) * tokens)
        for k in range(n):
            fs = slice(k * part, (k + 1) * part)
            d_ref[:, fs] = mm_nt(dgu_ref[at, :], w[k][:, :2 * units]).astype(d_ref.dtype)
            a_ref[:, fs] = mm_nt(hid_ref[at, :], w[k][:, 2 * units:]).astype(a_ref.dtype)


def units_grad_kernel(n, mz_ref, mo_ref, cz_ref, co_ref, hid_ref, dgu_ref, *outs):
    units = hid_ref.shape[1]
    part = outs[0].shape[0]
    tokens = mz_ref.shape[0]
    for k in range(n):
        fs = slice(k * part, (k + 1) * part)
        out = outs[k]
        out[:, :2 * units] = (
            mm_tn(mz_ref[:, fs], dgu_ref[:tokens, :]) + mm_tn(mo_ref[:, fs], dgu_ref[tokens:, :])
        ).astype(out.dtype)
        out[:, 2 * units:] = (
            mm_tn(cz_ref[:, fs], hid_ref[:tokens, :]) + mm_tn(co_ref[:, fs], hid_ref[tokens:, :])
        ).astype(out.dtype)


def mid_back_kernel(n, place, resid_ref, cot_ref, g2_ref, *rest):
    terms, (grad_ref, gain_ref) = rest[:n], rest[n:]
    z = place[0]
    dmid = terms[0][...].astype(F32)
    for term in terms[1:]:
        dmid = dmid + term[...].astype(F32)
    resid = resid_ref[...]
    r2 = lax.rsqrt(jnp.mean(resid * resid, axis=-1, keepdims=True) + EPSILON)
    inner = None
    for j in range(BLOCKS):
        at = slice(j * LANE, (j + 1) * LANE)
        b = j ^ (2 * z)
        part = dmid[:, at] * g2_ref[:, lanes(b)] * resid[:, at]
        inner = part if inner is None else inner + part
        gain_ref[:, lanes(b)] = jnp.sum(dmid[:, at] * resid[:, at] * r2, axis=0, keepdims=True)
    inner = jnp.sum(inner, axis=-1, keepdims=True)
    back = r2 * r2 * r2 * inner / D
    for j in range(BLOCKS):
        at = slice(j * LANE, (j + 1) * LANE)
        grad_ref[:, at] = (
            cot_ref[:, at].astype(F32) + r2 * g2_ref[:, lanes(j ^ (2 * z))] * dmid[:, at] - resid[:, at] * back
        ).astype(BF16)


def output_grad_kernel(n, place, ctx_ref, *rest):
    pieces, (dbr_ref, gz_ref, go_ref) = rest[:n], rest[n:]
    z = place[0]
    size = pieces[0].shape[0]
    for k in range(n):
        frm = z ^ k
        for j in range(BLOCKS):
            b = place[1 + j]
            dbr_ref[rows_of(frm, size), j * LANE:(j + 1) * LANE] = pieces[k][:, lanes(b ^ (2 * frm))]
    half = D // 2
    go_ref[...] = mm_tn(dbr_ref[:, half:], ctx_ref[...]).astype(go_ref.dtype)
    gz_ref[...] = mm_tn(dbr_ref[:, :half], ctx_ref[...]).astype(gz_ref.dtype)


def attend_back_kernel(dbr_ref, oz_ref, oo_ref, prob_ref, q_ref, k_ref, v_ref, raw_ref, gq_ref, gk_ref, cos_ref, sin_ref,
                       dqkv_ref, dgq_ref, dgk_ref):
    half = D // 2
    dctx = (mm(dbr_ref[:, :half], oz_ref[...]) + mm(dbr_ref[:, half:], oo_ref[...])).astype(BF16)
    qw, kw = q_ref.shape[1], k_ref.shape[1]
    heads, groups = qw // HD, kw // HD
    length = dbr_ref.shape[0]
    cosine, sine = cos_ref[...], sin_ref[...]

    def back(grad, h, gain):
        grad = grad * cosine - pltpu.roll(grad, HD // 2, 1) * sine
        value = raw_ref[:, h * HD:(h + 1) * HD]
        factor = lax.rsqrt(jnp.mean(value * value, axis=-1, keepdims=True) + EPSILON)
        inner = jnp.sum(grad * gain * value, axis=-1, keepdims=True)
        out = factor * gain * grad - value * (factor * factor * factor) * inner / HD
        return out.astype(BF16), jnp.sum(grad * value * factor, axis=0, keepdims=True)

    dgq = dgk = None
    for g in range(groups):
        dk = dv = None
        keys = k_ref[:, g * HD:(g + 1) * HD]
        vals = v_ref[:, g * HD:(g + 1) * HD]
        for h in range(g * heads // groups, (g + 1) * heads // groups):
            hs = slice(h * HD, (h + 1) * HD)
            p = prob_ref[h * length:(h + 1) * length, :]
            dp = mm_nt(dctx[:, hs], vals)
            delta = jnp.sum(p * dp, axis=-1, keepdims=True)
            ds = (p * (dp - delta)).astype(BF16)
            dq, gain_part = back(mm(ds, keys) * HD ** (-0.5), h, gq_ref[...])
            dqkv_ref[:, hs] = dq
            dgq = gain_part if dgq is None else dgq + gain_part
            dk_h = mm_tn(ds, q_ref[:, hs])
            dv_h = mm_tn(p.astype(BF16), dctx[:, hs])
            dk = dk_h if dk is None else dk + dk_h
            dv = dv_h if dv is None else dv + dv_h
        dk, gain_part = back(dk * HD ** (-0.5), heads + g, gk_ref[...])
        dgk = gain_part if dgk is None else dgk + gain_part
        dqkv_ref[:, qw + g * HD:qw + (g + 1) * HD] = dk
        dqkv_ref[:, qw + kw + g * HD:qw + kw + (g + 1) * HD] = dv.astype(BF16)
    dgq_ref[...] = dgq
    dgk_ref[...] = dgk


def qkv_grad_kernel(norm_ref, dqkv_ref, gz_ref, go_ref):
    half = D // 2
    go_ref[...] = mm_tn(norm_ref[:, half:], dqkv_ref[...]).astype(go_ref.dtype)
    gz_ref[...] = mm_tn(norm_ref[:, :half], dqkv_ref[...]).astype(gz_ref.dtype)


def input_grad_kernel(n, place, dqkv_ref, wz_ref, wo_ref, x_ref, g1_ref, *rest):
    outs, gain_ref, dn_ref, term_ref = rest[:n], rest[n], rest[n + 1], rest[n + 2]
    z = place[0]
    half = D // 2
    dqkv = dqkv_ref[...]
    dn_ref[:, :half] = mm_nt(dqkv, wz_ref[...])
    dn_ref[:, half:] = mm_nt(dqkv, wo_ref[...])
    x = x_ref[...].astype(F32)
    r1 = lax.rsqrt(jnp.mean(x * x, axis=-1, keepdims=True) + EPSILON)
    inner = None
    for j in range(BLOCKS):
        b = place[1 + j]
        dn = dn_ref[:, j * LANE:(j + 1) * LANE]
        xb = x_ref[:, lanes(b ^ (2 * z))].astype(F32)
        part = dn * g1_ref[:, lanes(b)] * xb
        inner = part if inner is None else inner + part
        gain_ref[:, lanes(b)] = jnp.sum(dn * xb * r1, axis=0, keepdims=True)
    inner = jnp.sum(inner, axis=-1, keepdims=True)
    back = r1 * r1 * r1 * inner / D
    for j in range(BLOCKS):
        b = place[1 + j]
        at = lanes(b ^ (2 * z))
        xb = x_ref[:, at].astype(F32)
        term_ref[:, at] = r1 * g1_ref[:, lanes(b)] * dn_ref[:, j * LANE:(j + 1) * LANE] - xb * back
    width = outs[0].shape[1]
    for k, out in enumerate(outs):
        out[...] = term_ref[:, k * width:(k + 1) * width].astype(out.dtype)


def act_grad_kernel(n, place, *rest):
    pieces, terms, out_ref = rest[:n], rest[n:2 * n], rest[2 * n]
    z = place[0]
    width = out_ref.shape[1]
    size = pieces[0].shape[0]
    for k in range(n):
        at = rows_of(z ^ k, size)
        total = terms[0][at, :].astype(F32)
        for term in terms[1:]:
            total = total + term[at, :].astype(F32)
        out_ref[at, :] = pieces[k][:, k * width:(k + 1) * width].astype(F32) + total


def act_out_kernel(n, resid_ref, *rest):
    terms, outs = rest[:n], rest[n:]
    total = terms[0][...].astype(F32)
    for term in terms[1:]:
        total = total + term[...].astype(F32)
    total = (resid_ref[...] + total).astype(BF16)
    width = outs[0].shape[1]
    for k, out in enumerate(outs):
        out[...] = total[:, k * width:(k + 1) * width]


def place_kernel(n, place, *rest):
    pieces, out_ref = rest[:n], rest[n]
    size = pieces[0].shape[0]
    for k in range(n):
        out_ref[rows_of(place[0] ^ k, size), :] = pieces[k][...]


def adamw(weight, first, second, grad, rate, decay):
    first_new = BETA_FIRST * first + (1.0 - BETA_FIRST) * grad
    second_new = BETA_SECOND * second + (1.0 - BETA_SECOND) * grad * grad
    first_hat = first_new / (1.0 - BETA_FIRST**STEP)
    second_hat = second_new / (1.0 - BETA_SECOND**STEP)
    weight_new = weight - rate * (
        first_hat / (jnp.sqrt(second_hat) + ADAM_EPSILON) + decay * weight
    )
    return (weight_new, first_new, second_new)


def body(sizes, act_in, act_cot, segments, positions, gains, gains_first, gains_second,
         query_weight, query_first, query_second, key_weight, key_first, key_second,
         value_weight, value_first, value_second, output_weight, output_first, output_second,
         gate_weight, gate_first, gate_second, up_weight, up_first, up_second,
         down_weight, down_first, down_second):
    n_dp, n_row, n_col = sizes
    n_plane = n_dp * n_col
    paired = n_dp == 2 and n_col == 4
    z = lax.axis_index("row").astype(jnp.int32)
    p = lax.axis_index(PLANE).astype(jnp.int32)

    def over_row(value, k):
        return lax.ppermute(value, "row", [(i, i ^ k) for i in range(n_row)])

    def over_plane(value, k):
        return lax.ppermute(value, PLANE, [(i, i ^ k) for i in range(n_plane)])

    def gather_row(value):
        return [value] + [over_row(value, k) for k in range(1, n_row)]

    def scatter_row(values):
        return [values[0]] + [over_row(values[k], k) for k in range(1, n_row)]

    def gather_plane(value):
        if not paired:
            whole = lax.all_gather(value, PLANE, axis=0, tiled=True)
            half = whole.shape[0] // 2
            return whole[:half], whole[half:]
        same = jnp.concatenate([value] + [over_plane(value, k) for k in (2, 4, 6)], axis=0)
        return same, over_plane(same, 1)

    def scatter_plane(same, other):
        if not paired:
            whole = jnp.concatenate([same, other.astype(F32)], axis=0)
            return [lax.psum_scatter(whole, PLANE, scatter_dimension=0, tiled=True)]
        total = same + over_plane(other, 1).astype(F32)
        size = total.shape[0] // 4
        return [total[:size]] + [
            over_plane(total[i * size:(i + 1) * size].astype(BF16), k) for i, k in ((1, 2), (2, 4), (3, 6))
        ]

    def sum_all(value):
        if not paired:
            return lax.psum(value, ("dp", "row", "col"))
        value = value + over_plane(value, 1)
        value = value + over_plane(value, 2) + over_plane(value, 4) + over_plane(value, 6)
        return value + over_row(value, 1) + over_row(value, 2) + over_row(value, 3)

    order = jnp.array([0, 2, 4, 6, 1, 3, 5, 7], jnp.int32) ^ p if paired else jnp.arange(BLOCKS, dtype=jnp.int32)
    place = jnp.concatenate([z[None], order])

    w_qkv = jnp.concatenate([query_weight, key_weight, value_weight], axis=1).astype(BF16)
    qkv_z, qkv_o = gather_plane(w_qkv)
    x_row = jnp.concatenate(gather_row(act_in), axis=1)
    out_z, out_o = gather_plane(output_weight.astype(BF16))
    w_units = gather_row(jnp.concatenate([gate_weight, up_weight, down_weight], axis=1).astype(BF16))
    length = act_in.shape[0]
    size = length // n_row
    cot_own = jnp.concatenate(
        scatter_row([lax.dynamic_slice_in_dim(act_cot, (z ^ k) * size, size, 0) for k in range(n_row)]), axis=1)
    cot_z, cot_o = gather_plane(cot_own)

    gain_in = gains[None, :D]
    gain_mid = gains[None, D:2 * D]
    gain_query = gains[None, 2 * D:2 * D + HD]
    gain_key = gains[None, 2 * D + HD:]
    inverse = THETA_BASE ** (-(jnp.arange(HD // 2, dtype=F32) * 2.0 / HD))
    angle = positions.astype(F32)[:, None] * inverse
    cosine, sine = jnp.cos(angle), jnp.sin(angle)
    cosine = jnp.concatenate([cosine, cosine], axis=1)
    sine = jnp.concatenate([-sine, sine], axis=1)

    qw, kw = query_weight.shape[1], key_weight.shape[1]
    heads = qw // HD
    context, probs, queries, keys, values, raw, normed = call(
        attend_kernel,
        [shape((length, qw), BF16), shape((heads * length, length), F32), shape((length, qw), BF16),
         shape((length, kw), BF16), shape((length, kw), BF16), shape((length, qw + kw), F32), shape((length, D), BF16)],
        place, x_row, qkv_z, qkv_o, gain_in, gain_query, gain_key, cosine, sine, segments[:, None], segments[None, :],
        scalars=1, flops=2 * length * D * (qw + 2 * kw) + 4 * heads * length * length * HD)
    terms = call(
        branch_kernel,
        [shape((size, D), F32)] + [shape((size, D), BF16)] * (n_row - 1),
        place, context, out_z, out_o,
        scalars=1, scratch=[pltpu.VMEM((length, D), F32)], flops=2 * length * D * qw)
    terms = scatter_row(terms)
    resid, mid = call(
        functools.partial(mid_kernel, n_row),
        [shape((size, D), F32), shape((size, D), BF16)],
        place, x_row, gain_mid, *terms, scalars=1, flops=1e6)

    mid_z, mid_o = gather_plane(mid)
    units = gate_weight.shape[1]
    tokens = mid_z.shape[0]
    if units % LANE == 0 and tokens <= 512:
        dmid_z, dmid_o, down_z, down_o, hidden, d_units = call(
            functools.partial(units_kernel, n_row),
            [shape((tokens, D), F32), shape((tokens, D), BF16), shape((tokens, D), F32), shape((tokens, D), BF16),
             shape((2 * tokens, units), BF16), shape((2 * tokens, 2 * units), BF16)],
            mid_z, mid_o, cot_z, cot_o, *w_units, flops=2 * 2 * tokens * D * units * 6)
        unit_grads = call(
            functools.partial(units_grad_kernel, n_row),
            [shape((D // n_row, 3 * units), F32 if k == 0 else BF16) for k in range(n_row)],
            mid_z, mid_o, cot_z, cot_o, hidden, d_units, flops=2 * 2 * tokens * D * units * 3)
    else:
        mid_all = jnp.concatenate([mid_z, mid_o], axis=0)
        cot_all = jnp.concatenate([cot_z, cot_o], axis=0)
        joined = jnp.concatenate(w_units, axis=0)
        gate_up = mm(mid_all, joined[:, :2 * units])
        hidden, dgate, dup = units_math(gate_up[:, :units], gate_up[:, units:], mm(cot_all, joined[:, 2 * units:]))
        d_units = jnp.concatenate([dgate, dup], axis=1)
        dmid = mm_nt(d_units, joined[:, :2 * units])
        down = mm_nt(hidden, joined[:, 2 * units:])
        dmid_z, dmid_o, down_z, down_o = dmid[:tokens], dmid[tokens:], down[:tokens], down[tokens:]
        whole = jnp.concatenate([mm_tn(mid_all, d_units), mm_tn(cot_all, hidden)], axis=1)
        unit_grads = [
            part.astype(F32 if k == 0 else BF16) for k, part in enumerate(jnp.split(whole, n_row, axis=0))
        ]
    dmid_terms = scatter_plane(dmid_z, dmid_o)
    branch_grad, mid_gain_grad = call(
        functools.partial(mid_back_kernel, len(dmid_terms)),
        [shape((size, D), BF16), shape((1, D), F32)],
        place, resid, cot_own, gain_mid, *dmid_terms, scalars=1, flops=1e6)

    pieces = gather_row(branch_grad)
    unit_grads = scatter_row(unit_grads)
    down_terms = scatter_plane(down_z, down_o)
    dbranch, out_grad_z, out_grad_o = call(
        functools.partial(output_grad_kernel, n_row),
        [shape((length, D), BF16), shape((D // 2, qw), F32), shape((D // 2, qw), BF16)],
        place, context, *pieces, scalars=1, flops=2 * length * D * qw)
    out_terms = scatter_plane(out_grad_z, out_grad_o)
    dqkv, query_gain_grad, key_gain_grad = call(
        attend_back_kernel,
        [shape((length, qw + 2 * kw), BF16), shape((1, HD), F32), shape((1, HD), F32)],
        dbranch, out_z, out_o, probs, queries, keys, values, raw, gain_query, gain_key, cosine, sine,
        flops=2 * length * D * qw + 8 * heads * length * length * HD)
    qkv_grad_z, qkv_grad_o = call(
        qkv_grad_kernel,
        [shape((D // 2, qw + 2 * kw), F32), shape((D // 2, qw + 2 * kw), BF16)],
        normed, dqkv, flops=2 * length * D * (qw + 2 * kw))
    qkv_terms = scatter_plane(qkv_grad_z, qkv_grad_o)
    width = act_in.shape[1]
    *in_terms, in_gain_grad = call(
        functools.partial(input_grad_kernel, n_row),
        [shape((length, width), F32 if k == 0 else BF16) for k in range(n_row)] + [shape((1, D), F32)],
        place, dqkv, qkv_z, qkv_o, x_row, gain_in,
        scalars=1, scratch=[pltpu.VMEM((length, D), F32)] * 2, flops=2 * length * D * (qw + 2 * kw))
    in_terms = scatter_row(in_terms)
    gains_grad = sum_all(jnp.concatenate([in_gain_grad, mid_gain_grad, query_gain_grad, key_gain_grad], axis=1))[0]

    out_parts = call(
        functools.partial(act_out_kernel, len(down_terms)),
        [shape((size, width), BF16)] * n_row,
        resid, *down_terms, flops=1e6)
    out_parts = scatter_row(out_parts)
    (act_out,) = call(functools.partial(place_kernel, n_row), [shape((length, width), BF16)],
                      place, *out_parts, scalars=1, flops=1e6)
    (act_grad,) = call(functools.partial(act_grad_kernel, n_row), [shape((length, width), F32)],
                       place, *pieces, *in_terms, scalars=1, flops=1e6)

    def total(terms):
        out = terms[0].astype(F32)
        for term in terms[1:]:
            out = out + term.astype(F32)
        return out

    unit_total, out_total, qkv_total = total(unit_grads), total(out_terms), total(qkv_terms)
    matrix = functools.partial(adamw, rate=MATRIX_RATE, decay=MATRIX_DECAY)
    return (
        act_out,
        act_grad,
        *adamw(gains, gains_first, gains_second, gains_grad, GAIN_RATE, 0.0),
        *matrix(query_weight, query_first, query_second, qkv_total[:, :qw]),
        *matrix(key_weight, key_first, key_second, qkv_total[:, qw:qw + kw]),
        *matrix(value_weight, value_first, value_second, qkv_total[:, qw + kw:]),
        *matrix(output_weight, output_first, output_second, out_total),
        *matrix(gate_weight, gate_first, gate_second, unit_total[:, :units]),
        *matrix(up_weight, up_first, up_second, unit_total[:, units:2 * units]),
        *matrix(down_weight, down_first, down_second, unit_total[:, 2 * units:]),
    )


def solution(mesh):
    token, proj, unit = P(PLANE, "row"), P(PLANE, "row"), P("row", PLANE)
    sizes = (mesh.shape["dp"], mesh.shape["row"], mesh.shape["col"])
    return jax.shard_map(
        functools.partial(body, sizes),
        mesh=mesh,
        in_specs=(token, token, P(PLANE), P(PLANE)) + (P(),) * 3 + (proj,) * 12 + (unit,) * 9,
        out_specs=(token, token) + (P(),) * 3 + (proj,) * 12 + (unit,) * 9,
        check_vma=False,
    )
```

time: 692 us -> 265 us (0.38)
  waiting for transfers between devices: 434 us -> 105 us
  blocking collectives: 153 us -> 0 us
  starting transfers between devices: 0.89 us -> 112 us
  matrix products: 35.4 us -> 0 us
  other arithmetic: 39.7 us -> 15 us
  Pallas kernels: 0 us -> 20.6 us
  between operations: 15.1 us -> 1.51 us
    reduce_scatter x13 -> x0, waiting for transfers between devices: 331 us -> none  [the longest x2 141 us: sum_units(): return lax.psum_scatter(terms, 'row', scatter_dimension=0, tiled=True)]
    ppermute x0 -> x63, starting transfers between devices: none -> 112 us  [the longest x27 56.6 us: over_row(): return lax.ppermute(value, 'row', [(i, i ^ k) for i in range(n_row)])]
    ppermute x0 -> x63, waiting for transfers between devices: none -> 105 us  [the longest x27 77.4 us: over_row(): return lax.ppermute(value, 'row', [(i, i ^ k) for i in range(n_row)])]
    all_gather x4 -> x0, waiting for transfers between devices: 102 us -> none  [the longest x2 97.4 us: gather_units(): return lax.all_gather(values, 'row', axis=0, tiled=True)]
    all_gather x9 -> x0, blocking collectives: 89.9 us -> none  [the longest x2 33.2 us: gather_width(): return lax.all_gather(values, 'row', axis=1, tiled=True)]
    psum x3 -> x0, blocking collectives: 63.4 us -> none  [the longest x1 39.5 us: body(): lax.psum(jnp.concatenate([gain_in_grad, mid_place, query_gain_grad, key_g...]
    dot_general x24 -> x0, matrix products: 35.4 us -> none  [the longest x6 12.4 us: matmul_tn(): lax.dot_general(left, right, (((0,), (0,)), ((), ())), preferred_element_...]
    pallas_call x0 -> x13, Pallas kernels: none -> 20.6 us  [call(): pl.pallas_call(kernel, out_shape=list(outs), in_specs=[smem] * scalars +...]
  transfers between devices with their start and end apart: 17 -> 63, of which waited for: 12 -> 21; matrix products, arithmetic and copies ran while one was open for 11% -> 8% of each run, Pallas kernels for 0% -> 7%
where the time goes in v1:
time: 265 us; the launch traced here: 263 us
  starting transfers between devices  112 us (42%)
  waiting for transfers between devices  105 us (40%)
  Pallas kernels  20.6 us (8%)
  other arithmetic  15 us (6%)
  local copies, waits for them, and re-layouts  9.62 us (4%)
    ppermute x27, waiting for transfers between devices, over_row(): return lax.ppermute(value, 'row', [(i, i ^ k) for i in range(n_row)])  77.4 us
    ppermute x27, starting transfers between devices, over_row(): return lax.ppermute(value, 'row', [(i, i ^ k) for i in range(n_row)])  56.6 us
    ppermute x36, starting transfers between devices, over_plane(): return lax.ppermute(value, PLANE, [(i, i ^ k) for i in range(n_plane)])  55.1 us
    ppermute x36, waiting for transfers between devices, over_plane(): return lax.ppermute(value, PLANE, [(i, i ^ k) for i in range(n_plane)])  27.6 us
    pallas_call x13, Pallas kernels, call(): pl.pallas_call(kernel, out_shape=list(outs), in_specs=[smem] * scalars +...  20.6 us
    sub x5, other arithmetic, adamw(): weight - rate * (first_hat / (jnp.sqrt(second_hat) + ADAM_EPSILON) + deca...  5.81 us
  transfers between devices with their start and end apart: 63, of which 21 were waited for; matrix products, arithmetic and copies ran while one was open for 8% of the time, Pallas kernels for 7%

profile of v1, /device:TPU:0, one launch (start us, length us, event | category | flops | bytes accessed | tf_op | source)
XLA Modules:
  0.0 263.5 jit_solution(7757430489328695531)
XLA Ops:
  1.7 4.0 %collective-permute-start.9 = (bf16[128,512]{1,0:T(8,128)(2,1)S(1)}, bf16[128,512]{1,0:T(8,128)(2,1)}, u32[]{:S(2)}, u32[]{:S(2)}) collective-permute-start(bf16[128,512]{1,0:T(8,128)(2,1)S(1)} %convert_element_type.60), channel_id=1, source_target_pairs={{0,18},{1,19},{2,16},{3,17},{16,2},{17,3},{18,0},{19,1},{4,22},{5,... | collective-permute-start | bytes 393224 | tf_op jit(solution)/shard_map/ppermute | solution.py:366
  15.7 3.4 %collective-permute-done.5 = bf16[128,1024]{1,0:T(8,128)(2,1)S(1)} collective-permute-done((bf16[128,1024]{1,0:T(8,128)(2,1)S(1)}, bf16[128,1024]{1,0:T(8,128)(2,1)S(1)}, u32[]{:S(2)}, u32[]{:S(2)}) %collective-permute-start.5) | collective-permute-done | bytes 262176 | tf_op jit(solution)/shard_map/ppermute | solution.py:366
  19.3 3.9 %collective-permute-done.4 = bf16[128,1024]{1,0:T(8,128)(2,1)S(1)} collective-permute-done((bf16[128,1024]{1,0:T(8,128)(2,1)S(1)}, bf16[128,1024]{1,0:T(8,128)(2,1)S(1)}, u32[]{:S(2)}, u32[]{:S(2)}) %collective-permute-start.4) | collective-permute-done | bytes 262176 | tf_op jit(solution)/shard_map/ppermute | solution.py:366
  23.1 2.8 %collective-permute-start.1 = (bf16[256,256]{1,0:T(8,128)(2,1)}, bf16[256,256]{1,0:T(8,128)(2,1)}, u32[]{:S(2)}, u32[]{:S(2)}) collective-permute-start(bf16[256,256]{1,0:T(8,128)(2,1)} %param.29), channel_id=1, source_target_pairs={{0,8},{4,12},{8,0},{12,4},{1,9},{5,13},{9,1},{13,5},{2,10},{6,14},... | collective-permute-start | bytes 393224 | tf_op jit(solution)/shard_map/ppermute | solution.py:363
  34.6 3.8 %collective-permute-done = bf16[256,256]{1,0:T(8,128)(2,1)} collective-permute-done((bf16[256,256]{1,0:T(8,128)(2,1)}, bf16[256,256]{1,0:T(8,128)(2,1)}, u32[]{:S(2)}, u32[]{:S(2)}) %collective-permute-start) | collective-permute-done | bytes 131104 | tf_op jit(solution)/shard_map/ppermute | solution.py:363
  39.3 3.4 %collective-permute-start.20 = (bf16[64,256]{1,0:T(8,128)(2,1)}, bf16[64,256]{1,0:T(8,128)(2,1)S(1)}, u32[]{:S(2)}, u32[]{:S(2)}) collective-permute-start(bf16[64,256]{1,0:T(8,128)(2,1)} %get-tuple-element.165), channel_id=1, source_target_pairs={{0,12},{4,8},{8,4},{12,0},{1,13},{5,9},{9,5},{13,1},{2,14},{6,10},... | collective-permute-start | bytes 98312 | tf_op jit(solution)/shard_map/ppermute | solution.py:363
  46.5 3.2 %shard_map.476 = (bf16[256,512]{1,0:T(8,128)(2,1)S(1)}, f32[1024,256]{1,0:T(8,128)S(1)}, bf16[256,512]{1,0:T(8,128)(2,1)S(1)}, bf16[256,256]{1,0:T(8,128)(2,1)S(...) custom-call(s32[9]{0:T(128)S(1)} %pad_add_fusion.place, ...), custom_call_target="tpu_custom_call" | custom-call | flops 671088640 | bytes 6036516 | tf_op jit(solution)/shard_map/pallas_call | solution.py:54
  55.7 2.9 %collective-permute-start.12 = (bf16[64,1024]{1,0:T(8,128)(2,1)S(1)}, bf16[64,1024]{1,0:T(8,128)(2,1)S(1)}, u32[]{:S(2)}, u32[]{:S(2)}) collective-permute-start(bf16[64,1024]{1,0:T(8,128)(2,1)S(1)} %get-tuple-element.71), channel_id=1, source_target_pairs={{0,8},{4,12},{8,0},{12,4},{1,9},{5,13},{9,1},{13,5},{2,10},{6,14},... | collective-permute-start | bytes 393224 | tf_op jit(solution)/shard_map/ppermute | solution.py:363
  59.6 7.7 %collective-permute-done.12.rest_2_ = bf16[64,1024]{1,0:T(8,128)(2,1)S(1)} collective-permute-done((bf16[64,1024]{1,0:T(8,128)(2,1)S(1)}, bf16[64,1024]{1,0:T(8,128)(2,1)S(1)}, u32[]{:S(2)}, u32[]{:S(2)}) %collective-permute-start.12) | collective-permute-done | bytes 131104 | tf_op jit(solution)/shard_map/ppermute | solution.py:363
  67.2 2.2 collective-permute-start.27
  73.4 18.9 %collective-permute-start.15 = (bf16[64,1024]{1,0:T(8,128)(2,1)S(1)}, bf16[64,1024]{1,0:T(8,128)(2,1)S(1)}, u32[]{:S(2)}, u32[]{:S(2)}) collective-permute-start(bf16[64,1024]{1,0:T(8,128)(2,1)S(1)} %get-tuple-element.74), channel_id=1, source_target_pairs={{0,16},{1,17},{2,18},{3,19},{16,0},{17,1},{18,2},{19,3},{4,20},{5,... | collective-permute-start | bytes 393224 | tf_op jit(solution)/shard_map/ppermute | solution.py:366
  92.4 4.3 %collective-permute-start.16 = (bf16[64,1024]{1,0:T(8,128)(2,1)S(1)}, bf16[64,1024]{1,0:T(8,128)(2,1)S(1)}, u32[]{:S(2)}, u32[]{:S(2)}) collective-permute-start(bf16[64,1024]{1,0:T(8,128)(2,1)S(1)} %get-tuple-element.74), channel_id=1, source_target_pairs={{0,18},{1,19},{2,16},{3,17},{16,2},{17,3},{18,0},{19,1},{4,22},{5,... | collective-permute-start | bytes 393224 | tf_op jit(solution)/shard_map/ppermute | solution.py:366
  96.8 2.8 %collective-permute-done.16 = bf16[64,1024]{1,0:T(8,128)(2,1)S(1)} collective-permute-done((bf16[64,1024]{1,0:T(8,128)(2,1)S(1)}, bf16[64,1024]{1,0:T(8,128)(2,1)S(1)}, u32[]{:S(2)}, u32[]{:S(2)}) %collective-permute-start.16) | collective-permute-done | bytes 131104 | tf_op jit(solution)/shard_map/ppermute | solution.py:366
  99.7 19.6 %collective-permute-done.26.rest_2_ = bf16[256,1152]{1,0:T(8,128)(2,1)S(1)} collective-permute-done((bf16[256,1152]{1,0:T(8,128)(2,1)S(1)}, bf16[256,1152]{1,0:T(8,128)(2,1)S(1)}, u32[]{:S(2)}, u32[]{:S(2)}) %collective-permute-start.26) | collective-permute-done | bytes 589856 | tf_op jit(solution)/shard_map/ppermute | solution.py:363
  119.3 3.0 %shard_map.479 = (f32[256,1024]{1,0:T(8,128)S(1)}, bf16[256,1024]{1,0:T(8,128)(2,1)S(1)}, f32[256,1024]{1,0:T(8,128)S(1)}, bf16[256,1024]{1,0:T(8,128)(2,1)S(1)}...) custom-call(bf16[256,1024]{1,0:T(8,128)(2,1)S(1)} %constant_dynamic-update-slice_fusion.4.mz_ref, ...), custom_call_target="tpu_custom_call" | custom-call | flops 2415919104 | bytes 8781824 | tf_op jit(solution)/shard_map/pallas_call | solution.py:54
  133.9 2.7 %collective-permute-start.62 = (bf16[256,1152]{1,0:T(8,128)(2,1)S(1)}, bf16[256,1152]{1,0:T(8,128)(2,1)S(1)}, u32[]{:S(2)}, u32[]{:S(2)}) collective-permute-start(bf16[256,1152]{1,0:T(8,128)(2,1)S(1)} %get-tuple-element.109), channel_id=1, source_target_pairs={{0,12},{4,8},{8,4},{12,0},{1,13},{5,9},{9,5},{13,1},{2,14},{6,10},... | collective-permute-start | bytes 1769480 | tf_op jit(solution)/shard_map/ppermute | solution.py:363
  138.8 36.4 %collective-permute-done.41.rest_3_ = bf16[64,1024]{1,0:T(8,128)(2,1)S(1)} collective-permute-done((bf16[64,1024]{1,0:T(8,128)(2,1)S(1)}, bf16[64,1024]{1,0:T(8,128)(2,1)S(1)}, u32[]{:S(2)}, u32[]{:S(2)}) %collective-permute-start.41) | collective-permute-done | bytes 131104 | tf_op jit(solution)/shard_map/ppermute | solution.py:363
  175.2 19.7 %collective-permute-start.39 = (bf16[64,1024]{1,0:T(8,128)(2,1)S(1)}, bf16[64,1024]{1,0:T(8,128)(2,1)S(1)}, u32[]{:S(2)}, u32[]{:S(2)}) collective-permute-start(bf16[64,1024]{1,0:T(8,128)(2,1)S(1)} %get-tuple-element.83.rest_0_), channel_id=1, source_target_pairs={{0,4},{4,0},{8,12},{12,8},{1,5},{5,1},{9,13},{13,9},{2,6},{6,2},{1... | collective-permute-start | bytes 393224 | tf_op jit(solution)/shard_map/ppermute | solution.py:363
  200.6 3.4 %shard_map.484 = (bf16[256,1024]{1,0:T(8,128)(2,1)S(1)}, f32[1,128]{1,0:T(1,128)S(1)}, f32[1,128]{1,0:T(1,128)S(1)}) custom-call(bf16[256,1024]{1,0:T(8,128)(2,1)S(1)} %get-tuple-element.84.dbr_ref, bf16[512,512]{1,0:T(8,128)(2,1)S(1)} %pad_maximum_fusion.2.oz_ref, bf16[512,512]{1,0:T(8,128)(2,1)} %collective-permute-done.10.oo_ref, ...), custom_call_target="tpu_custom_call" | custom-call | flops 536870912 | bytes 4720640 | tf_op jit(solution)/shard_map/pallas_call | solution.py:54
  206.8 4.2 %collective-permute-done.29.rest_1_ = bf16[64,1024]{1,0:T(8,128)(2,1)S(1)} collective-permute-done((bf16[64,1024]{1,0:T(8,128)(2,1)S(1)}, bf16[64,1024]{1,0:T(8,128)(2,1)S(1)}, u32[]{:S(2)}, u32[]{:S(2)}) %collective-permute-start.29) | collective-permute-done | bytes 131104 | tf_op jit(solution)/shard_map/ppermute | solution.py:366
  234.9 6.7 %collective-permute-done.43.rest_6_ = bf16[256,256]{1,0:T(8,128)(2,1)S(1)} collective-permute-done((bf16[256,256]{1,0:T(8,128)(2,1)S(1)}, bf16[256,256]{1,0:T(8,128)(2,1)S(1)}, u32[]{:S(2)}, u32[]{:S(2)}) %collective-permute-start.43) | collective-permute-done | bytes 131104 | tf_op jit(solution)/shard_map/ppermute | solution.py:363
  250.8 2.3 collective-permute-done.59
  253.2 2.5 collective-permute-done.58
  256.7 3.2 %collective-permute-done.55 = bf16[128,1024]{1,0:T(8,128)(2,1)S(1)} collective-permute-done((bf16[128,1024]{1,0:T(8,128)(2,1)S(1)}, bf16[128,1024]{1,0:T(8,128)(2,1)S(1)}, u32[]{:S(2)}, u32[]{:S(2)}) %collective-permute-start.55) | collective-permute-done | bytes 262176 | tf_op jit(solution)/shard_map/ppermute | solution.py:366
  (228 shorter events, 95.2 us)
Async XLA Ops:
  1.7 26.1 %collective-permute-start.9 = (bf16[128,512]{1,0:T(8,128)(2,1)S(1)}, bf16[128,512]{1,0:T(8,128)(2,1)}, u32[]{:S(2)}, u32[]{:S(2)}) collective-permute-start(bf16[128,512]{1,0:T(8,128)(2,1)S(1)} %convert_element_type.60), channel_id=1, source_target_pairs={{0,18},{1,19},{2,16},{3,17},{16,2},{17,3},{18,0},{19,1},{4,22},{5,... | collective-permute-start | bytes 393224 | tf_op jit(solution)/shard_map/ppermute | solution.py:366
  5.6 23.8 %collective-permute-start.8 = (bf16[128,512]{1,0:T(8,128)(2,1)S(1)}, bf16[128,512]{1,0:T(8,128)(2,1)}, u32[]{:S(2)}, u32[]{:S(2)}) collective-permute-start(bf16[128,512]{1,0:T(8,128)(2,1)S(1)} %convert_element_type.60), channel_id=1, source_target_pairs={{0,16},{1,17},{2,18},{3,19},{16,0},{17,1},{18,2},{19,3},{4,20},{5,... | collective-permute-start | bytes 393224 | tf_op jit(solution)/shard_map/ppermute | solution.py:366
  23.1 16.1 %collective-permute-start.1 = (bf16[256,256]{1,0:T(8,128)(2,1)}, bf16[256,256]{1,0:T(8,128)(2,1)}, u32[]{:S(2)}, u32[]{:S(2)}) collective-permute-start(bf16[256,256]{1,0:T(8,128)(2,1)} %param.29), channel_id=1, source_target_pairs={{0,8},{4,12},{8,0},{12,4},{1,9},{5,13},{9,1},{13,5},{2,10},{6,14},... | collective-permute-start | bytes 393224 | tf_op jit(solution)/shard_map/ppermute | solution.py:363
  26.0 19.1 %collective-permute-start.6 = (bf16[512,1024]{1,0:T(8,128)(2,1)S(1)}, bf16[512,1024]{1,0:T(8,128)(2,1)S(1)}, u32[]{:S(2)}, u32[]{:S(2)}) collective-permute-start(bf16[512,1024]{1,0:T(8,128)(2,1)S(1)} %pad_maximum_fusion.wz_ref), channel_id=1, source_target_pairs={{0,1},{1,0},{2,3},{3,2},{16,17},{17,16},{18,19},{19,18},{4,5},{5,4... | collective-permute-start | bytes 3145736 | tf_op jit(solution)/shard_map/ppermute | solution.py:366
  31.5 18.2 %collective-permute-start.10 = (bf16[512,512]{1,0:T(8,128)(2,1)S(1)}, bf16[512,512]{1,0:T(8,128)(2,1)}, u32[]{:S(2)}, u32[]{:S(2)}) collective-permute-start(bf16[512,512]{1,0:T(8,128)(2,1)S(1)} %pad_maximum_fusion.2.oz_ref), channel_id=1, source_target_pairs={{0,1},{1,0},{2,3},{3,2},{16,17},{17,16},{18,19},{19,18},{4,5},{5,4... | collective-permute-start | bytes 1572872 | tf_op jit(solution)/shard_map/ppermute | solution.py:366
  52.1 19.9 %collective-permute-start.23 = (bf16[64,1024]{1,0:T(8,128)(2,1)S(1)}, bf16[64,1024]{1,0:T(8,128)(2,1)S(1)}, u32[]{:S(2)}, u32[]{:S(2)}) collective-permute-start(bf16[64,1024]{1,0:T(8,128)(2,1)S(1)} %pad_maximum_fusion.7.cot_ref), channel_id=1, source_target_pairs={{0,18},{1,19},{2,16},{3,17},{16,2},{17,3},{18,0},{19,1},{4,22},{5,... | collective-permute-start | bytes 393224 | tf_op jit(solution)/shard_map/ppermute | solution.py:366
  53.6 18.8 %collective-permute-start.22 = (bf16[64,1024]{1,0:T(8,128)(2,1)S(1)}, bf16[64,1024]{1,0:T(8,128)(2,1)S(1)}, u32[]{:S(2)}, u32[]{:S(2)}) collective-permute-start(bf16[64,1024]{1,0:T(8,128)(2,1)S(1)} %pad_maximum_fusion.7.cot_ref), channel_id=1, source_target_pairs={{0,16},{1,17},{2,18},{3,19},{16,0},{17,1},{18,2},{19,3},{4,20},{5,... | collective-permute-start | bytes 393224 | tf_op jit(solution)/shard_map/ppermute | solution.py:366
  55.1 18.3 %collective-permute-start.21 = (bf16[64,1024]{1,0:T(8,128)(2,1)S(1)}, bf16[64,1024]{1,0:T(8,128)(2,1)S(1)}, u32[]{:S(2)}, u32[]{:S(2)}) collective-permute-start(bf16[64,1024]{1,0:T(8,128)(2,1)S(1)} %pad_maximum_fusion.7.cot_ref), channel_id=1, source_target_pairs={{0,2},{1,3},{2,0},{3,1},{16,18},{17,19},{18,16},{19,17},{4,6},{5,7... | collective-permute-start | bytes 393224 | tf_op jit(solution)/shard_map/ppermute | solution.py:366
  67.2 32.5 %collective-permute-start.27 = (bf16[256,1152]{1,0:T(8,128)(2,1)S(1)}, bf16[256,1152]{1,0:T(8,128)(2,1)S(1)}, u32[]{:S(2)}, u32[]{:S(2)}) collective-permute-start(bf16[256,1152]{1,0:T(8,128)(2,1)S(1)} %pad_maximum_fusion.1.rest_0_), channel_id=1, source_target_pairs={{0,12},{4,8},{8,4},{12,0},{1,13},{5,9},{9,5},{13,1},{2,14},{6,10},... | collective-permute-start | bytes 1769480 | tf_op jit(solution)/shard_map/ppermute | solution.py:363
  69.4 49.8 %collective-permute-start.26 = (bf16[256,1152]{1,0:T(8,128)(2,1)S(1)}, bf16[256,1152]{1,0:T(8,128)(2,1)S(1)}, u32[]{:S(2)}, u32[]{:S(2)}) collective-permute-start(bf16[256,1152]{1,0:T(8,128)(2,1)S(1)} %pad_maximum_fusion.1.rest_0_), channel_id=1, source_target_pairs={{0,8},{4,12},{8,0},{12,4},{1,9},{5,13},{9,1},{13,5},{2,10},{6,14},... | collective-permute-start | bytes 1769480 | tf_op jit(solution)/shard_map/ppermute | solution.py:363
  72.1 47.2 %collective-permute-start.25 = (bf16[256,1152]{1,0:T(8,128)(2,1)S(1)}, bf16[256,1152]{1,0:T(8,128)(2,1)S(1)}, u32[]{:S(2)}, u32[]{:S(2)}) collective-permute-start(bf16[256,1152]{1,0:T(8,128)(2,1)S(1)} %pad_maximum_fusion.1.rest_0_), channel_id=1, source_target_pairs={{0,4},{4,0},{8,12},{12,8},{1,5},{5,1},{9,13},{13,9},{2,6},{6,2},{1... | collective-permute-start | bytes 1769480 | tf_op jit(solution)/shard_map/ppermute | solution.py:363
  72.4 20.0 %collective-permute-start.14 = (bf16[64,1024]{1,0:T(8,128)(2,1)S(1)}, bf16[64,1024]{1,0:T(8,128)(2,1)S(1)}, u32[]{:S(2)}, u32[]{:S(2)}) collective-permute-start(bf16[64,1024]{1,0:T(8,128)(2,1)S(1)} %get-tuple-element.74), channel_id=1, source_target_pairs={{0,2},{1,3},{2,0},{3,1},{16,18},{17,19},{18,16},{19,17},{4,6},{5,7... | collective-permute-start | bytes 393224 | tf_op jit(solution)/shard_map/ppermute | solution.py:366
  73.4 23.2 %collective-permute-start.15 = (bf16[64,1024]{1,0:T(8,128)(2,1)S(1)}, bf16[64,1024]{1,0:T(8,128)(2,1)S(1)}, u32[]{:S(2)}, u32[]{:S(2)}) collective-permute-start(bf16[64,1024]{1,0:T(8,128)(2,1)S(1)} %get-tuple-element.74), channel_id=1, source_target_pairs={{0,16},{1,17},{2,18},{3,19},{16,0},{17,1},{18,2},{19,3},{4,20},{5,... | collective-permute-start | bytes 393224 | tf_op jit(solution)/shard_map/ppermute | solution.py:366
  96.7 22.6 %collective-permute-start.24 = (bf16[256,1024]{1,0:T(8,128)(2,1)S(1)}, bf16[256,1024]{1,0:T(8,128)(2,1)S(1)}, u32[]{:S(2)}, u32[]{:S(2)}) collective-permute-start(bf16[256,1024]{1,0:T(8,128)(2,1)S(1)} %pad_maximum_fusion.3.cz_ref), channel_id=1, source_target_pairs={{0,1},{1,0},{2,3},{3,2},{16,17},{17,16},{18,19},{19,18},{4,5},{5,4... | collective-permute-start | bytes 1572872 | tf_op jit(solution)/shard_map/ppermute | solution.py:366
  99.6 19.7 %collective-permute-start.17 = (bf16[256,1024]{1,0:T(8,128)(2,1)S(1)}, bf16[256,1024]{1,0:T(8,128)(2,1)S(1)}, u32[]{:S(2)}, u32[]{:S(2)}) collective-permute-start(bf16[256,1024]{1,0:T(8,128)(2,1)S(1)} %constant_dynamic-update-slice_fusion.4.mz_ref), channel_id=1, source_target_pairs={{0,1},{1,0},{2,3},{3,2},{16,17},{17,16},{18,19},{19,18},{4,5},{5,4... | collective-permute-start | bytes 1572872 | tf_op jit(solution)/shard_map/ppermute | solution.py:366
  122.4 16.1 %collective-permute-start.28 = (bf16[256,1024]{1,0:T(8,128)(2,1)S(1)}, bf16[256,1024]{1,0:T(8,128)(2,1)S(1)}, u32[]{:S(2)}, u32[]{:S(2)}) collective-permute-start(bf16[256,1024]{1,0:T(8,128)(2,1)S(1)} %get-tuple-element.76), channel_id=1, source_target_pairs={{0,1},{1,0},{2,3},{3,2},{16,17},{17,16},{18,19},{19,18},{4,5},{5,4... | collective-permute-start | bytes 1572872 | tf_op jit(solution)/shard_map/ppermute | solution.py:366
  129.7 76.3 %collective-permute-start.60 = (bf16[256,1152]{1,0:T(8,128)(2,1)S(1)}, bf16[256,1152]{1,0:T(8,128)(2,1)S(1)}, u32[]{:S(2)}, u32[]{:S(2)}) collective-permute-start(bf16[256,1152]{1,0:T(8,128)(2,1)S(1)} %get-tuple-element.107), channel_id=1, source_target_pairs={{0,4},{4,0},{8,12},{12,8},{1,5},{5,1},{9,13},{13,9},{2,6},{6,2},{1... | collective-permute-start | bytes 1769480 | tf_op jit(solution)/shard_map/ppermute | solution.py:363
  131.9 74.6 %collective-permute-start.61 = (bf16[256,1152]{1,0:T(8,128)(2,1)S(1)}, bf16[256,1152]{1,0:T(8,128)(2,1)S(1)}, u32[]{:S(2)}, u32[]{:S(2)}) collective-permute-start(bf16[256,1152]{1,0:T(8,128)(2,1)S(1)} %get-tuple-element.108), channel_id=1, source_target_pairs={{0,8},{4,12},{8,0},{12,4},{1,9},{5,13},{9,1},{13,5},{2,10},{6,14},... | collective-permute-start | bytes 1769480 | tf_op jit(solution)/shard_map/ppermute | solution.py:363
  133.9 72.6 %collective-permute-start.62 = (bf16[256,1152]{1,0:T(8,128)(2,1)S(1)}, bf16[256,1152]{1,0:T(8,128)(2,1)S(1)}, u32[]{:S(2)}, u32[]{:S(2)}) collective-permute-start(bf16[256,1152]{1,0:T(8,128)(2,1)S(1)} %get-tuple-element.109), channel_id=1, source_target_pairs={{0,12},{4,8},{8,4},{12,0},{1,13},{5,9},{9,5},{13,1},{2,14},{6,10},... | collective-permute-start | bytes 1769480 | tf_op jit(solution)/shard_map/ppermute | solution.py:363
  137.3 37.9 %collective-permute-start.41 = (bf16[64,1024]{1,0:T(8,128)(2,1)S(1)}, bf16[64,1024]{1,0:T(8,128)(2,1)S(1)}, u32[]{:S(2)}, u32[]{:S(2)}) collective-permute-start(bf16[64,1024]{1,0:T(8,128)(2,1)S(1)} %get-tuple-element.83.rest_0_), channel_id=1, source_target_pairs={{0,12},{4,8},{8,4},{12,0},{1,13},{5,9},{9,5},{13,1},{2,14},{6,10},... | collective-permute-start | bytes 393224 | tf_op jit(solution)/shard_map/ppermute | solution.py:363
  138.7 57.0 %collective-permute-start.40 = (bf16[64,1024]{1,0:T(8,128)(2,1)S(1)}, bf16[64,1024]{1,0:T(8,128)(2,1)S(1)}, u32[]{:S(2)}, u32[]{:S(2)}) collective-permute-start(bf16[64,1024]{1,0:T(8,128)(2,1)S(1)} %get-tuple-element.83.rest_0_), channel_id=1, source_target_pairs={{0,8},{4,12},{8,0},{12,4},{1,9},{5,13},{9,1},{13,5},{2,10},{6,14},... | collective-permute-start | bytes 393224 | tf_op jit(solution)/shard_map/ppermute | solution.py:363
  175.2 22.6 %collective-permute-start.39 = (bf16[64,1024]{1,0:T(8,128)(2,1)S(1)}, bf16[64,1024]{1,0:T(8,128)(2,1)S(1)}, u32[]{:S(2)}, u32[]{:S(2)}) collective-permute-start(bf16[64,1024]{1,0:T(8,128)(2,1)S(1)} %get-tuple-element.83.rest_0_), channel_id=1, source_target_pairs={{0,4},{4,0},{8,12},{12,8},{1,5},{5,1},{9,13},{13,9},{2,6},{6,2},{1... | collective-permute-start | bytes 393224 | tf_op jit(solution)/shard_map/ppermute | solution.py:363
  220.3 22.6 %collective-permute-start.56 = (bf16[512,512]{1,0:T(8,128)(2,1)S(1)}, bf16[512,512]{1,0:T(8,128)(2,1)S(1)}, u32[]{:S(2)}, u32[]{:S(2)}) collective-permute-start(bf16[512,512]{1,0:T(8,128)(2,1)S(1)} %get-tuple-element.103), channel_id=1, source_target_pairs={{0,1},{1,0},{2,3},{3,2},{16,17},{17,16},{18,19},{19,18},{4,5},{5,4... | collective-permute-start | bytes 1572872 | tf_op jit(solution)/shard_map/ppermute | solution.py:366
  220.3 26.4 %collective-permute-start.52 = (bf16[512,1024]{1,0:T(8,128)(2,1)S(1)}, bf16[512,1024]{1,0:T(8,128)(2,1)S(1)}, u32[]{:S(2)}, u32[]{:S(2)}) collective-permute-start(bf16[512,1024]{1,0:T(8,128)(2,1)S(1)} %get-tuple-element.101), channel_id=1, source_target_pairs={{0,1},{1,0},{2,3},{3,2},{16,17},{17,16},{18,19},{19,18},{4,5},{5,4... | collective-permute-start | bytes 3145736 | tf_op jit(solution)/shard_map/ppermute | solution.py:366
  (68 other events, 711.0 us)

commit v2 on v1

v2 whole, which is shorter than its diff:
```python
import functools
import math

import jax
import jax.numpy as jnp
from jax import lax
from jax.experimental import pallas as pl
from jax.experimental.pallas import tpu as pltpu
from jax.sharding import PartitionSpec as P

D = 1024
HD = 128
STEP = 10

EPSILON = 1e-06
THETA_BASE = 1000000.0
BETA_FIRST = 0.9
BETA_SECOND = 0.95
ADAM_EPSILON = 1e-08
MATRIX_RATE = 0.04
MATRIX_DECAY = 0.1
GAIN_RATE = 0.5
MASK_VALUE = -1e30
LANE = 128
BLOCKS = D // LANE
PLANE = ("dp", "col")
F32 = jnp.float32
BF16 = jnp.bfloat16


def mm(left, right):
    return jnp.dot(left, right, preferred_element_type=F32)


def mm_nt(left, right):
    return lax.dot_general(left, right, (((1,), (1,)), ((), ())), preferred_element_type=F32)


def mm_tn(left, right):
    return lax.dot_general(left, right, (((0,), (0,)), ((), ())), preferred_element_type=F32)


def lanes(block):
    return pl.ds(pl.multiple_of(block * LANE, LANE), LANE)


def rows_of(block, size):
    return pl.ds(pl.multiple_of(block * size, size), size)


def call(kernel, outs, *args, scalars=0, scratch=(), hbm=0, ties=0, limit=16):
    vmem = pl.BlockSpec(memory_space=pltpu.VMEM)
    smem = pl.BlockSpec(memory_space=pltpu.SMEM)
    return pl.pallas_call(
        kernel,
        out_shape=list(outs),
        in_specs=[smem] * scalars + [pl.BlockSpec(memory_space=pltpu.HBM)] * hbm
        + [vmem] * (len(args) - scalars - hbm - ties) + [pl.BlockSpec(memory_space=pl.ANY)] * ties,
        out_specs=[vmem] * len(outs),
        scratch_shapes=list(scratch),
        name=(kernel.func if hasattr(kernel, "func") else kernel).__name__,
        compiler_params=pltpu.CompilerParams(vmem_limit_bytes=limit << 20),
        cost_estimate=pl.CostEstimate(flops=1, bytes_accessed=1, transcendentals=0),
    )(*args)


def after(value, *others):
    return lax.optimization_barrier((value, *others))[0]


def shape(dims, dtype):
    return jax.ShapeDtypeStruct(tuple(dims), dtype)


def adamw(weight, first, second, grad, rate, decay):
    first_new = BETA_FIRST * first + (1.0 - BETA_FIRST) * grad
    second_new = BETA_SECOND * second + (1.0 - BETA_SECOND) * grad * grad
    first_hat = first_new / (1.0 - BETA_FIRST**STEP)
    second_hat = second_new / (1.0 - BETA_SECOND**STEP)
    weight_new = weight - rate * (
        first_hat / (jnp.sqrt(second_hat) + ADAM_EPSILON) + decay * weight
    )
    return (weight_new, first_new, second_new)


def gain_of(gains_ref, which):
    at = 2 * D + which * HD
    return gains_ref[:, at:at + HD]


def tables_kernel(pos_ref, seg_ref, cos_ref, sin_ref, mask_ref):
    length, half = pos_ref.shape[1], HD // 2
    column = jnp.broadcast_to(pos_ref[...].astype(F32), (HD, length)).T
    lane = lax.broadcasted_iota(jnp.int32, (1, HD), 1)
    step = (lane & (half - 1)).astype(F32) * (2.0 / HD)
    angle = column * jnp.exp(step * -math.log(THETA_BASE))
    cos_ref[...] = jnp.cos(angle)
    sine = jnp.sin(angle)
    sin_ref[...] = jnp.where(lane < half, -sine, sine)
    seg = jnp.broadcast_to(seg_ref[...].astype(F32), (length, length))
    i = lax.broadcasted_iota(jnp.int32, (length, length), 0)
    j = lax.broadcasted_iota(jnp.int32, (length, length), 1)
    mask_ref[...] = jnp.where((seg == seg.T) & (j <= i), 1.0, 0.0)


def attend_kernel(n, place, *rest):
    blocks = len(rest) - n - 14
    xs, ws, (gains_ref, cos_ref, sin_ref, mask_ref, ctx_ref, prob_ref, q_ref, k_ref, v_ref, raw_ref, norm_ref, x_ref,
             cot_ref, w_ref) = rest[:n], rest[n:n + blocks], rest[n + blocks:]
    height = D // blocks
    for i, w in enumerate(ws):
        w_ref[i * height:(i + 1) * height, :] = w[...]
    z = place[0]
    part = D // n
    for k in range(n):
        x_ref[:, k * part:(k + 1) * part] = xs[k][:x_ref.shape[0], :]
        cot_ref[:, k * part:(k + 1) * part] = xs[k][x_ref.shape[0]:2 * x_ref.shape[0], :]
    x = x_ref[...].astype(F32)
    r1 = lax.rsqrt(jnp.mean(x * x, axis=-1, keepdims=True) + EPSILON)
    for j in range(BLOCKS):
        b = place[1 + j]
        block = x_ref[:, lanes(b ^ (2 * z))].astype(F32)
        norm_ref[:, j * LANE:(j + 1) * LANE] = (block * r1 * gains_ref[:, lanes(b)]).astype(BF16)
    qw, kw = q_ref.shape[1], k_ref.shape[1]
    qkv = mm(norm_ref[...], w_ref[:, :qw + 2 * kw])
    raw_ref[...] = qkv[:, :qw + kw]
    v_ref[...] = qkv[:, qw + kw:].astype(BF16)
    cosine, sine = cos_ref[...], sin_ref[...]
    for h in range((qw + kw) // HD):
        part = qkv[:, h * HD:(h + 1) * HD]
        is_q = h * HD < qw
        gain = gain_of(gains_ref, 0 if is_q else 1)
        part = part * lax.rsqrt(jnp.mean(part * part, axis=-1, keepdims=True) + EPSILON) * gain
        part = (part * cosine + pltpu.roll(part, HD // 2, 1) * sine).astype(BF16)
        if is_q:
            q_ref[:, h * HD:(h + 1) * HD] = part
        else:
            at = h * HD - qw
            k_ref[:, at:at + HD] = part
    length = x.shape[0]
    allowed = mask_ref[...] > 0.5
    heads, groups = qw // HD, kw // HD
    for h in range(heads):
        g = h * groups // heads
        s = mm_nt(q_ref[:, h * HD:(h + 1) * HD], k_ref[:, g * HD:(g + 1) * HD]) * HD ** (-0.5)
        s = jnp.where(allowed, s, MASK_VALUE)
        peak = jnp.max(s, axis=-1, keepdims=True)
        total = peak + jnp.log(jnp.sum(jnp.exp(s - peak), axis=-1, keepdims=True))
        p = jnp.exp(s - total)
        prob_ref[h * length:(h + 1) * length, :] = p
        ctx_ref[:, h * HD:(h + 1) * HD] = mm(p.astype(BF16), v_ref[:, g * HD:(g + 1) * HD]).astype(BF16)


def branch_kernel(place, ctx_ref, w_ref, own_ref, *rest):
    sends, scratch = rest[:-1], rest[-1]
    z = place[0]
    here = w_ref.shape[1] - ctx_ref.shape[1]
    scratch[...] = mm_nt(ctx_ref[...], w_ref[:, here:])
    size = own_ref.shape[0]
    for k, out in enumerate((own_ref,) + sends):
        to = z ^ k
        for j in range(BLOCKS):
            b = place[1 + j]
            out[:, lanes(b ^ (2 * to))] = scratch[rows_of(to, size), j * LANE:(j + 1) * LANE].astype(out.dtype)


def mid_kernel(n, place, x_ref, gains_ref, *rest):
    terms, (resid_ref, mid_ref) = rest[:n], rest[n:]
    z = place[0]
    size = resid_ref.shape[0]
    resid = x_ref[rows_of(z, size), :].astype(F32)
    total = terms[0][...].astype(F32)
    for term in terms[1:]:
        total = total + term[...].astype(F32)
    resid = resid + total
    resid_ref[...] = resid
    scale = lax.rsqrt(jnp.mean(resid * resid, axis=-1, keepdims=True) + EPSILON)
    for j in range(BLOCKS):
        at = slice(j * LANE, (j + 1) * LANE)
        mid_ref[:, at] = (resid[:, at] * scale * gains_ref[:, lanes(BLOCKS + (j ^ (2 * z)))]).astype(BF16)


def units_math(gate, up, dhidden):
    sigmoid = jax.nn.sigmoid(gate)
    hidden = (gate * sigmoid * up).astype(BF16)
    dgate = (dhidden * up * sigmoid * (1.0 + gate * (1.0 - sigmoid))).astype(BF16)
    dup = (dhidden * gate * sigmoid).astype(BF16)
    return hidden, dgate, dup


def units_kernel(n, place, cot_ref, wz_ref, wo_ref, *rest):
    pieces, outs = rest[:n], rest[n:2 * n]
    mid_ref, hid_ref, dgu_ref, dmid_ref = rest[2 * n:]
    z = place[0]
    size = pieces[0].shape[0]
    part = D // n
    for k in range(n):
        for q in range(n):
            mid_ref[rows_of(z ^ k, size), q * part:(q + 1) * part] = (
                pieces[k][:, (q ^ k) * part:((q ^ k) + 1) * part])
    mid = mid_ref[...]
    cot = cot_ref[...]
    units = wz_ref.shape[1]
    for i, w in enumerate((wz_ref, wo_ref)):
        hidden, dgate, dup = units_math(mm_nt(mid, w[0]), mm_nt(mid, w[1]), mm_nt(cot, w[2]))
        at = slice(i * units, (i + 1) * units)
        hid_ref[:, at] = hidden
        dgu_ref[0, :, at] = dgate
        dgu_ref[1, :, at] = dup
        term = mm(dgate, w[0]) + mm(dup, w[1])
        dmid_ref[...] = term if i == 0 else dmid_ref[...] + term
    for k, out in enumerate(outs):
        out[...] = dmid_ref[rows_of(z ^ k, size), :].astype(out.dtype)


def units_grad_kernel(cot_ref, mid_ref, hid_ref, dgu_ref, gz_ref, go_ref):
    units = gz_ref.shape[1]
    for i, g in ((1, go_ref), (0, gz_ref)):
        at = slice(i * units, (i + 1) * units)
        g[0] = mm_tn(dgu_ref[0, :, at], mid_ref[...]).astype(g.dtype)
        g[1] = mm_tn(dgu_ref[1, :, at], mid_ref[...]).astype(g.dtype)
        g[2] = mm_tn(hid_ref[:, at], cot_ref[...]).astype(g.dtype)


def down_kernel(n, place, hid_ref, wz_ref, wo_ref, resid_ref, *rest):
    outs, total_ref = rest[:n], rest[n]
    units = wz_ref.shape[1]
    size = resid_ref.shape[0]
    total_ref[...] = mm(hid_ref[:, :units], wz_ref[2]) + mm(hid_ref[:, units:], wo_ref[2])
    own = rows_of(place[0], size)
    total_ref[own, :] = total_ref[own, :] + resid_ref[...]
    width = outs[0].shape[1]
    for k, out in enumerate(outs):
        out[...] = total_ref[:, k * width:(k + 1) * width].astype(out.dtype)


def pack_units_kernel(n, place, *rest):
    sources, (x_ref, cot_in_ref), outs, (g, u, d, scratch, sems) = rest[:3], rest[3:5], rest[6:6 + n], rest[6 + n:]
    copies = [pltpu.make_async_copy(src, dst, sems.at[i]) for i, (src, dst) in enumerate(zip(sources, (g, u, d)))]
    for copy in copies:
        copy.start()
    length = 2 * x_ref.shape[0]
    size = (outs[0].shape[0] - length) // 3
    for out in outs:
        out[:length // 2, :] = x_ref[...]
        out[length // 2:length, :] = cot_in_ref[...]
    for i, (copy, ref) in enumerate(zip(copies, (g, u, d))):
        copy.wait()
        scratch[...] = ref[...].T.astype(BF16)
        for k, out in enumerate(outs):
            out[length + i * size:length + (i + 1) * size, :] = scratch[rows_of(place[0] ^ k, size), :]


def join_kernel(n, *rest):
    pieces, out_ref = rest[:n], rest[-1]
    size, width = out_ref.shape[1], pieces[0].shape[1]
    length = pieces[0].shape[0] - 3 * size
    for k, piece in enumerate(pieces):
        for i in range(3):
            out_ref[i, :, k * width:(k + 1) * width] = piece[length + i * size:length + (i + 1) * size, :]


def units_update_kernel(n, place, *rest):
    pieces, states, outs, scratch = rest[:n], rest[n:n + 9], rest[n + 9:n + 18], rest[n + 18]
    size = scratch.shape[0] // n
    length = pieces[0].shape[0] - 3 * size
    for i in range(3):
        for k in range(n):
            scratch[rows_of(place[0] ^ k, size), :] = pieces[k][length + i * size:length + (i + 1) * size, :].astype(F32)
        w, m, v = (ref[...] for ref in states[3 * i:3 * i + 3])
        for ref, value in zip(outs[3 * i:3 * i + 3], adamw(w, m, v, scratch[...].T, MATRIX_RATE, MATRIX_DECAY)):
            ref[...] = value


def update_kernel(n, count, *rest):
    terms, states, outs = rest[:n], rest[n:n + 3 * count], rest[n + 3 * count:]
    total = terms[0][...].astype(F32)
    for term in terms[1:]:
        total = total + term[...].astype(F32)
    at = 0
    for i in range(count):
        w, m, v = (ref[...] for ref in states[3 * i:3 * i + 3])
        grad = total[:, at:at + w.shape[1]]
        at += w.shape[1]
        for ref, value in zip(outs[3 * i:3 * i + 3], adamw(w, m, v, grad, MATRIX_RATE, MATRIX_DECAY)):
            ref[...] = value


def pack_kernel(*rest):
    sources, out_ref, (q, k, v, o, sems) = rest[:4], rest[4], rest[5:]
    copies = [pltpu.make_async_copy(src, dst, sems.at[i]) for i, (src, dst) in enumerate(zip(sources, (q, k, v, o)))]
    for copy in copies:
        copy.start()
    at = 0
    for copy, ref in zip(copies, (q, k, v, o)):
        copy.wait()
        out_ref[:, at:at + ref.shape[1]] = ref[...].astype(BF16)
        at += ref.shape[1]


def mid_back_kernel(n, place, resid_ref, cot_ref, gains_ref, *rest):
    terms, (grad_ref, gain_ref, dmid_ref) = rest[:n], rest[n:]
    z = place[0]
    part = D // n
    for k, term in enumerate(terms):
        for q in range(n):
            at = slice(q * part, (q + 1) * part)
            value = term[:, (q ^ k) * part:((q ^ k) + 1) * part].astype(F32)
            dmid_ref[:, at] = value if k == 0 else dmid_ref[:, at] + value
    dmid = dmid_ref[...]
    resid = resid_ref[...]
    cot = cot_ref[rows_of(z, resid.shape[0]), :].astype(F32)
    r2 = lax.rsqrt(jnp.mean(resid * resid, axis=-1, keepdims=True) + EPSILON)
    inner = None
    for j in range(BLOCKS):
        at = slice(j * LANE, (j + 1) * LANE)
        b = j ^ (2 * z)
        part = dmid[:, at] * gains_ref[:, lanes(BLOCKS + b)] * resid[:, at]
        inner = part if inner is None else inner + part
        gain_ref[:, lanes(b)] = jnp.sum(dmid[:, at] * resid[:, at] * r2, axis=0, keepdims=True)
    inner = jnp.sum(inner, axis=-1, keepdims=True)
    back = r2 * r2 * r2 * inner / D
    for j in range(BLOCKS):
        at = slice(j * LANE, (j + 1) * LANE)
        grad_ref[:, at] = (
            cot[:, at] + r2 * gains_ref[:, lanes(BLOCKS + (j ^ (2 * z)))] * dmid[:, at] - resid[:, at] * back
        ).astype(BF16)


def attend_back_kernel(n, place, *rest):
    pieces, (w_ref, prob_ref, q_ref, k_ref, v_ref, raw_ref, gains_ref, cos_ref, sin_ref,
             dqkv_ref, dgq_ref, dgk_ref, dbr_ref) = rest[:n], rest[n:]
    z = place[0]
    size = pieces[0].shape[0]
    for k in range(n):
        frm = z ^ k
        for j in range(BLOCKS):
            b = place[1 + j]
            dbr_ref[rows_of(frm, size), j * LANE:(j + 1) * LANE] = pieces[k][:, lanes(b ^ (2 * frm))]
    here = dqkv_ref.shape[1]
    dctx = mm(dbr_ref[...], w_ref[:, here:]).astype(BF16)
    qw, kw = q_ref.shape[1], k_ref.shape[1]
    heads, groups = qw // HD, kw // HD
    length = dbr_ref.shape[0]
    cosine, sine = cos_ref[...], sin_ref[...]

    def back(grad, h, gain):
        grad = grad * cosine - pltpu.roll(grad, HD // 2, 1) * sine
        value = raw_ref[:, h * HD:(h + 1) * HD]
        factor = lax.rsqrt(jnp.mean(value * value, axis=-1, keepdims=True) + EPSILON)
        inner = jnp.sum(grad * gain * value, axis=-1, keepdims=True)
        out = factor * gain * grad - value * (factor * factor * factor) * inner / HD
        return out.astype(BF16), jnp.sum(grad * value * factor, axis=0, keepdims=True)

    dgq = dgk = None
    for g in range(groups):
        dk = dv = None
        keys = k_ref[:, g * HD:(g + 1) * HD]
        vals = v_ref[:, g * HD:(g + 1) * HD]
        for h in range(g * heads // groups, (g + 1) * heads // groups):
            hs = slice(h * HD, (h + 1) * HD)
            p = prob_ref[h * length:(h + 1) * length, :]
            dp = mm_nt(dctx[:, hs], vals)
            delta = jnp.sum(p * dp, axis=-1, keepdims=True)
            ds = (p * (dp - delta)).astype(BF16)
            dq, gain_part = back(mm(ds, keys) * HD ** (-0.5), h, gain_of(gains_ref, 0))
            dqkv_ref[:, hs] = dq
            dgq = gain_part if dgq is None else dgq + gain_part
            dk_h = mm_tn(ds, q_ref[:, hs])
            dv_h = mm_tn(p.astype(BF16), dctx[:, hs])
            dk = dk_h if dk is None else dk + dk_h
            dv = dv_h if dv is None else dv + dv_h
        dk, gain_part = back(dk * HD ** (-0.5), heads + g, gain_of(gains_ref, 1))
        dgk = gain_part if dgk is None else dgk + gain_part
        dqkv_ref[:, qw + g * HD:qw + (g + 1) * HD] = dk
        dqkv_ref[:, qw + kw + g * HD:qw + kw + (g + 1) * HD] = dv.astype(BF16)
    dgq_ref[...] = dgq
    dgk_ref[...] = dgk


def weight_grad_kernel(norm_ref, dqkv_ref, dbr_ref, ctx_ref, gz_ref, *outs):
    half = D // 2
    here = dqkv_ref.shape[1]
    step = half // len(outs)
    for left, right, cols in ((norm_ref, dqkv_ref, slice(0, here)), (dbr_ref, ctx_ref, slice(here, None))):
        other = mm_tn(left[:, half:], right[...]).astype(BF16)
        for i, out in enumerate(outs):
            out[:, cols] = other[i * step:(i + 1) * step, :]
    gz_ref[:, :here] = mm_tn(norm_ref[:, :half], dqkv_ref[...])
    gz_ref[:, here:] = mm_tn(dbr_ref[:, :half], ctx_ref[...])


def pair_sum_kernel(n, own_ref, *rest):
    others, outs = rest[:n], rest[n:]
    step = own_ref.shape[0] // n
    for i, (other, out) in enumerate(zip(others, outs)):
        out[...] = (own_ref[i * step:(i + 1) * step, :] + other[...].astype(F32)).astype(out.dtype)


def input_grad_kernel(n, count, place, dqkv_ref, w_ref, x_ref, gains_ref, *rest):
    units, rest = rest[:count], rest[count + 1:]
    outs, gain_ref, dn_ref, term_ref = rest[:n], rest[n], rest[n + 1], rest[n + 2]
    z = place[0]
    dn_ref[...] = mm_nt(dqkv_ref[...], w_ref[:, :dqkv_ref.shape[1]])
    x = x_ref[...].astype(F32)
    r1 = lax.rsqrt(jnp.mean(x * x, axis=-1, keepdims=True) + EPSILON)
    inner = None
    for j in range(BLOCKS):
        b = place[1 + j]
        dn = dn_ref[:, j * LANE:(j + 1) * LANE]
        xb = x_ref[:, lanes(b ^ (2 * z))].astype(F32)
        part = dn * gains_ref[:, lanes(b)] * xb
        inner = part if inner is None else inner + part
        gain_ref[:, lanes(b)] = jnp.sum(dn * xb * r1, axis=0, keepdims=True)
    inner = jnp.sum(inner, axis=-1, keepdims=True)
    back = r1 * r1 * r1 * inner / D
    for j in range(BLOCKS):
        b = place[1 + j]
        at = lanes(b ^ (2 * z))
        xb = x_ref[:, at].astype(F32)
        term_ref[:, at] = r1 * gains_ref[:, lanes(b)] * dn_ref[:, j * LANE:(j + 1) * LANE] - xb * back
    width = outs[0].shape[1]
    length = x.shape[0]
    for k, out in enumerate(outs):
        out[:length, :] = term_ref[:, k * width:(k + 1) * width].astype(out.dtype)
    if count:
        size = units[0].shape[1]
        for i in range(3):
            total = units[0][i]
            for unit in units[1:]:
                total = total + unit[i].astype(F32)
            for k, out in enumerate(outs):
                out[length + i * size:length + (i + 1) * size, :] = total[:, k * width:(k + 1) * width].astype(out.dtype)


def act_grad_kernel(n, place, *rest):
    pieces, terms, out_ref = rest[:n], rest[n:2 * n], rest[2 * n]
    z = place[0]
    width = out_ref.shape[1]
    size = pieces[0].shape[0]
    for k in range(n):
        at = rows_of(z ^ k, size)
        total = terms[0][at, :].astype(F32)
        for term in terms[1:]:
            total = total + term[at, :].astype(F32)
        out_ref[at, :] = pieces[k][:, k * width:(k + 1) * width].astype(F32) + total


def act_out_kernel(*rest):
    terms, out_ref = rest[:-1], rest[-1]
    total = terms[0][...].astype(F32)
    for term in terms[1:]:
        total = total + term[...].astype(F32)
    out_ref[...] = total.astype(BF16)


def body(sizes, act_in, act_cot, segments, positions, gains, gains_first, gains_second,
         query_weight, query_first, query_second, key_weight, key_first, key_second,
         value_weight, value_first, value_second, output_weight, output_first, output_second,
         gate_weight, gate_first, gate_second, up_weight, up_first, up_second,
         down_weight, down_first, down_second):
    n_dp, n_row, n_col = sizes
    n_plane = n_dp * n_col
    paired = n_dp == 2 and n_col == 4
    z = lax.axis_index("row").astype(jnp.int32)
    p = lax.axis_index(PLANE).astype(jnp.int32)

    def over_row(value, k):
        return lax.ppermute(value, "row", [(i, i ^ k) for i in range(n_row)])

    def over_plane(value, k):
        return lax.ppermute(value, PLANE, [(i, i ^ k) for i in range(n_plane)])

    def gather_row(value):
        return [value] + [over_row(value, k) for k in range(1, n_row)]

    def scatter_row(values):
        return [values[0]] + [over_row(values[k], k) for k in range(1, n_row)]

    def near_plane(value, axis=0):
        if not paired:
            return lax.all_gather(value, PLANE, axis=axis, tiled=True)
        return jnp.concatenate([value] + [over_plane(value, k) for k in (2, 4, 6)], axis=axis)

    def far_plane(same, axis=0):
        if not paired:
            return tuple(jnp.split(same, 2, axis=axis))
        return same, over_plane(same, 1)

    def gather_plane(value, axis=0):
        return far_plane(near_plane(value, axis), axis)

    def pair_plane(same, other, axis=0):
        if not paired:
            whole = jnp.concatenate([same.astype(F32), other.astype(F32)], axis=axis)
            return [lax.psum_scatter(whole, PLANE, scatter_dimension=axis, tiled=True)]
        total = same.astype(F32) + over_plane(other, 1).astype(F32)
        parts = jnp.split(total, 4, axis=axis)
        return parts[:1] + [part.astype(BF16) for part in parts[1:]]

    def rest_plane(parts):
        return list(parts[:1]) + [over_plane(part, k) for part, k in zip(parts[1:], (2, 4, 6))]

    def add(terms):
        out = terms[0].astype(F32)
        for term in terms[1:]:
            out = out + term.astype(F32)
        return out

    def sum_all(value):
        if not paired:
            return lax.psum(value, ("dp", "row", "col"))
        value = value + over_plane(value, 1)
        value = value + over_plane(value, 2) + over_plane(value, 4) + over_plane(value, 6)
        return value + over_row(value, 1) + over_row(value, 2) + over_row(value, 3)

    order = jnp.array([0, 2, 4, 6, 1, 3, 5, 7], jnp.int32) ^ p if paired else jnp.arange(BLOCKS, dtype=jnp.int32)
    place = jnp.concatenate([z[None], order])

    length, width = act_in.shape
    size = length // n_row
    qw, kw = query_weight.shape[1], key_weight.shape[1]
    rows = query_weight.shape[0]
    units = gate_weight.shape[1]
    gain = gains[None, :]
    if rows % 16 == 0:
        (w_proj,) = call(
            pack_kernel, [shape((rows, 2 * qw + 2 * kw), BF16)],
            query_weight, key_weight, value_weight, output_weight, hbm=4, limit=56,
            scratch=[pltpu.VMEM((rows, w), F32) for w in (qw, kw, kw, qw)] + [pltpu.SemaphoreType.DMA((4,))])
    else:
        w_proj = jnp.concatenate([query_weight, key_weight, value_weight, output_weight], axis=1).astype(BF16)
    if paired:
        near = [w_proj] + [over_plane(w_proj, k) for k in (2, 4, 6)]
    else:
        near = list(jnp.split(lax.all_gather(w_proj, PLANE, axis=0, tiled=True), 2, axis=0))
    share = units // n_row
    small = share % 16 != 0
    if small:
        joined = jnp.stack([gate_weight, up_weight, down_weight]).astype(BF16).transpose(0, 2, 1)
        parts = [lax.dynamic_slice_in_dim(joined, (z ^ k) * share, share, 1) for k in range(n_row)]
        units_mine = jnp.concatenate(scatter_row(parts), axis=2)
        xs = gather_row(jnp.concatenate([act_in, act_cot], axis=0))
    else:
        xs = call(
            functools.partial(pack_units_kernel, n_row), [shape((2 * length + 3 * share, width), BF16)] * n_row,
            place, gate_weight, up_weight, down_weight, act_in, act_cot, w_proj, scalars=1, hbm=3, ties=1, limit=48,
            scratch=[pltpu.VMEM((width, units), F32)] * 3
            + [pltpu.VMEM((units, width), BF16), pltpu.SemaphoreType.DMA((3,))])
        xs = scatter_row(xs)
    cosine, sine, mask = call(
        tables_kernel, [shape((length, HD), F32)] * 2 + [shape((length, length), F32)],
        positions[None, :], segments[None, :])
    w_parts = near + [over_plane(part, 1) for part in near] if paired else near

    heads = qw // HD
    context, probs, queries, keys, values, raw, normed, x_row, cot_row, w_proj = call(
        functools.partial(attend_kernel, n_row),
        [shape((length, qw), BF16), shape((heads * length, length), F32), shape((length, qw), BF16),
         shape((length, kw), BF16), shape((length, kw), BF16), shape((length, qw + kw), F32),
         shape((length, D), BF16), shape((length, D), BF16), shape((length, D), BF16),
         shape((D, 2 * qw + 2 * kw), BF16)],
        place, *xs, *w_parts, gain, cosine, sine, mask, scalars=1)
    if not small:
        (units_mine,) = call(functools.partial(join_kernel, n_row), [shape((3, share, D), BF16)],
                             *xs)
    units_near = near_plane(units_mine, axis=1)
    terms = call(
        branch_kernel,
        [shape((size, D), F32)] + [shape((size, D), BF16)] * (n_row - 1),
        place, context, w_proj,
        scalars=1, scratch=[pltpu.VMEM((length, D), F32)])
    terms = scatter_row(terms)
    resid, mid = call(
        functools.partial(mid_kernel, n_row),
        [shape((size, D), F32), shape((size, D), BF16)],
        place, x_row, gain, *terms, scalars=1)

    mids = gather_row(mid)
    units_z, units_o = far_plane(after(units_near, mid), axis=1)
    here = 2 * units_z.shape[1]
    *dmid_terms, mid_all, hidden, d_units = call(
        functools.partial(units_kernel, n_row),
        [shape((size, D), F32 if k == 0 else BF16) for k in range(n_row)]
        + [shape((length, D), BF16), shape((length, here), BF16), shape((2, length, here), BF16)],
        place, cot_row, units_z, units_o, *mids,
        scalars=1, scratch=[pltpu.VMEM((length, D), F32)])
    dmid_terms = scatter_row(dmid_terms)
    unit_grad_z, unit_grad_o = call(
        units_grad_kernel, [shape(units_z.shape, BF16)] * 2,
        cot_row, mid_all, hidden, d_units)
    unit_pair = pair_plane(unit_grad_z, unit_grad_o, axis=1)
    resid = after(resid, *unit_pair)
    unit_terms = rest_plane(unit_pair)
    branch_grad, mid_gain_grad = call(
        functools.partial(mid_back_kernel, n_row),
        [shape((size, D), BF16), shape((1, D), F32)],
        place, resid, cot_row, gain, *dmid_terms,
        scalars=1, scratch=[pltpu.VMEM((size, D), F32)])

    pieces = gather_row(branch_grad)
    down_terms = call(
        functools.partial(down_kernel, n_row),
        [shape((length, width), F32 if k == 0 else BF16) for k in range(n_row)],
        place, hidden, units_z, units_o, resid,
        scalars=1, scratch=[pltpu.VMEM((length, D), F32)])
    down_terms = scatter_row([after(term, *pieces) for term in down_terms])
    (act_out,) = call(act_out_kernel, [shape((length, width), BF16)], *down_terms)
    dqkv, query_gain_grad, key_gain_grad, dbranch = call(
        functools.partial(attend_back_kernel, n_row),
        [shape((length, qw + 2 * kw), BF16), shape((1, HD), F32), shape((1, HD), F32), shape((length, D), BF16)],
        place, *pieces, w_proj, probs, queries, keys, values, raw, gain, cosine, sine, scalars=1)
    merged = [] if small else unit_terms
    count = length if small else length + 3 * share
    *in_terms, in_gain_grad = call(
        functools.partial(input_grad_kernel, n_row, len(merged)),
        [shape((count, width), F32 if k == 0 else BF16) for k in range(n_row)] + [shape((1, D), F32)],
        place, dqkv, w_proj, x_row, gain, *merged, act_out,
        scalars=1, scratch=[pltpu.VMEM((length, D), F32)] * 2)
    cols = 2 * qw + 2 * kw
    grad_own, *grad_others = call(
        weight_grad_kernel,
        [shape((D // 2, cols), F32)] + [shape((D // 2 // 4, cols), BF16)] * 4,
        normed, dqkv, dbranch, after(context, in_terms[0]))
    if paired:
        grad_others = [over_plane(part, 1) for part in grad_others]
        proj_pair = call(functools.partial(pair_sum_kernel, 4),
                         [shape((rows, cols), F32 if i == 0 else BF16) for i in range(4)], grad_own, *grad_others)
        proj_terms = rest_plane(proj_pair)
    else:
        proj_pair = proj_terms = pair_plane(grad_own, jnp.concatenate(grad_others, axis=0))
    in_terms = scatter_row(in_terms)
    gains_grad = jnp.concatenate([in_gain_grad, mid_gain_grad, query_gain_grad, key_gain_grad], axis=1)
    gains_grad = sum_all(after(gains_grad, *proj_pair))[0]

    (act_grad,) = call(functools.partial(act_grad_kernel, n_row), [shape((length, width), F32)],
                       place, *pieces, *in_terms, scalars=1)
    states = (gate_weight, gate_first, gate_second, up_weight, up_first, up_second,
              down_weight, down_first, down_second)
    if small:
        unit_parts = scatter_row(jnp.split(add(unit_terms).astype(BF16), n_row, axis=2))
        whole = jnp.zeros((3, units, width), F32)
        for k, part in enumerate(unit_parts):
            whole = lax.dynamic_update_slice_in_dim(whole, part.astype(F32), (z ^ k) * share, 1)
        new_units = []
        for i in range(3):
            new_units += adamw(*states[3 * i:3 * i + 3], whole[i].T, MATRIX_RATE, MATRIX_DECAY)
    else:
        new_units = call(functools.partial(units_update_kernel, n_row), [shape((width, units), F32)] * 9,
                         place, *in_terms, *states,
                         scalars=1, scratch=[pltpu.VMEM((units, width), F32)])

    def update(terms, *states):
        return call(functools.partial(update_kernel, len(terms), len(states) // 3),
                    [shape(state.shape, F32) for state in states], *terms, *states)

    return (
        act_out,
        act_grad,
        *adamw(gains, gains_first, gains_second, gains_grad, GAIN_RATE, 0.0),
        *update(proj_terms, query_weight, query_first, query_second, key_weight, key_first, key_second,
                value_weight, value_first, value_second, output_weight, output_first, output_second),
        *new_units,
    )


def solution(mesh):
    token, proj, unit = P(PLANE, "row"), P(PLANE, "row"), P("row", PLANE)
    sizes = (mesh.shape["dp"], mesh.shape["row"], mesh.shape["col"])
    return jax.shard_map(
        functools.partial(body, sizes),
        mesh=mesh,
        in_specs=(token, token, P(PLANE), P(PLANE)) + (P(),) * 3 + (proj,) * 12 + (unit,) * 9,
        out_specs=(token, token) + (P(),) * 3 + (proj,) * 12 + (unit,) * 9,
        check_vma=False,
    )
```

time: 265 us -> 194 us (0.73)
  starting transfers between devices: 112 us -> 74 us
  waiting for transfers between devices: 105 us -> 78.5 us
  other arithmetic: 15 us -> 2.88 us
  Pallas kernels: 20.6 us -> 30.4 us
    ppermute x36 -> x26, starting transfers between devices: 55.1 us -> 20.8 us  [over_plane(): return lax.ppermute(value, PLANE, [(i, i ^ k) for i in range(n_plane)])]
    ppermute x36 -> x26, waiting for transfers between devices: 27.6 us -> 10 us  [over_plane(): return lax.ppermute(value, PLANE, [(i, i ^ k) for i in range(n_plane)])]
    pallas_call x13 -> x19, Pallas kernels: 20.6 us -> 30.4 us  [call(): pl.pallas_call(kernel, out_shape=list(outs), in_specs=[smem] * scalars +...]
    ppermute x27 -> x24, waiting for transfers between devices: 77.4 us -> 68.4 us  [over_row(): return lax.ppermute(value, 'row', [(i, i ^ k) for i in range(n_row)])]
    sub x5 -> x1, other arithmetic: 5.81 us -> 0.63 us  [adamw(): weight - rate * (first_hat / (jnp.sqrt(second_hat) + ADAM_EPSILON) + deca...]
    ppermute x27 -> x24, starting transfers between devices: 56.6 us -> 53.1 us  [over_row(): return lax.ppermute(value, 'row', [(i, i ^ k) for i in range(n_row)])]
    another operation x10 -> x1, other arithmetic: 3.91 us -> 1.22 us
    unnamed x67 -> x60, local copies, waits for them, and re-layouts: 4.26 us -> 6.82 us
  transfers between devices with their start and end apart: 63 -> 50, of which waited for: 21 -> 23; matrix products, arithmetic and copies ran while one was open for 8% -> 2% of each run, Pallas kernels for 7% -> 9%
where the time goes in v2:
time: 194 us
  waiting for transfers between devices  78.5 us (40%)
  starting transfers between devices  74 us (38%)
  Pallas kernels  30.4 us (16%)
  local copies, waits for them, and re-layouts  7.13 us (4%)
  other arithmetic  2.88 us (1%)
    ppermute x24, waiting for transfers between devices, over_row(): return lax.ppermute(value, 'row', [(i, i ^ k) for i in range(n_row)])  68.4 us
    ppermute x24, starting transfers between devices, over_row(): return lax.ppermute(value, 'row', [(i, i ^ k) for i in range(n_row)])  53.1 us
    pallas_call x19, Pallas kernels, call(): pl.pallas_call(kernel, out_shape=list(outs), in_specs=[smem] * scalars +...  30.4 us
    ppermute x26, starting transfers between devices, over_plane(): return lax.ppermute(value, PLANE, [(i, i ^ k) for i in range(n_plane)])  20.8 us
    ppermute x26, waiting for transfers between devices, over_plane(): return lax.ppermute(value, PLANE, [(i, i ^ k) for i in range(n_plane)])  10 us
    unnamed x60, local copies, waits for them, and re-layouts  6.82 us
  transfers between devices with their start and end apart: 50, of which 23 were waited for; matrix products, arithmetic and copies ran while one was open for 2% of the time, Pallas kernels for 9%

profile of v2, /device:TPU:0, one launch (start us, length us, event | category | flops | bytes accessed | tf_op | source)
XLA Modules:
  0.0 194.1 jit_solution(17542286724288747329)
XLA Ops:
  2.7 4.0 %collective-permute-start.5 = (bf16[128,1536]{1,0:T(8,128)(2,1)}, bf16[128,1536]{1,0:T(8,128)(2,1)S(1)}, u32[]{:S(2)}, u32[]{:S(2)}) collective-permute-start(bf16[128,1536]{1,0:T(8,128)(2,1)} %pack_kernel.1.rest_5_.rest_4_), channel_id=1, source_target_pairs={{0,18},{1,19},{2,16},{3,17},{16,2},{17,3},{18,0},{19,1},{4,22},{5,... | collective-permute-start | bytes 1179656 | tf_op jit(solution)/shard_map/ppermute | solution.py:472
  17.5 2.6 %collective-permute-start.1 = (bf16[800,256]{1,0:T(8,128)(2,1)S(1)}, bf16[800,256]{1,0:T(8,128)(2,1)S(1)}, u32[]{:S(2)}, u32[]{:S(2)}) collective-permute-start(bf16[800,256]{1,0:T(8,128)(2,1)S(1)} %get-tuple-element.113), channel_id=1, source_target_pairs={{0,8},{4,12},{8,0},{12,4},{1,9},{5,13},{9,1},{13,5},{2,10},{6,14},... | collective-permute-start | bytes 1228808 | tf_op jit(solution)/shard_map/ppermute | solution.py:469
  20.9 3.4 %collective-permute-done.4.rest_6_ = bf16[128,1536]{1,0:T(8,128)(2,1)S(1)} collective-permute-done((bf16[128,1536]{1,0:T(8,128)(2,1)}, bf16[128,1536]{1,0:T(8,128)(2,1)S(1)}, u32[]{:S(2)}, u32[]{:S(2)}) %collective-permute-start.4) | collective-permute-done | bytes 393248 | tf_op jit(solution)/shard_map/ppermute | solution.py:472
  24.9 8.9 %collective-permute-done.rest_1_ = bf16[800,256]{1,0:T(8,128)(2,1)S(1)} collective-permute-done((bf16[800,256]{1,0:T(8,128)(2,1)S(1)}, bf16[800,256]{1,0:T(8,128)(2,1)S(1)}, u32[]{:S(2)}, u32[]{:S(2)}) %collective-permute-start) | collective-permute-done | bytes 409632 | tf_op jit(solution)/shard_map/ppermute | solution.py:469
  33.8 14.6 %collective-permute-done.1.rest_2_ = bf16[800,256]{1,0:T(8,128)(2,1)S(1)} collective-permute-done((bf16[800,256]{1,0:T(8,128)(2,1)S(1)}, bf16[800,256]{1,0:T(8,128)(2,1)S(1)}, u32[]{:S(2)}, u32[]{:S(2)}) %collective-permute-start.1) | collective-permute-done | bytes 409632 | tf_op jit(solution)/shard_map/ppermute | solution.py:469
  52.6 3.3 %attend_kernel.1 = (bf16[256,512]{1,0:T(8,128)(2,1)S(1)}, f32[1024,256]{1,0:T(8,128)S(1)}, bf16[256,512]{1,0:T(8,128)(2,1)S(1)}, bf16[256,256]{1,0:T(8,128)(2,1)...) custom-call(s32[9]{0:T(128)S(1)} %pad_add_fusion.place, ...), custom_call_target="tpu_custom_call" | custom-call | flops 1 | bytes 1 | tf_op jit(solution)/shard_map/attend_kernel/pallas_call | solution.py:54
  57.1 7.1 %collective-permute-start.13 = (bf16[64,1024]{1,0:T(8,128)(2,1)S(1)}, bf16[64,1024]{1,0:T(8,128)(2,1)S(1)}, u32[]{:S(2)}, u32[]{:S(2)}) collective-permute-start(bf16[64,1024]{1,0:T(8,128)(2,1)S(1)} %get-tuple-element.123), channel_id=1, source_target_pairs={{0,4},{4,0},{8,12},{12,8},{1,5},{5,1},{9,13},{13,9},{2,6},{6,2},{1... | collective-permute-start | bytes 393224 | tf_op jit(solution)/shard_map/ppermute | solution.py:469
  67.2 4.0 %collective-permute-start.15 = (bf16[64,1024]{1,0:T(8,128)(2,1)S(1)}, bf16[64,1024]{1,0:T(8,128)(2,1)S(1)}, u32[]{:S(2)}, u32[]{:S(2)}) collective-permute-start(bf16[64,1024]{1,0:T(8,128)(2,1)S(1)} %get-tuple-element.125), channel_id=1, source_target_pairs={{0,12},{4,8},{8,4},{12,0},{1,13},{5,9},{9,5},{13,1},{2,14},{6,10},... | collective-permute-start | bytes 393224 | tf_op jit(solution)/shard_map/ppermute | solution.py:469
  71.2 3.1 %collective-permute-done.14.rest_2_ = bf16[64,1024]{1,0:T(8,128)(2,1)S(1)} collective-permute-done((bf16[64,1024]{1,0:T(8,128)(2,1)S(1)}, bf16[64,1024]{1,0:T(8,128)(2,1)S(1)}, u32[]{:S(2)}, u32[]{:S(2)}) %collective-permute-start.14) | collective-permute-done | bytes 131104 | tf_op jit(solution)/shard_map/ppermute | solution.py:469
  75.1 2.7 %collective-permute-done.11 = bf16[3,96,1024]{2,1,0:T(8,128)(2,1)S(1)} collective-permute-done((bf16[3,96,1024]{2,1,0:T(8,128)(2,1)S(1)}, bf16[3,96,1024]{2,1,0:T(8,128)(2,1)S(1)}, u32[]{:S(2)}, u32[]{:S(2)}) %collective-permute-start.11) | collective-permute-done | bytes 589856 | tf_op jit(solution)/shard_map/ppermute | solution.py:472
  80.7 3.4 %collective-permute-start.18 = (bf16[64,1024]{1,0:T(8,128)(2,1)S(1)}, bf16[64,1024]{1,0:T(8,128)(2,1)S(1)}, u32[]{:S(2)}, u32[]{:S(2)}) collective-permute-start(bf16[64,1024]{1,0:T(8,128)(2,1)S(1)} %get-tuple-element.126.rest_0_), channel_id=1, source_target_pairs={{0,8},{4,12},{8,0},{12,4},{1,9},{5,13},{9,1},{13,5},{2,10},{6,14},... | collective-permute-start | bytes 393224 | tf_op jit(solution)/shard_map/ppermute | solution.py:469
  86.0 8.3 %collective-permute-done.18.rest_2_ = bf16[64,1024]{1,0:T(8,128)(2,1)S(1)} collective-permute-done((bf16[64,1024]{1,0:T(8,128)(2,1)S(1)}, bf16[64,1024]{1,0:T(8,128)(2,1)S(1)}, u32[]{:S(2)}, u32[]{:S(2)}) %collective-permute-start.18) | collective-permute-done | bytes 131104 | tf_op jit(solution)/shard_map/ppermute | solution.py:469
  94.3 3.8 %units_kernel.1 = (f32[64,1024]{1,0:T(8,128)S(1)}, bf16[64,1024]{1,0:T(8,128)(2,1)S(1)}, bf16[64,1024]{1,0:T(8,128)(2,1)S(1)}, bf16[64,1024]{1,0:T(8,128)(2,1)S(...) custom-call(s32[9]{0:T(128)S(1)} %pad_add_fusion.place, ...), custom_call_target="tpu_custom_call" | custom-call | flops 1 | bytes 1 | tf_op jit(solution)/shard_map/units_kernel/pallas_call | solution.py:54
  99.7 3.0 %collective-permute-start.22 = (bf16[64,1024]{1,0:T(8,128)(2,1)S(1)}, bf16[64,1024]{1,0:T(8,128)(2,1)S(1)}, u32[]{:S(2)}, u32[]{:S(2)}) collective-permute-start(bf16[64,1024]{1,0:T(8,128)(2,1)S(1)} %get-tuple-element.138), channel_id=1, source_target_pairs={{0,8},{4,12},{8,0},{12,4},{1,9},{5,13},{9,1},{13,5},{2,10},{6,14},... | collective-permute-start | bytes 393224 | tf_op jit(solution)/shard_map/ppermute | solution.py:469
  109.7 3.1 %collective-permute-done.22.rest_2_ = bf16[64,1024]{1,0:T(8,128)(2,1)S(1)} collective-permute-done((bf16[64,1024]{1,0:T(8,128)(2,1)S(1)}, bf16[64,1024]{1,0:T(8,128)(2,1)S(1)}, u32[]{:S(2)}, u32[]{:S(2)}) %collective-permute-start.22) | collective-permute-done | bytes 131104 | tf_op jit(solution)/shard_map/ppermute | solution.py:469
  117.9 2.6 %collective-permute-done.26.rest_3_ = bf16[64,1024]{1,0:T(8,128)(2,1)S(1)} collective-permute-done((bf16[64,1024]{1,0:T(8,128)(2,1)S(1)}, bf16[64,1024]{1,0:T(8,128)(2,1)S(1)}, u32[]{:S(2)}, u32[]{:S(2)}) %collective-permute-start.26) | collective-permute-done | bytes 131104 | tf_op jit(solution)/shard_map/ppermute | solution.py:469
  120.5 6.0 %collective-permute-start.24 = (bf16[64,1024]{1,0:T(8,128)(2,1)S(1)}, bf16[64,1024]{1,0:T(8,128)(2,1)S(1)}, u32[]{:S(2)}, u32[]{:S(2)}) collective-permute-start(bf16[64,1024]{1,0:T(8,128)(2,1)S(1)} %get-tuple-element.140.rest_0_), channel_id=1, source_target_pairs={{0,4},{4,0},{8,12},{12,8},{1,5},{5,1},{9,13},{13,9},{2,6},{6,2},{1... | collective-permute-start | bytes 393224 | tf_op jit(solution)/shard_map/ppermute | solution.py:469
  128.4 2.7 %collective-permute-done.24.rest_1_ = bf16[64,1024]{1,0:T(8,128)(2,1)S(1)} collective-permute-done((bf16[64,1024]{1,0:T(8,128)(2,1)S(1)}, bf16[64,1024]{1,0:T(8,128)(2,1)S(1)}, u32[]{:S(2)}, u32[]{:S(2)}) %collective-permute-start.24) | collective-permute-done | bytes 131104 | tf_op jit(solution)/shard_map/ppermute | solution.py:469
  134.0 5.1 %collective-permute-done.27.rest_1_ = bf16[256,256]{1,0:T(8,128)(2,1)S(1)} collective-permute-done((bf16[256,256]{1,0:T(8,128)(2,1)S(1)}, bf16[256,256]{1,0:T(8,128)(2,1)S(1)}, u32[]{:S(2)}, u32[]{:S(2)}) %collective-permute-start.27) | collective-permute-done | bytes 131104 | tf_op jit(solution)/shard_map/ppermute | solution.py:469
  140.5 3.1 %attend_back_kernel.1 = (bf16[256,1024]{1,0:T(8,128)(2,1)S(1)}, f32[1,128]{1,0:T(1,128)S(1)}, f32[1,128]{1,0:T(1,128)S(1)}, bf16[256,1024]{1,0:T(8,128)(2,1)S(1)}) custom-call(s32[9]{0:T(128)S(1)} %pad_add_fusion.place, bf16[64,1024]{1,0:T(8,128)(2,1)S(1)} %get-tuple-element.140.rest_0_, bf16[64,1024]{1,0:T(8,128)(2,1)S(1)} %collective-permute-done.24.rest_1_, ...), custom_call_target="tpu_custom_call" | custom-call | flops 1 | bytes 1 | tf_op jit(solution)/shard_map/attend_back_kernel/pallas_call | solution.py:54
  165.4 13.9 %collective-permute-done.34.rest_6_.rest_2_ = bf16[544,256]{1,0:T(8,128)(2,1)S(1)} collective-permute-done((bf16[544,256]{1,0:T(8,128)(2,1)S(1)}, bf16[544,256]{1,0:T(8,128)(2,1)S(1)}, u32[]{:S(2)}, u32[]{:S(2)}) %collective-permute-start.34) | collective-permute-done | bytes 278560 | tf_op jit(solution)/shard_map/ppermute | solution.py:469
  179.3 3.2 %collective-permute-start.46 = (f32[1,2304]{1,0:T(1,128)S(1)}, f32[1,2304]{1,0:T(1,128)S(1)}, u32[]{:S(2)}, u32[]{:S(2)}) collective-permute-start(f32[1,2304]{1,0:T(1,128)S(1)} %add_add_fusion), channel_id=1, source_target_pairs={{0,12},{4,8},{8,4},{12,0},{1,13},{5,9},{9,5},{13,1},{2,14},{6,10},... | collective-permute-start | bytes 27656 | tf_op jit(solution)/shard_map/ppermute | solution.py:469
  182.5 4.2 %collective-permute-start.45 = (f32[1,2304]{1,0:T(1,128)S(1)}, f32[1,2304]{1,0:T(1,128)S(1)}, u32[]{:S(2)}, u32[]{:S(2)}) collective-permute-start(f32[1,2304]{1,0:T(1,128)S(1)} %add_add_fusion), channel_id=1, source_target_pairs={{0,8},{4,12},{8,0},{12,4},{1,9},{5,13},{9,1},{13,5},{2,10},{6,14},... | collective-permute-start | bytes 27656 | tf_op jit(solution)/shard_map/ppermute | solution.py:469
  188.3 2.9 %units_update_kernel.1 = (f32[256,384]{1,0:T(8,128)}, f32[256,384]{1,0:T(8,128)}, f32[256,384]{1,0:T(8,128)}, f32[256,384]{1,0:T(8,128)}, f32[256,384]{1,0:T(8,1...) custom-call(s32[9]{0:T(128)S(1)} %pad_add_fusion.place, ...), custom_call_target="tpu_custom_call" | custom-call | flops 1 | bytes 1 | tf_op jit(solution)/shard_map/units_update_kernel/pallas_call | solution.py:54
  (167 shorter events, 73.6 us)
Async XLA Ops:
  2.7 17.4 %collective-permute-start.5 = (bf16[128,1536]{1,0:T(8,128)(2,1)}, bf16[128,1536]{1,0:T(8,128)(2,1)S(1)}, u32[]{:S(2)}, u32[]{:S(2)}) collective-permute-start(bf16[128,1536]{1,0:T(8,128)(2,1)} %pack_kernel.1.rest_5_.rest_4_), channel_id=1, source_target_pairs={{0,18},{1,19},{2,16},{3,17},{16,2},{17,3},{18,0},{19,1},{4,22},{5,... | collective-permute-start | bytes 1179656 | tf_op jit(solution)/shard_map/ppermute | solution.py:472
  6.6 17.8 %collective-permute-start.4 = (bf16[128,1536]{1,0:T(8,128)(2,1)}, bf16[128,1536]{1,0:T(8,128)(2,1)S(1)}, u32[]{:S(2)}, u32[]{:S(2)}) collective-permute-start(bf16[128,1536]{1,0:T(8,128)(2,1)} %pack_kernel.1.rest_5_.rest_4_), channel_id=1, source_target_pairs={{0,16},{1,17},{2,18},{3,19},{16,0},{17,1},{18,2},{19,3},{4,20},{5,... | collective-permute-start | bytes 1179656 | tf_op jit(solution)/shard_map/ppermute | solution.py:472
  7.1 17.5 %collective-permute-start.3 = (bf16[128,1536]{1,0:T(8,128)(2,1)}, bf16[128,1536]{1,0:T(8,128)(2,1)S(1)}, u32[]{:S(2)}, u32[]{:S(2)}) collective-permute-start(bf16[128,1536]{1,0:T(8,128)(2,1)} %pack_kernel.1.rest_5_.rest_4_), channel_id=1, source_target_pairs={{0,2},{1,3},{2,0},{3,1},{16,18},{17,19},{18,16},{19,17},{4,6},{5,7... | collective-permute-start | bytes 1179656 | tf_op jit(solution)/shard_map/ppermute | solution.py:472
  15.5 18.3 %collective-permute-start = (bf16[800,256]{1,0:T(8,128)(2,1)S(1)}, bf16[800,256]{1,0:T(8,128)(2,1)S(1)}, u32[]{:S(2)}, u32[]{:S(2)}) collective-permute-start(bf16[800,256]{1,0:T(8,128)(2,1)S(1)} %get-tuple-element.112), channel_id=1, source_target_pairs={{0,4},{4,0},{8,12},{12,8},{1,5},{5,1},{9,13},{13,9},{2,6},{6,2},{1... | collective-permute-start | bytes 1228808 | tf_op jit(solution)/shard_map/ppermute | solution.py:469
  17.5 30.9 %collective-permute-start.1 = (bf16[800,256]{1,0:T(8,128)(2,1)S(1)}, bf16[800,256]{1,0:T(8,128)(2,1)S(1)}, u32[]{:S(2)}, u32[]{:S(2)}) collective-permute-start(bf16[800,256]{1,0:T(8,128)(2,1)S(1)} %get-tuple-element.113), channel_id=1, source_target_pairs={{0,8},{4,12},{8,0},{12,4},{1,9},{5,13},{9,1},{13,5},{2,10},{6,14},... | collective-permute-start | bytes 1228808 | tf_op jit(solution)/shard_map/ppermute | solution.py:469
  20.1 28.3 %collective-permute-start.2 = (bf16[800,256]{1,0:T(8,128)(2,1)S(1)}, bf16[800,256]{1,0:T(8,128)(2,1)S(1)}, u32[]{:S(2)}, u32[]{:S(2)}) collective-permute-start(bf16[800,256]{1,0:T(8,128)(2,1)S(1)} %get-tuple-element.114), channel_id=1, source_target_pairs={{0,12},{4,8},{8,4},{12,0},{1,13},{5,9},{9,5},{13,1},{2,14},{6,10},... | collective-permute-start | bytes 1228808 | tf_op jit(solution)/shard_map/ppermute | solution.py:469
  24.4 26.6 %collective-permute-start.6 = (bf16[128,1536]{1,0:T(8,128)(2,1)S(1)}, bf16[128,1536]{1,0:T(8,128)(2,1)S(1)}, u32[]{:S(2)}, u32[]{:S(2)}) collective-permute-start(bf16[128,1536]{1,0:T(8,128)(2,1)S(1)} %copy-done), channel_id=1, source_target_pairs={{0,1},{1,0},{2,3},{3,2},{16,17},{17,16},{18,19},{19,18},{4,5},{5,4... | collective-permute-start | bytes 1179656 | tf_op jit(solution)/shard_map/ppermute | solution.py:472
  24.7 26.8 %collective-permute-start.9 = (bf16[128,1536]{1,0:T(8,128)(2,1)S(1)}, bf16[128,1536]{1,0:T(8,128)(2,1)S(1)}, u32[]{:S(2)}, u32[]{:S(2)}) collective-permute-start(bf16[128,1536]{1,0:T(8,128)(2,1)S(1)} %collective-permute-done.5.rest_7_), channel_id=1, source_target_pairs={{0,1},{1,0},{2,3},{3,2},{16,17},{17,16},{18,19},{19,18},{4,5},{5,4... | collective-permute-start | bytes 1179656 | tf_op jit(solution)/shard_map/ppermute | solution.py:472
  33.8 18.8 %collective-permute-start.8 = (bf16[128,1536]{1,0:T(8,128)(2,1)S(1)}, bf16[128,1536]{1,0:T(8,128)(2,1)S(1)}, u32[]{:S(2)}, u32[]{:S(2)}) collective-permute-start(bf16[128,1536]{1,0:T(8,128)(2,1)S(1)} %collective-permute-done.4.rest_6_), channel_id=1, source_target_pairs={{0,1},{1,0},{2,3},{3,2},{16,17},{17,16},{18,19},{19,18},{4,5},{5,4... | collective-permute-start | bytes 1179656 | tf_op jit(solution)/shard_map/ppermute | solution.py:472
  48.4 26.6 %collective-permute-start.12 = (bf16[3,96,1024]{2,1,0:T(8,128)(2,1)S(1)}, bf16[3,96,1024]{2,1,0:T(8,128)(2,1)S(1)}, u32[]{:S(2)}, u32[]{:S(2)}) collective-permute-start(bf16[3,96,1024]{2,1,0:T(8,128)(2,1)S(1)} %join_kernel.1), channel_id=1, source_target_pairs={{0,18},{1,19},{2,16},{3,17},{16,2},{17,3},{18,0},{19,1},{4,22},{5,... | collective-permute-start | bytes 1769480 | tf_op jit(solution)/shard_map/ppermute | solution.py:472
  51.0 26.8 %collective-permute-start.11 = (bf16[3,96,1024]{2,1,0:T(8,128)(2,1)S(1)}, bf16[3,96,1024]{2,1,0:T(8,128)(2,1)S(1)}, u32[]{:S(2)}, u32[]{:S(2)}) collective-permute-start(bf16[3,96,1024]{2,1,0:T(8,128)(2,1)S(1)} %join_kernel.1), channel_id=1, source_target_pairs={{0,16},{1,17},{2,18},{3,19},{16,0},{17,1},{18,2},{19,3},{4,20},{5,... | collective-permute-start | bytes 1769480 | tf_op jit(solution)/shard_map/ppermute | solution.py:472
  51.5 26.4 %collective-permute-start.10 = (bf16[3,96,1024]{2,1,0:T(8,128)(2,1)S(1)}, bf16[3,96,1024]{2,1,0:T(8,128)(2,1)S(1)}, u32[]{:S(2)}, u32[]{:S(2)}) collective-permute-start(bf16[3,96,1024]{2,1,0:T(8,128)(2,1)S(1)} %join_kernel.1), channel_id=1, source_target_pairs={{0,2},{1,3},{2,0},{3,1},{16,18},{17,19},{18,16},{19,17},{4,6},{5,7... | collective-permute-start | bytes 1769480 | tf_op jit(solution)/shard_map/ppermute | solution.py:472
  78.1 16.2 %collective-permute-start.16 = (bf16[3,384,1024]{2,1,0:T(8,128)(2,1)S(1)}, bf16[3,384,1024]{2,1,0:T(8,128)(2,1)S(1)}, u32[]{:S(2)}, u32[]{:S(2)}) collective-permute-start(bf16[3,384,1024]{2,1,0:T(8,128)(2,1)S(1)} %pad_maximum_fusion.wz_ref), channel_id=1, source_target_pairs={{0,1},{1,0},{2,3},{3,2},{16,17},{17,16},{18,19},{19,18},{4,5},{5,4... | collective-permute-start | bytes 7077896 | tf_op jit(solution)/shard_map/ppermute | solution.py:472
  80.7 13.6 %collective-permute-start.18 = (bf16[64,1024]{1,0:T(8,128)(2,1)S(1)}, bf16[64,1024]{1,0:T(8,128)(2,1)S(1)}, u32[]{:S(2)}, u32[]{:S(2)}) collective-permute-start(bf16[64,1024]{1,0:T(8,128)(2,1)S(1)} %get-tuple-element.126.rest_0_), channel_id=1, source_target_pairs={{0,8},{4,12},{8,0},{12,4},{1,9},{5,13},{9,1},{13,5},{2,10},{6,14},... | collective-permute-start | bytes 393224 | tf_op jit(solution)/shard_map/ppermute | solution.py:469
  99.7 13.0 %collective-permute-start.22 = (bf16[64,1024]{1,0:T(8,128)(2,1)S(1)}, bf16[64,1024]{1,0:T(8,128)(2,1)S(1)}, u32[]{:S(2)}, u32[]{:S(2)}) collective-permute-start(bf16[64,1024]{1,0:T(8,128)(2,1)S(1)} %get-tuple-element.138), channel_id=1, source_target_pairs={{0,8},{4,12},{8,0},{12,4},{1,9},{5,13},{9,1},{13,5},{2,10},{6,14},... | collective-permute-start | bytes 393224 | tf_op jit(solution)/shard_map/ppermute | solution.py:469
  105.6 41.0 %collective-permute-start.32 = (bf16[3,96,1024]{2,1,0:T(8,128)(2,1)S(1)}, bf16[3,96,1024]{2,1,0:T(8,128)(2,1)S(1)}, u32[]{:S(2)}, u32[]{:S(2)}) collective-permute-start(bf16[3,96,1024]{2,1,0:T(8,128)(2,1)S(1)} %get-tuple-element.201), channel_id=1, source_target_pairs={{0,18},{1,19},{2,16},{3,17},{16,2},{17,3},{18,0},{19,1},{4,22},{5,... | collective-permute-start | bytes 1769480 | tf_op jit(solution)/shard_map/ppermute | solution.py:472
  107.3 39.3 %collective-permute-start.31 = (bf16[3,96,1024]{2,1,0:T(8,128)(2,1)S(1)}, bf16[3,96,1024]{2,1,0:T(8,128)(2,1)S(1)}, u32[]{:S(2)}, u32[]{:S(2)}) collective-permute-start(bf16[3,96,1024]{2,1,0:T(8,128)(2,1)S(1)} %get-tuple-element.202), channel_id=1, source_target_pairs={{0,16},{1,17},{2,18},{3,19},{16,0},{17,1},{18,2},{19,3},{4,20},{5,... | collective-permute-start | bytes 1769480 | tf_op jit(solution)/shard_map/ppermute | solution.py:472
  108.6 38.0 %collective-permute-start.30 = (bf16[3,96,1024]{2,1,0:T(8,128)(2,1)S(1)}, bf16[3,96,1024]{2,1,0:T(8,128)(2,1)S(1)}, u32[]{:S(2)}, u32[]{:S(2)}) collective-permute-start(bf16[3,96,1024]{2,1,0:T(8,128)(2,1)S(1)} %get-tuple-element.203), channel_id=1, source_target_pairs={{0,2},{1,3},{2,0},{3,1},{16,18},{17,19},{18,16},{19,17},{4,6},{5,7... | collective-permute-start | bytes 1769480 | tf_op jit(solution)/shard_map/ppermute | solution.py:472
  116.0 12.4 %collective-permute-start.25 = (bf16[64,1024]{1,0:T(8,128)(2,1)S(1)}, bf16[64,1024]{1,0:T(8,128)(2,1)S(1)}, u32[]{:S(2)}, u32[]{:S(2)}) collective-permute-start(bf16[64,1024]{1,0:T(8,128)(2,1)S(1)} %get-tuple-element.140.rest_0_), channel_id=1, source_target_pairs={{0,8},{4,12},{8,0},{12,4},{1,9},{5,13},{9,1},{13,5},{2,10},{6,14},... | collective-permute-start | bytes 393224 | tf_op jit(solution)/shard_map/ppermute | solution.py:469
  159.3 20.0 %collective-permute-start.34 = (bf16[544,256]{1,0:T(8,128)(2,1)S(1)}, bf16[544,256]{1,0:T(8,128)(2,1)S(1)}, u32[]{:S(2)}, u32[]{:S(2)}) collective-permute-start(bf16[544,256]{1,0:T(8,128)(2,1)S(1)} %get-tuple-element.156), channel_id=1, source_target_pairs={{0,8},{4,12},{8,0},{12,4},{1,9},{5,13},{9,1},{13,5},{2,10},{6,14},... | collective-permute-start | bytes 835592 | tf_op jit(solution)/shard_map/ppermute | solution.py:469
  160.7 21.8 %collective-permute-start.35 = (bf16[544,256]{1,0:T(8,128)(2,1)S(1)}, bf16[544,256]{1,0:T(8,128)(2,1)S(1)}, u32[]{:S(2)}, u32[]{:S(2)}) collective-permute-start(bf16[544,256]{1,0:T(8,128)(2,1)S(1)} %get-tuple-element.157), channel_id=1, source_target_pairs={{0,12},{4,8},{8,4},{12,0},{1,13},{5,9},{9,5},{13,1},{2,14},{6,10},... | collective-permute-start | bytes 835592 | tf_op jit(solution)/shard_map/ppermute | solution.py:469
  161.9 30.0 %collective-permute-start.47 = (bf16[128,1536]{1,0:T(8,128)(2,1)S(1)}, bf16[128,1536]{1,0:T(8,128)(2,1)S(1)}, u32[]{:S(2)}, u32[]{:S(2)}) collective-permute-start(bf16[128,1536]{1,0:T(8,128)(2,1)S(1)} %get-tuple-element.171), channel_id=1, source_target_pairs={{0,2},{1,3},{2,0},{3,1},{16,18},{17,19},{18,16},{19,17},{4,6},{5,7... | collective-permute-start | bytes 1179656 | tf_op jit(solution)/shard_map/ppermute | solution.py:472
  163.4 28.5 %collective-permute-start.48 = (bf16[128,1536]{1,0:T(8,128)(2,1)S(1)}, bf16[128,1536]{1,0:T(8,128)(2,1)S(1)}, u32[]{:S(2)}, u32[]{:S(2)}) collective-permute-start(bf16[128,1536]{1,0:T(8,128)(2,1)S(1)} %get-tuple-element.172), channel_id=1, source_target_pairs={{0,16},{1,17},{2,18},{3,19},{16,0},{17,1},{18,2},{19,3},{4,20},{5,... | collective-permute-start | bytes 1179656 | tf_op jit(solution)/shard_map/ppermute | solution.py:472
  164.1 27.8 %collective-permute-start.49 = (bf16[128,1536]{1,0:T(8,128)(2,1)S(1)}, bf16[128,1536]{1,0:T(8,128)(2,1)S(1)}, u32[]{:S(2)}, u32[]{:S(2)}) collective-permute-start(bf16[128,1536]{1,0:T(8,128)(2,1)S(1)} %get-tuple-element.173), channel_id=1, source_target_pairs={{0,18},{1,19},{2,16},{3,17},{16,2},{17,3},{18,0},{19,1},{4,22},{5,... | collective-permute-start | bytes 1179656 | tf_op jit(solution)/shard_map/ppermute | solution.py:472
  (56 other events, 591.5 us)

commit v3 on v2

--- a/solution.py
+++ b/solution.py
@@ -23,6 +23,9 @@
 MASK_VALUE = -1e30
 LANE = 128
 BLOCKS = D // LANE
+ATTEND_LIMIT = 40
+UPDATE_LIMIT = 16
+GAIN_ROWS = 16
 PLANE = ("dp", "col")
 F32 = jnp.float32
 BF16 = jnp.bfloat16
@@ -75,8 +78,8 @@
 def adamw(weight, first, second, grad, rate, decay):
     first_new = BETA_FIRST * first + (1.0 - BETA_FIRST) * grad
     second_new = BETA_SECOND * second + (1.0 - BETA_SECOND) * grad * grad
-    first_hat = first_new / (1.0 - BETA_FIRST**STEP)
-    second_hat = second_new / (1.0 - BETA_SECOND**STEP)
+    first_hat = first_new * (1.0 / (1.0 - BETA_FIRST**STEP))
+    second_hat = second_new * (1.0 / (1.0 - BETA_SECOND**STEP))
     weight_new = weight - rate * (
         first_hat / (jnp.sqrt(second_hat) + ADAM_EPSILON) + decay * weight
     )
@@ -109,7 +112,7 @@
              cot_ref, w_ref) = rest[:n], rest[n:n + blocks], rest[n + blocks:]
     height = D // blocks
     for i, w in enumerate(ws):
-        w_ref[i * height:(i + 1) * height, :] = w[...]
+        w_ref[i * height:(i + 1) * height, :] = w[0]
     z = place[0]
     part = D // n
     for k in range(n):
@@ -234,21 +237,31 @@
         out[...] = total_ref[:, k * width:(k + 1) * width].astype(out.dtype)
 
 
-def pack_units_kernel(n, place, *rest):
-    sources, (x_ref, cot_in_ref), outs, (g, u, d, scratch, sems) = rest[:3], rest[3:5], rest[6:6 + n], rest[6 + n:]
-    copies = [pltpu.make_async_copy(src, dst, sems.at[i]) for i, (src, dst) in enumerate(zip(sources, (g, u, d)))]
+def pack_kernel(n, *rest):
+    z = lax.axis_index("row")
+    sources, out_ref, outs, buffers = rest[:9], rest[9], rest[10:10 + n], rest[10 + n:]
+    (*held, scratch, sems) = buffers
+    copies = [pltpu.make_async_copy(src, dst, sems.at[i]) for i, (src, dst) in enumerate(zip(sources, held))]
     for copy in copies:
         copy.start()
-    length = 2 * x_ref.shape[0]
+    at = 0
+    for copy, ref in zip(copies[:4], held[:4]):
+        copy.wait()
+        out_ref[0, :, at:at + ref.shape[1]] = ref[...].astype(BF16)
+        at += ref.shape[1]
+    x, cot = held[4:6]
+    length = 2 * x.shape[0]
     size = (outs[0].shape[0] - length) // 3
+    copies[4].wait()
+    copies[5].wait()
     for out in outs:
-        out[:length // 2, :] = x_ref[...]
-        out[length // 2:length, :] = cot_in_ref[...]
-    for i, (copy, ref) in enumerate(zip(copies, (g, u, d))):
+        out[:length // 2, :] = x[...]
+        out[length // 2:length, :] = cot[...]
+    for i, (copy, ref) in enumerate(zip(copies[6:], held[6:])):
         copy.wait()
         scratch[...] = ref[...].T.astype(BF16)
         for k, out in enumerate(outs):
-            out[length + i * size:length + (i + 1) * size, :] = scratch[rows_of(place[0] ^ k, size), :]
+            out[length + i * size:length + (i + 1) * size, :] = scratch[rows_of(z ^ k, size), :]
 
 
 def join_kernel(n, *rest):
@@ -260,13 +273,59 @@
             out_ref[i, :, k * width:(k + 1) * width] = piece[length + i * size:length + (i + 1) * size, :]
 
 
+def pair_sum_kernel(own_ref, *rest):
+    others, (keep_ref, keep_x, keep_y, send_x, send_y) = rest[:-5], rest[-5:]
+    lead, size, cols = keep_ref.shape
+    half = cols // 2
+
+    def block(i, at):
+        rows = slice(i * size, (i + 1) * size)
+        other = others[0][:, rows, at] if len(others) == 1 else others[i][:, :, at]
+        return own_ref[:, rows, at].astype(F32) + other.astype(F32)
+
+    first, second = slice(0, half), slice(half, cols)
+    send_x[:lead] = block(1, first).astype(BF16)
+    send_x[lead:] = block(3, first).astype(BF16)
+    send_y[:lead] = block(2, second).astype(BF16)
+    send_y[lead:] = block(3, second).astype(BF16)
+    keep_ref[...] = block(0, slice(0, cols))
+    keep_x[...] = block(1, second)
+    keep_y[...] = block(2, first)
+
+
+def block_sum_kernel(own_ref, other_ref, *outs):
+    size = outs[0].shape[1]
+    for i, out in enumerate(outs):
+        rows = slice(i * size, (i + 1) * size)
+        out[...] = (own_ref[:, rows, :].astype(F32) + other_ref[:, rows, :].astype(F32)).astype(out.dtype)
+
+
+def relay_sum_kernel(keep_x, keep_y, got_x, got_y, send_x, send_y):
+    lead = keep_x.shape[0]
+    send_y[...] = (keep_y[...] + got_x[lead:].astype(F32)).astype(BF16)
+    send_x[...] = (keep_x[...] + got_y[lead:].astype(F32)).astype(BF16)
+
+
+def plane_total(terms, i):
+    if len(terms) != 5:
+        total = terms[0][i].astype(F32)
+        for term in terms[1:]:
+            total = total + term[i].astype(F32)
+        return total
+    keep, got_x, got_y, last_x, last_y = terms
+    half = keep.shape[2] // 2
+    first = keep[i, :, :half] + (got_x[i].astype(F32) + last_y[i].astype(F32))
+    second = keep[i, :, half:] + (got_y[i].astype(F32) + last_x[i].astype(F32))
+    return jnp.concatenate([first, second], axis=1)
+
+
 def units_update_kernel(n, place, *rest):
     pieces, states, outs, scratch = rest[:n], rest[n:n + 9], rest[n + 9:n + 18], rest[n + 18]
     size = scratch.shape[0] // n
-    length = pieces[0].shape[0] - 3 * size
+    base = pieces[0].shape[0] - 3 * size
     for i in range(3):
         for k in range(n):
-            scratch[rows_of(place[0] ^ k, size), :] = pieces[k][length + i * size:length + (i + 1) * size, :].astype(F32)
+            scratch[rows_of(place[0] ^ k, size), :] = pieces[k][base + i * size:base + (i + 1) * size, :].astype(F32)
         w, m, v = (ref[...] for ref in states[3 * i:3 * i + 3])
         for ref, value in zip(outs[3 * i:3 * i + 3], adamw(w, m, v, scratch[...].T, MATRIX_RATE, MATRIX_DECAY)):
             ref[...] = value
@@ -274,9 +333,7 @@
 
 def update_kernel(n, count, *rest):
     terms, states, outs = rest[:n], rest[n:n + 3 * count], rest[n + 3 * count:]
-    total = terms[0][...].astype(F32)
-    for term in terms[1:]:
-        total = total + term[...].astype(F32)
+    total = plane_total(terms, 0)
     at = 0
     for i in range(count):
         w, m, v = (ref[...] for ref in states[3 * i:3 * i + 3])
@@ -284,18 +341,6 @@
         at += w.shape[1]
         for ref, value in zip(outs[3 * i:3 * i + 3], adamw(w, m, v, grad, MATRIX_RATE, MATRIX_DECAY)):
             ref[...] = value
-
-
-def pack_kernel(*rest):
-    sources, out_ref, (q, k, v, o, sems) = rest[:4], rest[4], rest[5:]
-    copies = [pltpu.make_async_copy(src, dst, sems.at[i]) for i, (src, dst) in enumerate(zip(sources, (q, k, v, o)))]
-    for copy in copies:
-        copy.start()
-    at = 0
-    for copy, ref in zip(copies, (q, k, v, o)):
-        copy.wait()
-        out_ref[:, at:at + ref.shape[1]] = ref[...].astype(BF16)
-        at += ref.shape[1]
 
 
 def mid_back_kernel(n, place, resid_ref, cot_ref, gains_ref, *rest):
@@ -385,21 +430,13 @@
     for left, right, cols in ((norm_ref, dqkv_ref, slice(0, here)), (dbr_ref, ctx_ref, slice(here, None))):
         other = mm_tn(left[:, half:], right[...]).astype(BF16)
         for i, out in enumerate(outs):
-            out[:, cols] = other[i * step:(i + 1) * step, :]
-    gz_ref[:, :here] = mm_tn(norm_ref[:, :half], dqkv_ref[...])
-    gz_ref[:, here:] = mm_tn(dbr_ref[:, :half], ctx_ref[...])
-
-
-def pair_sum_kernel(n, own_ref, *rest):
-    others, outs = rest[:n], rest[n:]
-    step = own_ref.shape[0] // n
-    for i, (other, out) in enumerate(zip(others, outs)):
-        out[...] = (own_ref[i * step:(i + 1) * step, :] + other[...].astype(F32)).astype(out.dtype)
+            out[0, :, cols] = other[i * step:(i + 1) * step, :]
+        gz_ref[0, :, cols] = mm_tn(left[:, :half], right[...])
 
 
 def input_grad_kernel(n, count, place, dqkv_ref, w_ref, x_ref, gains_ref, *rest):
-    units, rest = rest[:count], rest[count + 1:]
-    outs, gain_ref, dn_ref, term_ref = rest[:n], rest[n], rest[n + 1], rest[n + 2]
+    units, rest = rest[:count], rest[count:]
+    (dg2_ref, dgq_ref, dgk_ref), outs, (gain_ref, dn_ref, term_ref) = rest[:3], rest[3:n + 3], rest[n + 3:]
     z = place[0]
     dn_ref[...] = mm_nt(dqkv_ref[...], w_ref[:, :dqkv_ref.shape[1]])
     x = x_ref[...].astype(F32)
@@ -421,37 +458,45 @@
         term_ref[:, at] = r1 * gains_ref[:, lanes(b)] * dn_ref[:, j * LANE:(j + 1) * LANE] - xb * back
     width = outs[0].shape[1]
     length = x.shape[0]
+    gain_ref[:, D:2 * D] = dg2_ref[...]
+    gain_ref[:, 2 * D:2 * D + HD] = dgq_ref[...]
+    gain_ref[:, 2 * D + HD:2 * D + 2 * HD] = dgk_ref[...]
+    gain_ref[:, 2 * D + 2 * HD:] = jnp.zeros((1, GAIN_ROWS * width - 2 * D - 2 * HD), F32)
+    gain_rows = jnp.concatenate([gain_ref[:, i * width:(i + 1) * width] for i in range(GAIN_ROWS)], axis=0)
     for k, out in enumerate(outs):
+        out[length:length + GAIN_ROWS, :] = gain_rows.astype(out.dtype)
         out[:length, :] = term_ref[:, k * width:(k + 1) * width].astype(out.dtype)
     if count:
-        size = units[0].shape[1]
+        base, size = length + GAIN_ROWS, units[0].shape[1]
         for i in range(3):
-            total = units[0][i]
-            for unit in units[1:]:
-                total = total + unit[i].astype(F32)
+            total = plane_total(units, i)
             for k, out in enumerate(outs):
-                out[length + i * size:length + (i + 1) * size, :] = total[:, k * width:(k + 1) * width].astype(out.dtype)
-
-
-def act_grad_kernel(n, place, *rest):
-    pieces, terms, out_ref = rest[:n], rest[n:2 * n], rest[2 * n]
+                out[base + i * size:base + (i + 1) * size, :] = total[:, k * width:(k + 1) * width].astype(out.dtype)
+
+
+def gain_kernel(base, *rest):
+    terms, out_ref = rest[:-1], rest[-1]
+    total = terms[0][base:base + GAIN_ROWS, :].astype(F32)
+    for term in terms[1:]:
+        total = total + term[base:base + GAIN_ROWS, :].astype(F32)
+    out_ref[...] = total
+
+
+def act_kernel(n, place, *rest):
+    pieces, terms, downs, (out_ref, grad_ref) = rest[:n], rest[n:2 * n], rest[2 * n:3 * n], rest[3 * n:]
     z = place[0]
-    width = out_ref.shape[1]
+    length, width = out_ref.shape
     size = pieces[0].shape[0]
+    total = downs[0][...].astype(F32)
+    for term in downs[1:]:
+        total = total + term[...].astype(F32)
+    out_ref[...] = total.astype(BF16)
     for k in range(n):
         at = rows_of(z ^ k, size)
         total = terms[0][at, :].astype(F32)
         for term in terms[1:]:
             total = total + term[at, :].astype(F32)
-        out_ref[at, :] = pieces[k][:, k * width:(k + 1) * width].astype(F32) + total
-
-
-def act_out_kernel(*rest):
-    terms, out_ref = rest[:-1], rest[-1]
-    total = terms[0][...].astype(F32)
-    for term in terms[1:]:
-        total = total + term[...].astype(F32)
-    out_ref[...] = total.astype(BF16)
+        grad_ref[at, :] = pieces[k][:, k * width:(k + 1) * width].astype(F32) + total
 
 
 def body(sizes, act_in, act_cot, segments, positions, gains, gains_first, gains_second,
@@ -490,29 +535,26 @@
     def gather_plane(value, axis=0):
         return far_plane(near_plane(value, axis), axis)
 
-    def pair_plane(same, other, axis=0):
+    def scatter_plane(same, others):
         if not paired:
-            whole = jnp.concatenate([same.astype(F32), other.astype(F32)], axis=axis)
-            return [lax.psum_scatter(whole, PLANE, scatter_dimension=axis, tiled=True)]
-        total = same.astype(F32) + over_plane(other, 1).astype(F32)
-        parts = jnp.split(total, 4, axis=axis)
-        return parts[:1] + [part.astype(BF16) for part in parts[1:]]
-
-    def rest_plane(parts):
-        return list(parts[:1]) + [over_plane(part, k) for part, k in zip(parts[1:], (2, 4, 6))]
-
-    def add(terms):
-        out = terms[0].astype(F32)
-        for term in terms[1:]:
-            out = out + term.astype(F32)
-        return out
-
-    def sum_all(value):
+            whole = jnp.concatenate([part.astype(F32) for part in (same, *others)], axis=1)
+            return [lax.psum_scatter(whole, PLANE, scatter_dimension=1, tiled=True)], (), ()
+        lead, size, cols = same.shape
+        size, half = size // 4, cols // 2
+        keep, keep_x, keep_y, send_x, send_y = call(
+            pair_sum_kernel,
+            [shape((lead, size, cols), F32)] + [shape((lead, size, half), F32)] * 2
+            + [shape((2 * lead, size, half), BF16)] * 2,
+            same, *[over_plane(part, 1) for part in others])
+        got_x, got_y = over_plane(send_x, 2), over_plane(send_y, 4)
+        last_x, last_y = call(relay_sum_kernel, [shape((lead, size, half), BF16)] * 2, keep_x, keep_y, got_x, got_y)
+        return [keep, got_x, got_y, over_plane(last_x, 2), over_plane(last_y, 4)], (send_x, send_y), (last_x, last_y)
+
+    def sum_plane(value, first):
         if not paired:
-            return lax.psum(value, ("dp", "row", "col"))
-        value = value + over_plane(value, 1)
-        value = value + over_plane(value, 2) + over_plane(value, 4) + over_plane(value, 6)
-        return value + over_row(value, 1) + over_row(value, 2) + over_row(value, 3)
+            return lax.psum(value, PLANE)
+        value = after(value + over_plane(value, 1), first)
+        return value + over_plane(value, 2) + over_plane(value, 4) + over_plane(value, 6)
 
     order = jnp.array([0, 2, 4, 6, 1, 3, 5, 7], jnp.int32) ^ p if paired else jnp.arange(BLOCKS, dtype=jnp.int32)
     place = jnp.concatenate([z[None], order])
@@ -523,34 +565,32 @@
     rows = query_weight.shape[0]
     units = gate_weight.shape[1]
     gain = gains[None, :]
-    if rows % 16 == 0:
-        (w_proj,) = call(
-            pack_kernel, [shape((rows, 2 * qw + 2 * kw), BF16)],
-            query_weight, key_weight, value_weight, output_weight, hbm=4, limit=56,
-            scratch=[pltpu.VMEM((rows, w), F32) for w in (qw, kw, kw, qw)] + [pltpu.SemaphoreType.DMA((4,))])
-    else:
-        w_proj = jnp.concatenate([query_weight, key_weight, value_weight, output_weight], axis=1).astype(BF16)
-    if paired:
-        near = [w_proj] + [over_plane(w_proj, k) for k in (2, 4, 6)]
-    else:
-        near = list(jnp.split(lax.all_gather(w_proj, PLANE, axis=0, tiled=True), 2, axis=0))
+    cols = 2 * qw + 2 * kw
     share = units // n_row
     small = share % 16 != 0
     if small:
+        w_here = jnp.concatenate([query_weight, key_weight, value_weight, output_weight], axis=1).astype(BF16)[None]
         joined = jnp.stack([gate_weight, up_weight, down_weight]).astype(BF16).transpose(0, 2, 1)
         parts = [lax.dynamic_slice_in_dim(joined, (z ^ k) * share, share, 1) for k in range(n_row)]
         units_mine = jnp.concatenate(scatter_row(parts), axis=2)
         xs = gather_row(jnp.concatenate([act_in, act_cot], axis=0))
     else:
-        xs = call(
-            functools.partial(pack_units_kernel, n_row), [shape((2 * length + 3 * share, width), BF16)] * n_row,
-            place, gate_weight, up_weight, down_weight, act_in, act_cot, w_proj, scalars=1, hbm=3, ties=1, limit=48,
-            scratch=[pltpu.VMEM((width, units), F32)] * 3
-            + [pltpu.VMEM((units, width), BF16), pltpu.SemaphoreType.DMA((3,))])
+        w_here, *xs = call(
+            functools.partial(pack_kernel, n_row),
+            [shape((1, rows, cols), BF16)] + [shape((2 * length + 3 * share, width), BF16)] * n_row,
+            query_weight, key_weight, value_weight, output_weight, act_in, act_cot,
+            gate_weight, up_weight, down_weight, hbm=9, limit=59,
+            scratch=[pltpu.VMEM((rows, w), F32) for w in (qw, kw, kw, qw)] + [pltpu.VMEM((length, width), BF16)] * 2
+            + [pltpu.VMEM((width, units), F32)] * 3 + [pltpu.VMEM((units, width), BF16), pltpu.SemaphoreType.DMA((9,))])
         xs = scatter_row(xs)
+    if paired:
+        near = [w_here] + [over_plane(w_here, k) for k in (2, 4, 6)]
+    else:
+        near = list(jnp.split(lax.all_gather(w_here, PLANE, axis=1, tiled=True), 2, axis=1))
     cosine, sine, mask = call(
         tables_kernel, [shape((length, HD), F32)] * 2 + [shape((length, length), F32)],
         positions[None, :], segments[None, :])
+    near[-1] = after(near[-1], mask)
     w_parts = near + [over_plane(part, 1) for part in near] if paired else near
 
     heads = qw // HD
@@ -560,7 +600,7 @@
          shape((length, kw), BF16), shape((length, kw), BF16), shape((length, qw + kw), F32),
          shape((length, D), BF16), shape((length, D), BF16), shape((length, D), BF16),
          shape((D, 2 * qw + 2 * kw), BF16)],
-        place, *xs, *w_parts, gain, cosine, sine, mask, scalars=1)
+        place, *xs, *w_parts, gain, cosine, sine, mask, scalars=1, limit=ATTEND_LIMIT)
     if not small:
         (units_mine,) = call(functools.partial(join_kernel, n_row), [shape((3, share, D), BF16)],
                              *xs)
@@ -589,56 +629,65 @@
     unit_grad_z, unit_grad_o = call(
         units_grad_kernel, [shape(units_z.shape, BF16)] * 2,
         cot_row, mid_all, hidden, d_units)
-    unit_pair = pair_plane(unit_grad_z, unit_grad_o, axis=1)
-    resid = after(resid, *unit_pair)
-    unit_terms = rest_plane(unit_pair)
+    if paired:
+        unit_pair = call(
+            block_sum_kernel, [shape((3, share, D), F32 if i == 0 else BF16) for i in range(4)],
+            unit_grad_z, over_plane(unit_grad_o, 1))
+        resid = after(resid, unit_pair[1])
+    else:
+        unit_pair = scatter_plane(unit_grad_z, [unit_grad_o])[0]
     branch_grad, mid_gain_grad = call(
         functools.partial(mid_back_kernel, n_row),
         [shape((size, D), BF16), shape((1, D), F32)],
         place, resid, cot_row, gain, *dmid_terms,
         scalars=1, scratch=[pltpu.VMEM((size, D), F32)])
 
+    unit_terms = unit_pair[:1]
+    if paired:
+        unit_terms = [unit_pair[0]] + [over_plane(after(unit_pair[i], branch_grad), k) for i, k in ((1, 2), (2, 4))]
     pieces = gather_row(branch_grad)
+    if paired:
+        unit_terms.append(over_plane(after(unit_pair[3], *pieces), 6))
     down_terms = call(
         functools.partial(down_kernel, n_row),
         [shape((length, width), F32 if k == 0 else BF16) for k in range(n_row)],
         place, hidden, units_z, units_o, resid,
         scalars=1, scratch=[pltpu.VMEM((length, D), F32)])
     down_terms = scatter_row([after(term, *pieces) for term in down_terms])
-    (act_out,) = call(act_out_kernel, [shape((length, width), BF16)], *down_terms)
     dqkv, query_gain_grad, key_gain_grad, dbranch = call(
         functools.partial(attend_back_kernel, n_row),
         [shape((length, qw + 2 * kw), BF16), shape((1, HD), F32), shape((1, HD), F32), shape((length, D), BF16)],
         place, *pieces, w_proj, probs, queries, keys, values, raw, gain, cosine, sine, scalars=1)
+    proj_grad, *proj_others = call(
+        weight_grad_kernel, [shape((1, D // 2, cols), F32)] + [shape((1, D // 8, cols), BF16)] * 4,
+        normed, after(dqkv, *down_terms, *unit_terms[1:]), dbranch, context)
+    proj_terms, _, sent = scatter_plane(proj_grad, proj_others)
     merged = [] if small else unit_terms
-    count = length if small else length + 3 * share
-    *in_terms, in_gain_grad = call(
+    *in_terms, _ = call(
         functools.partial(input_grad_kernel, n_row, len(merged)),
-        [shape((count, width), F32 if k == 0 else BF16) for k in range(n_row)] + [shape((1, D), F32)],
-        place, dqkv, w_proj, x_row, gain, *merged, act_out,
+        [shape((length + GAIN_ROWS + 3 * share * bool(merged), width), F32 if k == 0 else BF16)
+         for k in range(n_row)]
+        + [shape((1, GAIN_ROWS * width), F32)],
+        place, dqkv, w_proj, x_row, gain, *merged, mid_gain_grad, query_gain_grad, key_gain_grad,
         scalars=1, scratch=[pltpu.VMEM((length, D), F32)] * 2)
-    cols = 2 * qw + 2 * kw
-    grad_own, *grad_others = call(
-        weight_grad_kernel,
-        [shape((D // 2, cols), F32)] + [shape((D // 2 // 4, cols), BF16)] * 4,
-        normed, dqkv, dbranch, after(context, in_terms[0]))
-    if paired:
-        grad_others = [over_plane(part, 1) for part in grad_others]
-        proj_pair = call(functools.partial(pair_sum_kernel, 4),
-                         [shape((rows, cols), F32 if i == 0 else BF16) for i in range(4)], grad_own, *grad_others)
-        proj_terms = rest_plane(proj_pair)
-    else:
-        proj_pair = proj_terms = pair_plane(grad_own, jnp.concatenate(grad_others, axis=0))
     in_terms = scatter_row(in_terms)
-    gains_grad = jnp.concatenate([in_gain_grad, mid_gain_grad, query_gain_grad, key_gain_grad], axis=1)
-    gains_grad = sum_all(after(gains_grad, *proj_pair))[0]
-
-    (act_grad,) = call(functools.partial(act_grad_kernel, n_row), [shape((length, width), F32)],
-                       place, *pieces, *in_terms, scalars=1)
+    def update(terms, *states):
+        return call(functools.partial(update_kernel, len(terms), len(states) // 3),
+                    [shape(state.shape, F32) for state in states], *terms, *states, limit=UPDATE_LIMIT)
+
+    new_proj = update(proj_terms, query_weight, query_first, query_second, key_weight, key_first, key_second,
+                      value_weight, value_first, value_second, output_weight, output_first, output_second)
+
+    (gains_grad,) = call(functools.partial(gain_kernel, length), [shape((GAIN_ROWS, width), F32)],
+                        after(in_terms[0], new_proj[0]), *in_terms[1:])
+    act_out, act_grad = call(
+        functools.partial(act_kernel, n_row), [shape((length, width), BF16), shape((length, width), F32)],
+        place, *pieces, *in_terms, *down_terms, scalars=1)
+    gains_grad = sum_plane(gains_grad, act_out).reshape(-1)[:2 * D + 2 * HD]
     states = (gate_weight, gate_first, gate_second, up_weight, up_first, up_second,
               down_weight, down_first, down_second)
     if small:
-        unit_parts = scatter_row(jnp.split(add(unit_terms).astype(BF16), n_row, axis=2))
+        unit_parts = scatter_row(jnp.split(unit_terms[0].astype(BF16), n_row, axis=2))
         whole = jnp.zeros((3, units, width), F32)
         for k, part in enumerate(unit_parts):
             whole = lax.dynamic_update_slice_in_dim(whole, part.astype(F32), (z ^ k) * share, 1)
@@ -647,19 +696,14 @@
             new_units += adamw(*states[3 * i:3 * i + 3], whole[i].T, MATRIX_RATE, MATRIX_DECAY)
     else:
         new_units = call(functools.partial(units_update_kernel, n_row), [shape((width, units), F32)] * 9,
-                         place, *in_terms, *states,
+                         place, *in_terms, *states, limit=UPDATE_LIMIT,
                          scalars=1, scratch=[pltpu.VMEM((units, width), F32)])
-
-    def update(terms, *states):
-        return call(functools.partial(update_kernel, len(terms), len(states) // 3),
-                    [shape(state.shape, F32) for state in states], *terms, *states)
 
     return (
         act_out,
         act_grad,
         *adamw(gains, gains_first, gains_second, gains_grad, GAIN_RATE, 0.0),
-        *update(proj_terms, query_weight, query_first, query_second, key_weight, key_first, key_second,
-                value_weight, value_first, value_second, output_weight, output_first, output_second),
+        *new_proj,
         *new_units,
     )
 

time: 194 us -> 186 us (0.959); the launches traced: 194 us -> 183 us
  starting transfers between devices: 74 us -> 65.5 us
  waiting for transfers between devices: 78.5 us -> 81.9 us
  local copies, waits for them, and re-layouts: 7.13 us -> 3.92 us
  other arithmetic: 2.88 us -> 0.93 us
    ppermute x26 -> x27, waiting for transfers between devices: 10 us -> 19.9 us  [over_plane(): return lax.ppermute(value, PLANE, [(i, i ^ k) for i in range(n_plane)])]
    ppermute x24 -> x21, starting transfers between devices: 53.1 us -> 44 us  [over_row(): return lax.ppermute(value, 'row', [(i, i ^ k) for i in range(n_row)])]
    ppermute x24 -> x21, waiting for transfers between devices: 68.4 us -> 62 us  [over_row(): return lax.ppermute(value, 'row', [(i, i ^ k) for i in range(n_row)])]
    unnamed x60 -> x64, local copies, waits for them, and re-layouts: 6.82 us -> 3.21 us
    ppermute x26 -> x27, starting transfers between devices: 20.8 us -> 21.5 us  [over_plane(): return lax.ppermute(value, PLANE, [(i, i ^ k) for i in range(n_plane)])]
    pallas_call x19 -> x20, Pallas kernels: 30.4 us -> 30 us  [call(): pl.pallas_call(kernel, out_shape=list(outs), in_specs=[smem] * scalars +...]
  transfers between devices with their start and end apart: 50 -> 48, of which waited for: 23 -> 28; matrix products, arithmetic and copies ran while one was open for 2% -> 0% of each run, Pallas kernels for 9% -> 11%
where the time goes in v3:
time: 186 us; the launch traced here: 183 us
  waiting for transfers between devices  81.9 us (44%)
  starting transfers between devices  65.5 us (35%)
  Pallas kernels  30 us (16%)
  local copies, waits for them, and re-layouts  3.92 us (2%)
    ppermute x21, waiting for transfers between devices, over_row(): return lax.ppermute(value, 'row', [(i, i ^ k) for i in range(n_row)])  62 us
    ppermute x21, starting transfers between devices, over_row(): return lax.ppermute(value, 'row', [(i, i ^ k) for i in range(n_row)])  44 us
    pallas_call x20, Pallas kernels, call(): pl.pallas_call(kernel, out_shape=list(outs), in_specs=[smem] * scalars +...  30 us
    ppermute x27, starting transfers between devices, over_plane(): return lax.ppermute(value, PLANE, [(i, i ^ k) for i in range(n_plane)])  21.5 us
    ppermute x27, waiting for transfers between devices, over_plane(): return lax.ppermute(value, PLANE, [(i, i ^ k) for i in range(n_plane)])  19.9 us
  transfers between devices with their start and end apart: 48, of which 28 were waited for; matrix products, arithmetic and copies ran while one was open for 0% of the time, Pallas kernels for 11%

profile of v3, /device:TPU:0, one launch (start us, length us, event | category | flops | bytes accessed | tf_op | source)
XLA Modules:
  0.0 183.5 jit_solution(8217976385031143756)
XLA Ops:
  0.7 3.1 %pack_kernel.1 = (bf16[1,128,1536]{2,1,0:T(8,128)(2,1)}, bf16[800,256]{1,0:T(8,128)(2,1)}, bf16[800,256]{1,0:T(8,128)(2,1)}, bf16[800,256]{1,0:T(8,128)(2,1)}, bf16[800,256]{1,0:T(8,128)(2,1)}) custom-call(f32[128,512]{1,0:T(8,128)} %rest_5_.4, f32[128,256]{1,0:T(8,128)} %rest_8_.4, f32[128,256]{1,0:T(8,128)} %rest_11_.2, f32[128,512]{1,0:T(8,128)} %rest_14_.1, ...), custom_call_target="tpu_custom_call" | custom-call | flops 1 | bytes 1 | tf_op jit(solution)/shard_map/pack_kernel/pallas_call | solution.py:57
  3.8 4.0 %collective-permute-start.5 = (bf16[1,128,1536]{2,1,0:T(8,128)(2,1)}, bf16[1,128,1536]{2,1,0:T(8,128)(2,1)S(1)}, u32[]{:S(2)}, u32[]{:S(2)}) collective-permute-start(bf16[1,128,1536]{2,1,0:T(8,128)(2,1)} %get-tuple-element.129.rest_4_), channel_id=1, source_target_pairs={{0,18},{1,19},{2,16},{3,17},{16,2},{17,3},{18,0},{19,1},{4,22},{5,... | collective-permute-start | bytes 1179656 | tf_op jit(solution)/shard_map/ppermute | solution.py:517
  10.4 2.6 %collective-permute-start.1 = (bf16[800,256]{1,0:T(8,128)(2,1)}, bf16[800,256]{1,0:T(8,128)(2,1)S(1)}, u32[]{:S(2)}, u32[]{:S(2)}) collective-permute-start(bf16[800,256]{1,0:T(8,128)(2,1)} %get-tuple-element.127), channel_id=1, source_target_pairs={{0,8},{4,12},{8,0},{12,4},{1,9},{5,13},{9,1},{13,5},{2,10},{6,14},... | collective-permute-start | bytes 1228808 | tf_op jit(solution)/shard_map/ppermute | solution.py:514
  13.0 5.0 %collective-permute-done.5.rest_7_ = bf16[1,128,1536]{2,1,0:T(8,128)(2,1)S(1)} collective-permute-done((bf16[1,128,1536]{2,1,0:T(8,128)(2,1)}, bf16[1,128,1536]{2,1,0:T(8,128)(2,1)S(1)}, u32[]{:S(2)}, u32[]{:S(2)}) %collective-permute-start.5) | collective-permute-done | bytes 393248 | tf_op jit(solution)/shard_map/ppermute | solution.py:517
  17.9 4.1 %collective-permute-start.2 = (bf16[800,256]{1,0:T(8,128)(2,1)}, bf16[800,256]{1,0:T(8,128)(2,1)S(1)}, u32[]{:S(2)}, u32[]{:S(2)}) collective-permute-start(bf16[800,256]{1,0:T(8,128)(2,1)} %get-tuple-element.128), channel_id=1, source_target_pairs={{0,12},{4,8},{8,4},{12,0},{1,13},{5,9},{9,5},{13,1},{2,14},{6,10},... | collective-permute-start | bytes 1228808 | tf_op jit(solution)/shard_map/ppermute | solution.py:514
  27.1 13.9 %collective-permute-done.1.rest_2_ = bf16[800,256]{1,0:T(8,128)(2,1)S(1)} collective-permute-done((bf16[800,256]{1,0:T(8,128)(2,1)}, bf16[800,256]{1,0:T(8,128)(2,1)S(1)}, u32[]{:S(2)}, u32[]{:S(2)}) %collective-permute-start.1) | collective-permute-done | bytes 409632 | tf_op jit(solution)/shard_map/ppermute | solution.py:514
  46.5 3.9 %attend_kernel.1 = (bf16[256,512]{1,0:T(8,128)(2,1)S(1)}, f32[1024,256]{1,0:T(8,128)S(1)}, bf16[256,512]{1,0:T(8,128)(2,1)S(1)}, bf16[256,256]{1,0:T(8,128)(2,1)...) custom-call(s32[9]{0:T(128)S(1)} %pad_add_fusion.place, ...), custom_call_target="tpu_custom_call" | custom-call | flops 1 | bytes 1 | tf_op jit(solution)/shard_map/attend_kernel/pallas_call | solution.py:57
  51.5 6.9 %collective-permute-start.10 = (bf16[64,1024]{1,0:T(8,128)(2,1)S(1)}, bf16[64,1024]{1,0:T(8,128)(2,1)S(1)}, u32[]{:S(2)}, u32[]{:S(2)}) collective-permute-start(bf16[64,1024]{1,0:T(8,128)(2,1)S(1)} %get-tuple-element.138), channel_id=1, source_target_pairs={{0,4},{4,0},{8,12},{12,8},{1,5},{5,1},{9,13},{13,9},{2,6},{6,2},{1... | collective-permute-start | bytes 393224 | tf_op jit(solution)/shard_map/ppermute | solution.py:514
  61.3 3.2 %collective-permute-start.12 = (bf16[64,1024]{1,0:T(8,128)(2,1)S(1)}, bf16[64,1024]{1,0:T(8,128)(2,1)S(1)}, u32[]{:S(2)}, u32[]{:S(2)}) collective-permute-start(bf16[64,1024]{1,0:T(8,128)(2,1)S(1)} %get-tuple-element.140), channel_id=1, source_target_pairs={{0,12},{4,8},{8,4},{12,0},{1,13},{5,9},{9,5},{13,1},{2,14},{6,10},... | collective-permute-start | bytes 393224 | tf_op jit(solution)/shard_map/ppermute | solution.py:514
  64.5 4.4 %collective-permute-done.11.rest_2_ = bf16[64,1024]{1,0:T(8,128)(2,1)S(1)} collective-permute-done((bf16[64,1024]{1,0:T(8,128)(2,1)S(1)}, bf16[64,1024]{1,0:T(8,128)(2,1)S(1)}, u32[]{:S(2)}, u32[]{:S(2)}) %collective-permute-start.11) | collective-permute-done | bytes 131104 | tf_op jit(solution)/shard_map/ppermute | solution.py:514
  72.5 3.0 %collective-permute-start.19 = (bf16[64,1024]{1,0:T(8,128)(2,1)S(1)}, bf16[64,1024]{1,0:T(8,128)(2,1)S(1)}, u32[]{:S(2)}, u32[]{:S(2)}) collective-permute-start(bf16[64,1024]{1,0:T(8,128)(2,1)S(1)} %get-tuple-element.143.rest_0_), channel_id=1, source_target_pairs={{0,12},{4,8},{8,4},{12,0},{1,13},{5,9},{9,5},{13,1},{2,14},{6,10},... | collective-permute-start | bytes 393224 | tf_op jit(solution)/shard_map/ppermute | solution.py:514
  75.5 3.1 %collective-permute-start.18 = (bf16[64,1024]{1,0:T(8,128)(2,1)S(1)}, bf16[64,1024]{1,0:T(8,128)(2,1)S(1)}, u32[]{:S(2)}, u32[]{:S(2)}) collective-permute-start(bf16[64,1024]{1,0:T(8,128)(2,1)S(1)} %get-tuple-element.143.rest_0_), channel_id=1, source_target_pairs={{0,8},{4,12},{8,0},{12,4},{1,9},{5,13},{9,1},{13,5},{2,10},{6,14},... | collective-permute-start | bytes 393224 | tf_op jit(solution)/shard_map/ppermute | solution.py:514
  80.3 8.4 %collective-permute-done.18.rest_2_ = bf16[64,1024]{1,0:T(8,128)(2,1)S(1)} collective-permute-done((bf16[64,1024]{1,0:T(8,128)(2,1)S(1)}, bf16[64,1024]{1,0:T(8,128)(2,1)S(1)}, u32[]{:S(2)}, u32[]{:S(2)}) %collective-permute-start.18) | collective-permute-done | bytes 131104 | tf_op jit(solution)/shard_map/ppermute | solution.py:514
  88.7 3.8 %units_kernel.1 = (f32[64,1024]{1,0:T(8,128)S(1)}, bf16[64,1024]{1,0:T(8,128)(2,1)S(1)}, bf16[64,1024]{1,0:T(8,128)(2,1)S(1)}, bf16[64,1024]{1,0:T(8,128)(2,1)S(...) custom-call(s32[9]{0:T(128)S(1)} %pad_add_fusion.place, ...), custom_call_target="tpu_custom_call" | custom-call | flops 1 | bytes 1 | tf_op jit(solution)/shard_map/units_kernel/pallas_call | solution.py:57
  94.2 3.4 %collective-permute-start.22 = (bf16[64,1024]{1,0:T(8,128)(2,1)S(1)}, bf16[64,1024]{1,0:T(8,128)(2,1)S(1)}, u32[]{:S(2)}, u32[]{:S(2)}) collective-permute-start(bf16[64,1024]{1,0:T(8,128)(2,1)S(1)} %get-tuple-element.154), channel_id=1, source_target_pairs={{0,8},{4,12},{8,0},{12,4},{1,9},{5,13},{9,1},{13,5},{2,10},{6,14},... | collective-permute-start | bytes 393224 | tf_op jit(solution)/shard_map/ppermute | solution.py:514
  99.0 3.3 %collective-permute-done.21.rest_1_ = bf16[64,1024]{1,0:T(8,128)(2,1)S(1)} collective-permute-done((bf16[64,1024]{1,0:T(8,128)(2,1)S(1)}, bf16[64,1024]{1,0:T(8,128)(2,1)S(1)}, u32[]{:S(2)}, u32[]{:S(2)}) %collective-permute-start.21) | collective-permute-done | bytes 131104 | tf_op jit(solution)/shard_map/ppermute | solution.py:514
  102.4 5.2 %collective-permute-done.22.rest_2_ = bf16[64,1024]{1,0:T(8,128)(2,1)S(1)} collective-permute-done((bf16[64,1024]{1,0:T(8,128)(2,1)S(1)}, bf16[64,1024]{1,0:T(8,128)(2,1)S(1)}, u32[]{:S(2)}, u32[]{:S(2)}) %collective-permute-start.22) | collective-permute-done | bytes 131104 | tf_op jit(solution)/shard_map/ppermute | solution.py:514
  115.3 7.7 %collective-permute-done.25.rest_2_ = bf16[64,1024]{1,0:T(8,128)(2,1)S(1)} collective-permute-done((bf16[64,1024]{1,0:T(8,128)(2,1)S(1)}, bf16[64,1024]{1,0:T(8,128)(2,1)S(1)}, u32[]{:S(2)}, u32[]{:S(2)}) %collective-permute-start.25) | collective-permute-done | bytes 131104 | tf_op jit(solution)/shard_map/ppermute | solution.py:514
  126.1 2.9 %collective-permute-start.34 = (bf16[256,256]{1,0:T(8,128)(2,1)S(1)}, bf16[256,256]{1,0:T(8,128)(2,1)S(1)}, u32[]{:S(2)}, u32[]{:S(2)}) collective-permute-start(bf16[256,256]{1,0:T(8,128)(2,1)S(1)} %get-tuple-element.181), channel_id=1, source_target_pairs={{0,8},{4,12},{8,0},{12,4},{1,9},{5,13},{9,1},{13,5},{2,10},{6,14},... | collective-permute-start | bytes 393224 | tf_op jit(solution)/shard_map/ppermute | solution.py:514
  129.0 3.8 %collective-permute-done.33.rest_9_ = bf16[256,256]{1,0:T(8,128)(2,1)S(1)} collective-permute-done((bf16[256,256]{1,0:T(8,128)(2,1)S(1)}, bf16[256,256]{1,0:T(8,128)(2,1)S(1)}, u32[]{:S(2)}, u32[]{:S(2)}) %collective-permute-start.33) | collective-permute-done | bytes 131104 | tf_op jit(solution)/shard_map/ppermute | solution.py:514
  134.6 3.1 %attend_back_kernel.1 = (bf16[256,1024]{1,0:T(8,128)(2,1)S(1)}, f32[1,128]{1,0:T(1,128)S(1)}, f32[1,128]{1,0:T(1,128)S(1)}, bf16[256,1024]{1,0:T(8,128)(2,1)S(1)}) custom-call(s32[9]{0:T(128)S(1)} %pad_add_fusion.place, bf16[64,1024]{1,0:T(8,128)(2,1)S(1)} %get-tuple-element.156.rest_0_, bf16[64,1024]{1,0:T(8,128)(2,1)S(1)} %collective-permute-done.24.rest_1_, ...), custom_call_target="tpu_custom_call" | custom-call | flops 1 | bytes 1 | tf_op jit(solution)/shard_map/attend_back_kernel/pallas_call | solution.py:57
  159.5 3.6 %collective-permute-done.42.rest_3_ = bf16[1,128,768]{2,1,0:T(8,128)(2,1)S(1)} collective-permute-done((bf16[1,128,768]{2,1,0:T(8,128)(2,1)S(1)}, bf16[1,128,768]{2,1,0:T(8,128)(2,1)S(1)}, u32[]{:S(2)}, u32[]{:S(2)}) %collective-permute-start.42) | collective-permute-done | bytes 196640 | tf_op jit(solution)/shard_map/ppermute | solution.py:517
  166.5 8.3 %collective-permute-done.31.rest_6_.rest_2_ = bf16[560,256]{1,0:T(8,128)(2,1)S(1)} collective-permute-done((bf16[560,256]{1,0:T(8,128)(2,1)S(1)}, bf16[560,256]{1,0:T(8,128)(2,1)S(1)}, u32[]{:S(2)}, u32[]{:S(2)}) %collective-permute-start.31) | collective-permute-done | bytes 286752 | tf_op jit(solution)/shard_map/ppermute | solution.py:514
  179.9 2.9 %units_update_kernel.1 = (f32[256,384]{1,0:T(8,128)}, f32[256,384]{1,0:T(8,128)}, f32[256,384]{1,0:T(8,128)}, f32[256,384]{1,0:T(8,128)}, f32[256,384]{1,0:T(8,1...) custom-call(s32[9]{0:T(128)S(1)} %pad_add_fusion.place, ...), custom_call_target="tpu_custom_call" | custom-call | flops 1 | bytes 1 | tf_op jit(solution)/shard_map/units_update_kernel/pallas_call | solution.py:57
  (164 shorter events, 68.6 us)
Async XLA Ops:
  3.8 14.2 %collective-permute-start.5 = (bf16[1,128,1536]{2,1,0:T(8,128)(2,1)}, bf16[1,128,1536]{2,1,0:T(8,128)(2,1)S(1)}, u32[]{:S(2)}, u32[]{:S(2)}) collective-permute-start(bf16[1,128,1536]{2,1,0:T(8,128)(2,1)} %get-tuple-element.129.rest_4_), channel_id=1, source_target_pairs={{0,18},{1,19},{2,16},{3,17},{16,2},{17,3},{18,0},{19,1},{4,22},{5,... | collective-permute-start | bytes 1179656 | tf_op jit(solution)/shard_map/ppermute | solution.py:517
  7.7 17.8 %collective-permute-start.4 = (bf16[1,128,1536]{2,1,0:T(8,128)(2,1)}, bf16[1,128,1536]{2,1,0:T(8,128)(2,1)S(1)}, u32[]{:S(2)}, u32[]{:S(2)}) collective-permute-start(bf16[1,128,1536]{2,1,0:T(8,128)(2,1)} %get-tuple-element.129.rest_4_), channel_id=1, source_target_pairs={{0,16},{1,17},{2,18},{3,19},{16,0},{17,1},{18,2},{19,3},{4,20},{5,... | collective-permute-start | bytes 1179656 | tf_op jit(solution)/shard_map/ppermute | solution.py:517
  8.3 17.5 %collective-permute-start.3 = (bf16[1,128,1536]{2,1,0:T(8,128)(2,1)}, bf16[1,128,1536]{2,1,0:T(8,128)(2,1)S(1)}, u32[]{:S(2)}, u32[]{:S(2)}) collective-permute-start(bf16[1,128,1536]{2,1,0:T(8,128)(2,1)} %get-tuple-element.129.rest_4_), channel_id=1, source_target_pairs={{0,2},{1,3},{2,0},{3,1},{16,18},{17,19},{18,16},{19,17},{4,6},{5,7... | collective-permute-start | bytes 1179656 | tf_op jit(solution)/shard_map/ppermute | solution.py:517
  8.4 18.7 %collective-permute-start = (bf16[800,256]{1,0:T(8,128)(2,1)}, bf16[800,256]{1,0:T(8,128)(2,1)S(1)}, u32[]{:S(2)}, u32[]{:S(2)}) collective-permute-start(bf16[800,256]{1,0:T(8,128)(2,1)} %get-tuple-element.126), channel_id=1, source_target_pairs={{0,4},{4,0},{8,12},{12,8},{1,5},{5,1},{9,13},{13,9},{2,6},{6,2},{1... | collective-permute-start | bytes 1228808 | tf_op jit(solution)/shard_map/ppermute | solution.py:514
  10.4 30.6 %collective-permute-start.1 = (bf16[800,256]{1,0:T(8,128)(2,1)}, bf16[800,256]{1,0:T(8,128)(2,1)S(1)}, u32[]{:S(2)}, u32[]{:S(2)}) collective-permute-start(bf16[800,256]{1,0:T(8,128)(2,1)} %get-tuple-element.127), channel_id=1, source_target_pairs={{0,8},{4,12},{8,0},{12,4},{1,9},{5,13},{9,1},{13,5},{2,10},{6,14},... | collective-permute-start | bytes 1228808 | tf_op jit(solution)/shard_map/ppermute | solution.py:514
  17.9 23.8 %collective-permute-start.2 = (bf16[800,256]{1,0:T(8,128)(2,1)}, bf16[800,256]{1,0:T(8,128)(2,1)S(1)}, u32[]{:S(2)}, u32[]{:S(2)}) collective-permute-start(bf16[800,256]{1,0:T(8,128)(2,1)} %get-tuple-element.128), channel_id=1, source_target_pairs={{0,12},{4,8},{8,4},{12,0},{1,13},{5,9},{9,5},{13,1},{2,14},{6,10},... | collective-permute-start | bytes 1228808 | tf_op jit(solution)/shard_map/ppermute | solution.py:514
  25.5 19.8 %collective-permute-start.6 = (bf16[1,128,1536]{2,1,0:T(8,128)(2,1)}, bf16[1,128,1536]{2,1,0:T(8,128)(2,1)S(1)}, u32[]{:S(2)}, u32[]{:S(2)}) collective-permute-start(bf16[1,128,1536]{2,1,0:T(8,128)(2,1)} %get-tuple-element.129.rest_4_), channel_id=1, source_target_pairs={{0,1},{1,0},{2,3},{3,2},{16,17},{17,16},{18,19},{19,18},{4,5},{5,4... | collective-permute-start | bytes 1179656 | tf_op jit(solution)/shard_map/ppermute | solution.py:517
  25.8 20.0 %collective-permute-start.9 = (bf16[1,128,1536]{2,1,0:T(8,128)(2,1)S(1)}, bf16[1,128,1536]{2,1,0:T(8,128)(2,1)S(1)}, u32[]{:S(2)}, u32[]{:S(2)}) collective-permute-start(bf16[1,128,1536]{2,1,0:T(8,128)(2,1)S(1)} %collective-permute-done.5.rest_7_), channel_id=1, source_target_pairs={{0,1},{1,0},{2,3},{3,2},{16,17},{17,16},{18,19},{19,18},{4,5},{5,4... | collective-permute-start | bytes 1179656 | tf_op jit(solution)/shard_map/ppermute | solution.py:517
  27.1 19.4 %collective-permute-start.8 = (bf16[1,128,1536]{2,1,0:T(8,128)(2,1)S(1)}, bf16[1,128,1536]{2,1,0:T(8,128)(2,1)}, u32[]{:S(2)}, u32[]{:S(2)}) collective-permute-start(bf16[1,128,1536]{2,1,0:T(8,128)(2,1)S(1)} %collective-permute-done.4.rest_6_), channel_id=1, source_target_pairs={{0,1},{1,0},{2,3},{3,2},{16,17},{17,16},{18,19},{19,18},{4,5},{5,4... | collective-permute-start | bytes 1179656 | tf_op jit(solution)/shard_map/ppermute | solution.py:517
  42.8 26.9 %collective-permute-start.15 = (bf16[3,96,1024]{2,1,0:T(8,128)(2,1)S(1)}, bf16[3,96,1024]{2,1,0:T(8,128)(2,1)S(1)}, u32[]{:S(2)}, u32[]{:S(2)}) collective-permute-start(bf16[3,96,1024]{2,1,0:T(8,128)(2,1)S(1)} %join_kernel.1), channel_id=1, source_target_pairs={{0,18},{1,19},{2,16},{3,17},{16,2},{17,3},{18,0},{19,1},{4,22},{5,... | collective-permute-start | bytes 1769480 | tf_op jit(solution)/shard_map/ppermute | solution.py:517
  45.3 26.9 %collective-permute-start.14 = (bf16[3,96,1024]{2,1,0:T(8,128)(2,1)S(1)}, bf16[3,96,1024]{2,1,0:T(8,128)(2,1)S(1)}, u32[]{:S(2)}, u32[]{:S(2)}) collective-permute-start(bf16[3,96,1024]{2,1,0:T(8,128)(2,1)S(1)} %join_kernel.1), channel_id=1, source_target_pairs={{0,16},{1,17},{2,18},{3,19},{16,0},{17,1},{18,2},{19,3},{4,20},{5,... | collective-permute-start | bytes 1769480 | tf_op jit(solution)/shard_map/ppermute | solution.py:517
  45.8 26.4 %collective-permute-start.13 = (bf16[3,96,1024]{2,1,0:T(8,128)(2,1)S(1)}, bf16[3,96,1024]{2,1,0:T(8,128)(2,1)S(1)}, u32[]{:S(2)}, u32[]{:S(2)}) collective-permute-start(bf16[3,96,1024]{2,1,0:T(8,128)(2,1)S(1)} %join_kernel.1), channel_id=1, source_target_pairs={{0,2},{1,3},{2,0},{3,1},{16,18},{17,19},{18,16},{19,17},{4,6},{5,7... | collective-permute-start | bytes 1769480 | tf_op jit(solution)/shard_map/ppermute | solution.py:517
  72.4 16.2 %collective-permute-start.16 = (bf16[3,384,1024]{2,1,0:T(8,128)(2,1)S(1)}, bf16[3,384,1024]{2,1,0:T(8,128)(2,1)S(1)}, u32[]{:S(2)}, u32[]{:S(2)}) collective-permute-start(bf16[3,384,1024]{2,1,0:T(8,128)(2,1)S(1)} %pad_maximum_fusion.wz_ref), channel_id=1, source_target_pairs={{0,1},{1,0},{2,3},{3,2},{16,17},{17,16},{18,19},{19,18},{4,5},{5,4... | collective-permute-start | bytes 7077896 | tf_op jit(solution)/shard_map/ppermute | solution.py:517
  75.5 13.1 %collective-permute-start.18 = (bf16[64,1024]{1,0:T(8,128)(2,1)S(1)}, bf16[64,1024]{1,0:T(8,128)(2,1)S(1)}, u32[]{:S(2)}, u32[]{:S(2)}) collective-permute-start(bf16[64,1024]{1,0:T(8,128)(2,1)S(1)} %get-tuple-element.143.rest_0_), channel_id=1, source_target_pairs={{0,8},{4,12},{8,0},{12,4},{1,9},{5,13},{9,1},{13,5},{2,10},{6,14},... | collective-permute-start | bytes 393224 | tf_op jit(solution)/shard_map/ppermute | solution.py:514
  94.2 13.3 %collective-permute-start.22 = (bf16[64,1024]{1,0:T(8,128)(2,1)S(1)}, bf16[64,1024]{1,0:T(8,128)(2,1)S(1)}, u32[]{:S(2)}, u32[]{:S(2)}) collective-permute-start(bf16[64,1024]{1,0:T(8,128)(2,1)S(1)} %get-tuple-element.154), channel_id=1, source_target_pairs={{0,8},{4,12},{8,0},{12,4},{1,9},{5,13},{9,1},{13,5},{2,10},{6,14},... | collective-permute-start | bytes 393224 | tf_op jit(solution)/shard_map/ppermute | solution.py:514
  110.8 12.3 %collective-permute-start.25 = (bf16[64,1024]{1,0:T(8,128)(2,1)S(1)}, bf16[64,1024]{1,0:T(8,128)(2,1)S(1)}, u32[]{:S(2)}, u32[]{:S(2)}) collective-permute-start(bf16[64,1024]{1,0:T(8,128)(2,1)S(1)} %get-tuple-element.156.rest_0_), channel_id=1, source_target_pairs={{0,8},{4,12},{8,0},{12,4},{1,9},{5,13},{9,1},{13,5},{2,10},{6,14},... | collective-permute-start | bytes 393224 | tf_op jit(solution)/shard_map/ppermute | solution.py:514
  112.7 27.0 %collective-permute-start.27 = (bf16[3,96,1024]{2,1,0:T(8,128)(2,1)S(1)}, bf16[3,96,1024]{2,1,0:T(8,128)(2,1)S(1)}, u32[]{:S(2)}, u32[]{:S(2)}) collective-permute-start(bf16[3,96,1024]{2,1,0:T(8,128)(2,1)S(1)} %get-tuple-element.164), channel_id=1, source_target_pairs={{0,2},{1,3},{2,0},{3,1},{16,18},{17,19},{18,16},{19,17},{4,6},{5,7... | collective-permute-start | bytes 1769480 | tf_op jit(solution)/shard_map/ppermute | solution.py:517
  114.2 26.7 %collective-permute-start.28 = (bf16[3,96,1024]{2,1,0:T(8,128)(2,1)S(1)}, bf16[3,96,1024]{2,1,0:T(8,128)(2,1)S(1)}, u32[]{:S(2)}, u32[]{:S(2)}) collective-permute-start(bf16[3,96,1024]{2,1,0:T(8,128)(2,1)S(1)} %get-tuple-element.166), channel_id=1, source_target_pairs={{0,16},{1,17},{2,18},{3,19},{16,0},{17,1},{18,2},{19,3},{4,20},{5,... | collective-permute-start | bytes 1769480 | tf_op jit(solution)/shard_map/ppermute | solution.py:517
  123.1 17.8 %collective-permute-start.29 = (bf16[3,96,1024]{2,1,0:T(8,128)(2,1)S(1)}, bf16[3,96,1024]{2,1,0:T(8,128)(2,1)S(1)}, u32[]{:S(2)}, u32[]{:S(2)}) collective-permute-start(bf16[3,96,1024]{2,1,0:T(8,128)(2,1)S(1)} %get-tuple-element.168), channel_id=1, source_target_pairs={{0,18},{1,19},{2,16},{3,17},{16,2},{17,3},{18,0},{19,1},{4,22},{5,... | collective-permute-start | bytes 1769480 | tf_op jit(solution)/shard_map/ppermute | solution.py:517
  126.1 11.6 %collective-permute-start.34 = (bf16[256,256]{1,0:T(8,128)(2,1)S(1)}, bf16[256,256]{1,0:T(8,128)(2,1)S(1)}, u32[]{:S(2)}, u32[]{:S(2)}) collective-permute-start(bf16[256,256]{1,0:T(8,128)(2,1)S(1)} %get-tuple-element.181), channel_id=1, source_target_pairs={{0,8},{4,12},{8,0},{12,4},{1,9},{5,13},{9,1},{13,5},{2,10},{6,14},... | collective-permute-start | bytes 393224 | tf_op jit(solution)/shard_map/ppermute | solution.py:514
  145.7 11.2 %collective-permute-start.40 = (bf16[2,128,768]{2,1,0:T(8,128)(2,1)S(1)}, bf16[2,128,768]{2,1,0:T(8,128)(2,1)S(1)}, u32[]{:S(2)}, u32[]{:S(2)}) collective-permute-start(bf16[2,128,768]{2,1,0:T(8,128)(2,1)S(1)} %get-tuple-element.195), channel_id=1, source_target_pairs={{0,2},{1,3},{2,0},{3,1},{16,18},{17,19},{18,16},{19,17},{4,6},{5,7... | collective-permute-start | bytes 1179656 | tf_op jit(solution)/shard_map/ppermute | solution.py:517
  150.0 16.5 %collective-permute-start.30 = (bf16[560,256]{1,0:T(8,128)(2,1)S(1)}, bf16[560,256]{1,0:T(8,128)(2,1)S(1)}, u32[]{:S(2)}, u32[]{:S(2)}) collective-permute-start(bf16[560,256]{1,0:T(8,128)(2,1)S(1)} %get-tuple-element.173), channel_id=1, source_target_pairs={{0,4},{4,0},{8,12},{12,8},{1,5},{5,1},{9,13},{13,9},{2,6},{6,2},{1... | collective-permute-start | bytes 860168 | tf_op jit(solution)/shard_map/ppermute | solution.py:514
  151.8 23.0 %collective-permute-start.31 = (bf16[560,256]{1,0:T(8,128)(2,1)S(1)}, bf16[560,256]{1,0:T(8,128)(2,1)S(1)}, u32[]{:S(2)}, u32[]{:S(2)}) collective-permute-start(bf16[560,256]{1,0:T(8,128)(2,1)S(1)} %get-tuple-element.174), channel_id=1, source_target_pairs={{0,8},{4,12},{8,0},{12,4},{1,9},{5,13},{9,1},{13,5},{2,10},{6,14},... | collective-permute-start | bytes 860168 | tf_op jit(solution)/shard_map/ppermute | solution.py:514
  152.8 21.9 %collective-permute-start.32 = (bf16[560,256]{1,0:T(8,128)(2,1)S(1)}, bf16[560,256]{1,0:T(8,128)(2,1)S(1)}, u32[]{:S(2)}, u32[]{:S(2)}) collective-permute-start(bf16[560,256]{1,0:T(8,128)(2,1)S(1)} %get-tuple-element.175), channel_id=1, source_target_pairs={{0,12},{4,8},{8,4},{12,0},{1,13},{5,9},{9,5},{13,1},{2,14},{6,10},... | collective-permute-start | bytes 860168 | tf_op jit(solution)/shard_map/ppermute | solution.py:514
  (56 other events, 555.8 us)

commit v4 on v3

--- a/solution.py
+++ b/solution.py
@@ -23,7 +23,7 @@
 MASK_VALUE = -1e30
 LANE = 128
 BLOCKS = D // LANE
-ATTEND_LIMIT = 40
+ATTEND_LIMIT = 28
 UPDATE_LIMIT = 16
 GAIN_ROWS = 16
 PLANE = ("dp", "col")
@@ -107,9 +107,9 @@
 
 
 def attend_kernel(n, place, *rest):
-    blocks = len(rest) - n - 14
+    blocks = len(rest) - n - 13
     xs, ws, (gains_ref, cos_ref, sin_ref, mask_ref, ctx_ref, prob_ref, q_ref, k_ref, v_ref, raw_ref, norm_ref, x_ref,
-             cot_ref, w_ref) = rest[:n], rest[n:n + blocks], rest[n + blocks:]
+             w_ref) = rest[:n], rest[n:n + blocks], rest[n + blocks:]
     height = D // blocks
     for i, w in enumerate(ws):
         w_ref[i * height:(i + 1) * height, :] = w[0]
@@ -117,7 +117,6 @@
     part = D // n
     for k in range(n):
         x_ref[:, k * part:(k + 1) * part] = xs[k][:x_ref.shape[0], :]
-        cot_ref[:, k * part:(k + 1) * part] = xs[k][x_ref.shape[0]:2 * x_ref.shape[0], :]
     x = x_ref[...].astype(F32)
     r1 = lax.rsqrt(jnp.mean(x * x, axis=-1, keepdims=True) + EPSILON)
     for j in range(BLOCKS):
@@ -191,9 +190,9 @@
     return hidden, dgate, dup
 
 
-def units_kernel(n, place, cot_ref, wz_ref, wo_ref, *rest):
-    pieces, outs = rest[:n], rest[n:2 * n]
-    mid_ref, hid_ref, dgu_ref, dmid_ref = rest[2 * n:]
+def units_kernel(n, place, wz_ref, wo_ref, *rest):
+    cots, pieces, outs = rest[:n], rest[n:2 * n], rest[2 * n:3 * n]
+    mid_ref, hid_ref, dgu_ref, cot_ref, dmid_ref = rest[3 * n:]
     z = place[0]
     size = pieces[0].shape[0]
     part = D // n
@@ -201,6 +200,7 @@
         for q in range(n):
             mid_ref[rows_of(z ^ k, size), q * part:(q + 1) * part] = (
                 pieces[k][:, (q ^ k) * part:((q ^ k) + 1) * part])
+        cot_ref[:, k * part:(k + 1) * part] = cots[k][...]
     mid = mid_ref[...]
     cot = cot_ref[...]
     units = wz_ref.shape[1]
@@ -239,7 +239,7 @@
 
 def pack_kernel(n, *rest):
     z = lax.axis_index("row")
-    sources, out_ref, outs, buffers = rest[:9], rest[9], rest[10:10 + n], rest[10 + n:]
+    sources, out_ref, outs, buffers = rest[:8], rest[8], rest[9:9 + n], rest[9 + n:]
     (*held, scratch, sems) = buffers
     copies = [pltpu.make_async_copy(src, dst, sems.at[i]) for i, (src, dst) in enumerate(zip(sources, held))]
     for copy in copies:
@@ -249,15 +249,13 @@
         copy.wait()
         out_ref[0, :, at:at + ref.shape[1]] = ref[...].astype(BF16)
         at += ref.shape[1]
-    x, cot = held[4:6]
-    length = 2 * x.shape[0]
+    x = held[4]
+    length = x.shape[0]
     size = (outs[0].shape[0] - length) // 3
     copies[4].wait()
-    copies[5].wait()
     for out in outs:
-        out[:length // 2, :] = x[...]
-        out[length // 2:length, :] = cot[...]
-    for i, (copy, ref) in enumerate(zip(copies[6:], held[6:])):
+        out[:length, :] = x[...]
+    for i, (copy, ref) in enumerate(zip(copies[5:], held[5:])):
         copy.wait()
         scratch[...] = ref[...].T.astype(BF16)
         for k, out in enumerate(outs):
@@ -573,15 +571,15 @@
         joined = jnp.stack([gate_weight, up_weight, down_weight]).astype(BF16).transpose(0, 2, 1)
         parts = [lax.dynamic_slice_in_dim(joined, (z ^ k) * share, share, 1) for k in range(n_row)]
         units_mine = jnp.concatenate(scatter_row(parts), axis=2)
-        xs = gather_row(jnp.concatenate([act_in, act_cot], axis=0))
+        xs = gather_row(act_in)
     else:
         w_here, *xs = call(
             functools.partial(pack_kernel, n_row),
-            [shape((1, rows, cols), BF16)] + [shape((2 * length + 3 * share, width), BF16)] * n_row,
-            query_weight, key_weight, value_weight, output_weight, act_in, act_cot,
-            gate_weight, up_weight, down_weight, hbm=9, limit=59,
-            scratch=[pltpu.VMEM((rows, w), F32) for w in (qw, kw, kw, qw)] + [pltpu.VMEM((length, width), BF16)] * 2
-            + [pltpu.VMEM((width, units), F32)] * 3 + [pltpu.VMEM((units, width), BF16), pltpu.SemaphoreType.DMA((9,))])
+            [shape((1, rows, cols), BF16)] + [shape((length + 3 * share, width), BF16)] * n_row,
+            query_weight, key_weight, value_weight, output_weight, act_in,
+            gate_weight, up_weight, down_weight, hbm=8, limit=59,
+            scratch=[pltpu.VMEM((rows, w), F32) for w in (qw, kw, kw, qw)] + [pltpu.VMEM((length, width), BF16)]
+            + [pltpu.VMEM((width, units), F32)] * 3 + [pltpu.VMEM((units, width), BF16), pltpu.SemaphoreType.DMA((8,))])
         xs = scatter_row(xs)
     if paired:
         near = [w_here] + [over_plane(w_here, k) for k in (2, 4, 6)]
@@ -594,11 +592,11 @@
     w_parts = near + [over_plane(part, 1) for part in near] if paired else near
 
     heads = qw // HD
-    context, probs, queries, keys, values, raw, normed, x_row, cot_row, w_proj = call(
+    context, probs, queries, keys, values, raw, normed, x_row, w_proj = call(
         functools.partial(attend_kernel, n_row),
         [shape((length, qw), BF16), shape((heads * length, length), F32), shape((length, qw), BF16),
          shape((length, kw), BF16), shape((length, kw), BF16), shape((length, qw + kw), F32),
-         shape((length, D), BF16), shape((length, D), BF16), shape((length, D), BF16),
+         shape((length, D), BF16), shape((length, D), BF16),
          shape((D, 2 * qw + 2 * kw), BF16)],
         place, *xs, *w_parts, gain, cosine, sine, mask, scalars=1, limit=ATTEND_LIMIT)
     if not small:
@@ -617,13 +615,15 @@
         place, x_row, gain, *terms, scalars=1)
 
     mids = gather_row(mid)
-    units_z, units_o = far_plane(after(units_near, mid), axis=1)
+    units_z, units_o = far_plane(after(units_near, *mids), axis=1)
+    cots = gather_row(after(act_cot, mid))
     here = 2 * units_z.shape[1]
-    *dmid_terms, mid_all, hidden, d_units = call(
+    *dmid_terms, mid_all, hidden, d_units, cot_row = call(
         functools.partial(units_kernel, n_row),
         [shape((size, D), F32 if k == 0 else BF16) for k in range(n_row)]
-        + [shape((length, D), BF16), shape((length, here), BF16), shape((2, length, here), BF16)],
-        place, cot_row, units_z, units_o, *mids,
+        + [shape((length, D), BF16), shape((length, here), BF16), shape((2, length, here), BF16),
+           shape((length, D), BF16)],
+        place, units_z, units_o, *cots, *mids,
         scalars=1, scratch=[pltpu.VMEM((length, D), F32)])
     dmid_terms = scatter_row(dmid_terms)
     unit_grad_z, unit_grad_o = call(

time: 186 us -> 183 us (0.984)
  starting transfers between devices: 65.5 us -> 56.9 us
  waiting for transfers between devices: 81.9 us -> 84.8 us
  local copies, waits for them, and re-layouts: 3.92 us -> 6.78 us
    ppermute x21 -> x24, waiting for transfers between devices: 62 us -> 70.4 us  [over_row(): return lax.ppermute(value, 'row', [(i, i ^ k) for i in range(n_row)])]
    ppermute x21 -> x24, starting transfers between devices: 44 us -> 37.3 us  [over_row(): return lax.ppermute(value, 'row', [(i, i ^ k) for i in range(n_row)])]
    ppermute x27, waiting for transfers between devices: 19.9 us -> 14.4 us  [over_plane(): return lax.ppermute(value, PLANE, [(i, i ^ k) for i in range(n_plane)])]
    unnamed x64 -> x66, local copies, waits for them, and re-layouts: 3.21 us -> 6.06 us
    ppermute x27, starting transfers between devices: 21.5 us -> 19.6 us  [over_plane(): return lax.ppermute(value, PLANE, [(i, i ^ k) for i in range(n_plane)])]
  transfers between devices with their start and end apart: 48 -> 51, of which waited for: 28 -> 28; matrix products, arithmetic and copies ran while one was open for 0% -> 1% of each run, Pallas kernels for 11% -> 11%
where the time goes in v4:
time: 183 us; the launch traced here: 180 us
  waiting for transfers between devices  84.8 us (46%)
  starting transfers between devices  56.9 us (31%)
  Pallas kernels  29.7 us (16%)
  local copies, waits for them, and re-layouts  6.78 us (4%)
    ppermute x24, waiting for transfers between devices, over_row(): return lax.ppermute(value, 'row', [(i, i ^ k) for i in range(n_row)])  70.4 us
    ppermute x24, starting transfers between devices, over_row(): return lax.ppermute(value, 'row', [(i, i ^ k) for i in range(n_row)])  37.3 us
    pallas_call x20, Pallas kernels, call(): pl.pallas_call(kernel, out_shape=list(outs), in_specs=[smem] * scalars +...  29.7 us
    ppermute x27, starting transfers between devices, over_plane(): return lax.ppermute(value, PLANE, [(i, i ^ k) for i in range(n_plane)])  19.6 us
    ppermute x27, waiting for transfers between devices, over_plane(): return lax.ppermute(value, PLANE, [(i, i ^ k) for i in range(n_plane)])  14.4 us
    unnamed x66, local copies, waits for them, and re-layouts  6.06 us
  transfers between devices with their start and end apart: 51, of which 28 were waited for; matrix products, arithmetic and copies ran while one was open for 1% of the time, Pallas kernels for 11%

profile of v4, /device:TPU:0, one launch (start us, length us, event | category | flops | bytes accessed | tf_op | source)
XLA Modules:
  0.0 180.3 jit_solution(6416336087786158195)
XLA Ops:
  0.7 2.8 %pack_kernel.1 = (bf16[1,128,1536]{2,1,0:T(8,128)(2,1)}, bf16[544,256]{1,0:T(8,128)(2,1)}, bf16[544,256]{1,0:T(8,128)(2,1)}, bf16[544,256]{1,0:T(8,128)(2,1)}, bf16[544,256]{1,0:T(8,128)(2,1)}) custom-call(f32[128,512]{1,0:T(8,128)} %rest_5_.4, f32[128,256]{1,0:T(8,128)} %rest_8_.2, f32[128,256]{1,0:T(8,128)} %rest_11_.2, f32[128,512]{1,0:T(8,128)} %rest_14_.1, ...), custom_call_target="tpu_custom_call" | custom-call | flops 1 | bytes 1 | tf_op jit(solution)/shard_map/pack_kernel/pallas_call | solution.py:57
  3.5 4.0 %collective-permute-start.5 = (bf16[1,128,1536]{2,1,0:T(8,128)(2,1)}, bf16[1,128,1536]{2,1,0:T(8,128)(2,1)S(1)}, u32[]{:S(2)}, u32[]{:S(2)}) collective-permute-start(bf16[1,128,1536]{2,1,0:T(8,128)(2,1)} %get-tuple-element.130.rest_4_), channel_id=1, source_target_pairs={{0,18},{1,19},{2,16},{3,17},{16,2},{17,3},{18,0},{19,1},{4,22},{5,... | collective-permute-start | bytes 1179656 | tf_op jit(solution)/shard_map/ppermute | solution.py:515
  9.1 2.6 %collective-permute-start.1 = (bf16[544,256]{1,0:T(8,128)(2,1)}, bf16[544,256]{1,0:T(8,128)(2,1)S(1)}, u32[]{:S(2)}, u32[]{:S(2)}) collective-permute-start(bf16[544,256]{1,0:T(8,128)(2,1)} %get-tuple-element.128), channel_id=1, source_target_pairs={{0,8},{4,12},{8,0},{12,4},{1,9},{5,13},{9,1},{13,5},{2,10},{6,14},... | collective-permute-start | bytes 835592 | tf_op jit(solution)/shard_map/ppermute | solution.py:512
  17.7 4.0 %collective-permute-done.rest_1_ = bf16[544,256]{1,0:T(8,128)(2,1)S(1)} collective-permute-done((bf16[544,256]{1,0:T(8,128)(2,1)}, bf16[544,256]{1,0:T(8,128)(2,1)S(1)}, u32[]{:S(2)}, u32[]{:S(2)}) %collective-permute-start) | collective-permute-done | bytes 278560 | tf_op jit(solution)/shard_map/ppermute | solution.py:512
  24.0 2.5 %collective-permute-start.2 = (bf16[544,256]{1,0:T(8,128)(2,1)}, bf16[544,256]{1,0:T(8,128)(2,1)S(1)}, u32[]{:S(2)}, u32[]{:S(2)}) collective-permute-start(bf16[544,256]{1,0:T(8,128)(2,1)} %get-tuple-element.129), channel_id=1, source_target_pairs={{0,12},{4,8},{8,4},{12,0},{1,13},{5,9},{9,5},{13,1},{2,14},{6,10},... | collective-permute-start | bytes 835592 | tf_op jit(solution)/shard_map/ppermute | solution.py:512
  27.8 5.1 %collective-permute-done.2.rest_3_ = bf16[544,256]{1,0:T(8,128)(2,1)S(1)} collective-permute-done((bf16[544,256]{1,0:T(8,128)(2,1)}, bf16[544,256]{1,0:T(8,128)(2,1)S(1)}, u32[]{:S(2)}, u32[]{:S(2)}) %collective-permute-start.2) | collective-permute-done | bytes 278560 | tf_op jit(solution)/shard_map/ppermute | solution.py:512
  40.5 3.7 %attend_kernel.1 = (bf16[256,512]{1,0:T(8,128)(2,1)S(1)}, f32[1024,256]{1,0:T(8,128)S(1)}, bf16[256,512]{1,0:T(8,128)(2,1)S(1)}, bf16[256,256]{1,0:T(8,128)(2,1)...) custom-call(s32[9]{0:T(128)S(1)} %pad_add_fusion.place, ...), custom_call_target="tpu_custom_call" | custom-call | flops 1 | bytes 1 | tf_op jit(solution)/shard_map/attend_kernel/pallas_call | solution.py:57
  45.3 5.0 %collective-permute-start.10 = (bf16[64,1024]{1,0:T(8,128)(2,1)S(1)}, bf16[64,1024]{1,0:T(8,128)(2,1)S(1)}, u32[]{:S(2)}, u32[]{:S(2)}) collective-permute-start(bf16[64,1024]{1,0:T(8,128)(2,1)S(1)} %get-tuple-element.139), channel_id=1, source_target_pairs={{0,4},{4,0},{8,12},{12,8},{1,5},{5,1},{9,13},{13,9},{2,6},{6,2},{1... | collective-permute-start | bytes 393224 | tf_op jit(solution)/shard_map/ppermute | solution.py:512
  50.3 4.3 %collective-permute-done.10.rest_1_ = bf16[64,1024]{1,0:T(8,128)(2,1)S(1)} collective-permute-done((bf16[64,1024]{1,0:T(8,128)(2,1)S(1)}, bf16[64,1024]{1,0:T(8,128)(2,1)S(1)}, u32[]{:S(2)}, u32[]{:S(2)}) %collective-permute-start.10) | collective-permute-done | bytes 131104 | tf_op jit(solution)/shard_map/ppermute | solution.py:512
  54.6 5.1 %collective-permute-done.11.rest_2_ = bf16[64,1024]{1,0:T(8,128)(2,1)S(1)} collective-permute-done((bf16[64,1024]{1,0:T(8,128)(2,1)S(1)}, bf16[64,1024]{1,0:T(8,128)(2,1)S(1)}, u32[]{:S(2)}, u32[]{:S(2)}) %collective-permute-start.11) | collective-permute-done | bytes 131104 | tf_op jit(solution)/shard_map/ppermute | solution.py:512
  66.9 2.8 %collective-permute-done.18.rest_7_ = bf16[64,1024]{1,0:T(8,128)(2,1)S(1)} collective-permute-done((bf16[64,1024]{1,0:T(8,128)(2,1)S(1)}, bf16[64,1024]{1,0:T(8,128)(2,1)S(1)}, u32[]{:S(2)}, u32[]{:S(2)}) %collective-permute-start.18) | collective-permute-done | bytes 131104 | tf_op jit(solution)/shard_map/ppermute | solution.py:512
  69.7 4.1 %collective-permute-done.17.rest_6_ = bf16[64,1024]{1,0:T(8,128)(2,1)S(1)} collective-permute-done((bf16[64,1024]{1,0:T(8,128)(2,1)S(1)}, bf16[64,1024]{1,0:T(8,128)(2,1)S(1)}, u32[]{:S(2)}, u32[]{:S(2)}) %collective-permute-start.17) | collective-permute-done | bytes 131104 | tf_op jit(solution)/shard_map/ppermute | solution.py:512
  75.4 2.8 %collective-permute-start.20 = (bf16[256,256]{1,0:T(8,128)(2,1)S(1)}, bf16[256,256]{1,0:T(8,128)(2,1)S(1)}, u32[]{:S(2)}, u32[]{:S(2)}) collective-permute-start(bf16[256,256]{1,0:T(8,128)(2,1)S(1)} %copy-done.22), channel_id=1, source_target_pairs={{0,4},{4,0},{8,12},{12,8},{1,5},{5,1},{9,13},{13,9},{2,6},{6,2},{1... | collective-permute-start | bytes 393224 | tf_op jit(solution)/shard_map/ppermute | solution.py:512
  78.2 3.9 %collective-permute-done.22.rest_3_ = bf16[256,256]{1,0:T(8,128)(2,1)S(1)} collective-permute-done((bf16[256,256]{1,0:T(8,128)(2,1)S(1)}, bf16[256,256]{1,0:T(8,128)(2,1)S(1)}, u32[]{:S(2)}, u32[]{:S(2)}) %collective-permute-start.22) | collective-permute-done | bytes 131104 | tf_op jit(solution)/shard_map/ppermute | solution.py:512
  82.0 5.1 %collective-permute-done.21.rest_2_ = bf16[256,256]{1,0:T(8,128)(2,1)S(1)} collective-permute-done((bf16[256,256]{1,0:T(8,128)(2,1)S(1)}, bf16[256,256]{1,0:T(8,128)(2,1)S(1)}, u32[]{:S(2)}, u32[]{:S(2)}) %collective-permute-start.21) | collective-permute-done | bytes 131104 | tf_op jit(solution)/shard_map/ppermute | solution.py:512
  87.1 3.8 %units_kernel.1 = (f32[64,1024]{1,0:T(8,128)S(1)}, bf16[64,1024]{1,0:T(8,128)(2,1)S(1)}, bf16[64,1024]{1,0:T(8,128)(2,1)S(1)}, bf16[64,1024]{1,0:T(8,128)(2,1)S(...) custom-call(s32[9]{0:T(128)S(1)} %pad_add_fusion.place, ...), custom_call_target="tpu_custom_call" | custom-call | flops 1 | bytes 1 | tf_op jit(solution)/shard_map/units_kernel/pallas_call | solution.py:57
  97.5 2.9 %collective-permute-done.24.rest_1_ = bf16[64,1024]{1,0:T(8,128)(2,1)S(1)} collective-permute-done((bf16[64,1024]{1,0:T(8,128)(2,1)S(1)}, bf16[64,1024]{1,0:T(8,128)(2,1)S(1)}, u32[]{:S(2)}, u32[]{:S(2)}) %collective-permute-start.24) | collective-permute-done | bytes 131104 | tf_op jit(solution)/shard_map/ppermute | solution.py:512
  100.4 5.1 %collective-permute-done.25.rest_2_ = bf16[64,1024]{1,0:T(8,128)(2,1)S(1)} collective-permute-done((bf16[64,1024]{1,0:T(8,128)(2,1)S(1)}, bf16[64,1024]{1,0:T(8,128)(2,1)S(1)}, u32[]{:S(2)}, u32[]{:S(2)}) %collective-permute-start.25) | collective-permute-done | bytes 131104 | tf_op jit(solution)/shard_map/ppermute | solution.py:512
  114.2 6.7 %collective-permute-done.28.rest_2_ = bf16[64,1024]{1,0:T(8,128)(2,1)S(1)} collective-permute-done((bf16[64,1024]{1,0:T(8,128)(2,1)S(1)}, bf16[64,1024]{1,0:T(8,128)(2,1)S(1)}, u32[]{:S(2)}, u32[]{:S(2)}) %collective-permute-start.28) | collective-permute-done | bytes 131104 | tf_op jit(solution)/shard_map/ppermute | solution.py:512
  125.1 4.3 %collective-permute-done.36.rest_9_ = bf16[256,256]{1,0:T(8,128)(2,1)S(1)} collective-permute-done((bf16[256,256]{1,0:T(8,128)(2,1)S(1)}, bf16[256,256]{1,0:T(8,128)(2,1)S(1)}, u32[]{:S(2)}, u32[]{:S(2)}) %collective-permute-start.36) | collective-permute-done | bytes 131104 | tf_op jit(solution)/shard_map/ppermute | solution.py:512
  130.8 3.1 %attend_back_kernel.1 = (bf16[256,1024]{1,0:T(8,128)(2,1)S(1)}, f32[1,128]{1,0:T(1,128)S(1)}, f32[1,128]{1,0:T(1,128)S(1)}, bf16[256,1024]{1,0:T(8,128)(2,1)S(1)}) custom-call(s32[9]{0:T(128)S(1)} %pad_add_fusion.place, bf16[64,1024]{1,0:T(8,128)(2,1)S(1)} %get-tuple-element.158.rest_0_, bf16[64,1024]{1,0:T(8,128)(2,1)S(1)} %collective-permute-done.27.rest_1_, ...), custom_call_target="tpu_custom_call" | custom-call | flops 1 | bytes 1 | tf_op jit(solution)/shard_map/attend_back_kernel/pallas_call | solution.py:57
  156.8 4.1 %collective-permute-done.45.rest_3_ = bf16[1,128,768]{2,1,0:T(8,128)(2,1)S(1)} collective-permute-done((bf16[1,128,768]{2,1,0:T(8,128)(2,1)S(1)}, bf16[1,128,768]{2,1,0:T(8,128)(2,1)S(1)}, u32[]{:S(2)}, u32[]{:S(2)}) %collective-permute-start.45) | collective-permute-done | bytes 196640 | tf_op jit(solution)/shard_map/ppermute | solution.py:515
  163.3 8.3 %collective-permute-done.34.rest_6_.rest_2_ = bf16[560,256]{1,0:T(8,128)(2,1)S(1)} collective-permute-done((bf16[560,256]{1,0:T(8,128)(2,1)S(1)}, bf16[560,256]{1,0:T(8,128)(2,1)S(1)}, u32[]{:S(2)}, u32[]{:S(2)}) %collective-permute-start.34) | collective-permute-done | bytes 286752 | tf_op jit(solution)/shard_map/ppermute | solution.py:512
  176.7 2.9 %units_update_kernel.1 = (f32[256,384]{1,0:T(8,128)}, f32[256,384]{1,0:T(8,128)}, f32[256,384]{1,0:T(8,128)}, f32[256,384]{1,0:T(8,128)}, f32[256,384]{1,0:T(8,1...) custom-call(s32[9]{0:T(128)S(1)} %pad_add_fusion.place, ...), custom_call_target="tpu_custom_call" | custom-call | flops 1 | bytes 1 | tf_op jit(solution)/shard_map/units_update_kernel/pallas_call | solution.py:57
  (172 shorter events, 80.4 us)
Async XLA Ops:
  3.5 14.2 %collective-permute-start.5 = (bf16[1,128,1536]{2,1,0:T(8,128)(2,1)}, bf16[1,128,1536]{2,1,0:T(8,128)(2,1)S(1)}, u32[]{:S(2)}, u32[]{:S(2)}) collective-permute-start(bf16[1,128,1536]{2,1,0:T(8,128)(2,1)} %get-tuple-element.130.rest_4_), channel_id=1, source_target_pairs={{0,18},{1,19},{2,16},{3,17},{16,2},{17,3},{18,0},{19,1},{4,22},{5,... | collective-permute-start | bytes 1179656 | tf_op jit(solution)/shard_map/ppermute | solution.py:515
  7.5 14.2 %collective-permute-start = (bf16[544,256]{1,0:T(8,128)(2,1)}, bf16[544,256]{1,0:T(8,128)(2,1)S(1)}, u32[]{:S(2)}, u32[]{:S(2)}) collective-permute-start(bf16[544,256]{1,0:T(8,128)(2,1)} %get-tuple-element.127), channel_id=1, source_target_pairs={{0,4},{4,0},{8,12},{12,8},{1,5},{5,1},{9,13},{13,9},{2,6},{6,2},{1... | collective-permute-start | bytes 835592 | tf_op jit(solution)/shard_map/ppermute | solution.py:512
  9.1 15.0 %collective-permute-start.1 = (bf16[544,256]{1,0:T(8,128)(2,1)}, bf16[544,256]{1,0:T(8,128)(2,1)S(1)}, u32[]{:S(2)}, u32[]{:S(2)}) collective-permute-start(bf16[544,256]{1,0:T(8,128)(2,1)} %get-tuple-element.128), channel_id=1, source_target_pairs={{0,8},{4,12},{8,0},{12,4},{1,9},{5,13},{9,1},{13,5},{2,10},{6,14},... | collective-permute-start | bytes 835592 | tf_op jit(solution)/shard_map/ppermute | solution.py:512
  11.7 14.9 %collective-permute-start.4 = (bf16[1,128,1536]{2,1,0:T(8,128)(2,1)}, bf16[1,128,1536]{2,1,0:T(8,128)(2,1)S(1)}, u32[]{:S(2)}, u32[]{:S(2)}) collective-permute-start(bf16[1,128,1536]{2,1,0:T(8,128)(2,1)} %get-tuple-element.130.rest_4_), channel_id=1, source_target_pairs={{0,16},{1,17},{2,18},{3,19},{16,0},{17,1},{18,2},{19,3},{4,20},{5,... | collective-permute-start | bytes 1179656 | tf_op jit(solution)/shard_map/ppermute | solution.py:515
  12.2 14.4 %collective-permute-start.3 = (bf16[1,128,1536]{2,1,0:T(8,128)(2,1)}, bf16[1,128,1536]{2,1,0:T(8,128)(2,1)S(1)}, u32[]{:S(2)}, u32[]{:S(2)}) collective-permute-start(bf16[1,128,1536]{2,1,0:T(8,128)(2,1)} %get-tuple-element.130.rest_4_), channel_id=1, source_target_pairs={{0,2},{1,3},{2,0},{3,1},{16,18},{17,19},{18,16},{19,17},{4,6},{5,7... | collective-permute-start | bytes 1179656 | tf_op jit(solution)/shard_map/ppermute | solution.py:515
  17.7 16.7 %collective-permute-start.6 = (bf16[1,128,1536]{2,1,0:T(8,128)(2,1)}, bf16[1,128,1536]{2,1,0:T(8,128)(2,1)S(1)}, u32[]{:S(2)}, u32[]{:S(2)}) collective-permute-start(bf16[1,128,1536]{2,1,0:T(8,128)(2,1)} %get-tuple-element.130.rest_4_), channel_id=1, source_target_pairs={{0,1},{1,0},{2,3},{3,2},{16,17},{17,16},{18,19},{19,18},{4,5},{5,4... | collective-permute-start | bytes 1179656 | tf_op jit(solution)/shard_map/ppermute | solution.py:515
  21.7 14.3 %collective-permute-start.9 = (bf16[1,128,1536]{2,1,0:T(8,128)(2,1)S(1)}, bf16[1,128,1536]{2,1,0:T(8,128)(2,1)S(1)}, u32[]{:S(2)}, u32[]{:S(2)}) collective-permute-start(bf16[1,128,1536]{2,1,0:T(8,128)(2,1)S(1)} %collective-permute-done.5.rest_7_), channel_id=1, source_target_pairs={{0,1},{1,0},{2,3},{3,2},{16,17},{17,16},{18,19},{19,18},{4,5},{5,4... | collective-permute-start | bytes 1179656 | tf_op jit(solution)/shard_map/ppermute | solution.py:515
  26.5 11.0 %collective-permute-start.8 = (bf16[1,128,1536]{2,1,0:T(8,128)(2,1)S(1)}, bf16[1,128,1536]{2,1,0:T(8,128)(2,1)S(1)}, u32[]{:S(2)}, u32[]{:S(2)}) collective-permute-start(bf16[1,128,1536]{2,1,0:T(8,128)(2,1)S(1)} %collective-permute-done.4.rest_6_), channel_id=1, source_target_pairs={{0,1},{1,0},{2,3},{3,2},{16,17},{17,16},{18,19},{19,18},{4,5},{5,4... | collective-permute-start | bytes 1179656 | tf_op jit(solution)/shard_map/ppermute | solution.py:515
  26.5 11.0 %collective-permute-start.7 = (bf16[1,128,1536]{2,1,0:T(8,128)(2,1)S(1)}, bf16[1,128,1536]{2,1,0:T(8,128)(2,1)}, u32[]{:S(2)}, u32[]{:S(2)}) collective-permute-start(bf16[1,128,1536]{2,1,0:T(8,128)(2,1)S(1)} %collective-permute-done.3.rest_5_), channel_id=1, source_target_pairs={{0,1},{1,0},{2,3},{3,2},{16,17},{17,16},{18,19},{19,18},{4,5},{5,4... | collective-permute-start | bytes 1179656 | tf_op jit(solution)/shard_map/ppermute | solution.py:515
  33.9 31.4 %collective-permute-start.15 = (bf16[3,96,1024]{2,1,0:T(8,128)(2,1)S(1)}, bf16[3,96,1024]{2,1,0:T(8,128)(2,1)S(1)}, u32[]{:S(2)}, u32[]{:S(2)}) collective-permute-start(bf16[3,96,1024]{2,1,0:T(8,128)(2,1)S(1)} %join_kernel.1), channel_id=1, source_target_pairs={{0,18},{1,19},{2,16},{3,17},{16,2},{17,3},{18,0},{19,1},{4,22},{5,... | collective-permute-start | bytes 1769480 | tf_op jit(solution)/shard_map/ppermute | solution.py:515
  34.3 32.3 %collective-permute-start.14 = (bf16[3,96,1024]{2,1,0:T(8,128)(2,1)S(1)}, bf16[3,96,1024]{2,1,0:T(8,128)(2,1)S(1)}, u32[]{:S(2)}, u32[]{:S(2)}) collective-permute-start(bf16[3,96,1024]{2,1,0:T(8,128)(2,1)S(1)} %join_kernel.1), channel_id=1, source_target_pairs={{0,16},{1,17},{2,18},{3,19},{16,0},{17,1},{18,2},{19,3},{4,20},{5,... | collective-permute-start | bytes 1769480 | tf_op jit(solution)/shard_map/ppermute | solution.py:515
  36.0 30.7 %collective-permute-start.13 = (bf16[3,96,1024]{2,1,0:T(8,128)(2,1)S(1)}, bf16[3,96,1024]{2,1,0:T(8,128)(2,1)S(1)}, u32[]{:S(2)}, u32[]{:S(2)}) collective-permute-start(bf16[3,96,1024]{2,1,0:T(8,128)(2,1)S(1)} %join_kernel.1), channel_id=1, source_target_pairs={{0,2},{1,3},{2,0},{3,1},{16,18},{17,19},{18,16},{19,17},{4,6},{5,7... | collective-permute-start | bytes 1769480 | tf_op jit(solution)/shard_map/ppermute | solution.py:515
  73.7 13.4 %collective-permute-start.19 = (bf16[3,384,1024]{2,1,0:T(8,128)(2,1)S(1)}, bf16[3,384,1024]{2,1,0:T(8,128)(2,1)S(1)}, u32[]{:S(2)}, u32[]{:S(2)}) collective-permute-start(bf16[3,384,1024]{2,1,0:T(8,128)(2,1)S(1)} %pad_maximum_fusion.wz_ref), channel_id=1, source_target_pairs={{0,1},{1,0},{2,3},{3,2},{16,17},{17,16},{18,19},{19,18},{4,5},{5,4... | collective-permute-start | bytes 7077896 | tf_op jit(solution)/shard_map/ppermute | solution.py:515
  75.4 11.7 %collective-permute-start.21 = (bf16[256,256]{1,0:T(8,128)(2,1)S(1)}, bf16[256,256]{1,0:T(8,128)(2,1)S(1)}, u32[]{:S(2)}, u32[]{:S(2)}) collective-permute-start(bf16[256,256]{1,0:T(8,128)(2,1)S(1)} %copy-done.22), channel_id=1, source_target_pairs={{0,8},{4,12},{8,0},{12,4},{1,9},{5,13},{9,1},{13,5},{2,10},{6,14},... | collective-permute-start | bytes 393224 | tf_op jit(solution)/shard_map/ppermute | solution.py:512
  75.4 11.7 %collective-permute-start.20 = (bf16[256,256]{1,0:T(8,128)(2,1)S(1)}, bf16[256,256]{1,0:T(8,128)(2,1)S(1)}, u32[]{:S(2)}, u32[]{:S(2)}) collective-permute-start(bf16[256,256]{1,0:T(8,128)(2,1)S(1)} %copy-done.22), channel_id=1, source_target_pairs={{0,4},{4,0},{8,12},{12,8},{1,5},{5,1},{9,13},{13,9},{2,6},{6,2},{1... | collective-permute-start | bytes 393224 | tf_op jit(solution)/shard_map/ppermute | solution.py:512
  92.5 12.9 %collective-permute-start.25 = (bf16[64,1024]{1,0:T(8,128)(2,1)S(1)}, bf16[64,1024]{1,0:T(8,128)(2,1)S(1)}, u32[]{:S(2)}, u32[]{:S(2)}) collective-permute-start(bf16[64,1024]{1,0:T(8,128)(2,1)S(1)} %get-tuple-element.156), channel_id=1, source_target_pairs={{0,8},{4,12},{8,0},{12,4},{1,9},{5,13},{9,1},{13,5},{2,10},{6,14},... | collective-permute-start | bytes 393224 | tf_op jit(solution)/shard_map/ppermute | solution.py:512
  108.3 12.6 %collective-permute-start.28 = (bf16[64,1024]{1,0:T(8,128)(2,1)S(1)}, bf16[64,1024]{1,0:T(8,128)(2,1)S(1)}, u32[]{:S(2)}, u32[]{:S(2)}) collective-permute-start(bf16[64,1024]{1,0:T(8,128)(2,1)S(1)} %get-tuple-element.158.rest_0_), channel_id=1, source_target_pairs={{0,8},{4,12},{8,0},{12,4},{1,9},{5,13},{9,1},{13,5},{2,10},{6,14},... | collective-permute-start | bytes 393224 | tf_op jit(solution)/shard_map/ppermute | solution.py:512
  110.7 25.6 %collective-permute-start.30 = (bf16[3,96,1024]{2,1,0:T(8,128)(2,1)S(1)}, bf16[3,96,1024]{2,1,0:T(8,128)(2,1)S(1)}, u32[]{:S(2)}, u32[]{:S(2)}) collective-permute-start(bf16[3,96,1024]{2,1,0:T(8,128)(2,1)S(1)} %get-tuple-element.166), channel_id=1, source_target_pairs={{0,2},{1,3},{2,0},{3,1},{16,18},{17,19},{18,16},{19,17},{4,6},{5,7... | collective-permute-start | bytes 1769480 | tf_op jit(solution)/shard_map/ppermute | solution.py:515
  111.2 26.5 %collective-permute-start.31 = (bf16[3,96,1024]{2,1,0:T(8,128)(2,1)S(1)}, bf16[3,96,1024]{2,1,0:T(8,128)(2,1)S(1)}, u32[]{:S(2)}, u32[]{:S(2)}) collective-permute-start(bf16[3,96,1024]{2,1,0:T(8,128)(2,1)S(1)} %get-tuple-element.168), channel_id=1, source_target_pairs={{0,16},{1,17},{2,18},{3,19},{16,0},{17,1},{18,2},{19,3},{4,20},{5,... | collective-permute-start | bytes 1769480 | tf_op jit(solution)/shard_map/ppermute | solution.py:515
  120.9 16.8 %collective-permute-start.32 = (bf16[3,96,1024]{2,1,0:T(8,128)(2,1)S(1)}, bf16[3,96,1024]{2,1,0:T(8,128)(2,1)S(1)}, u32[]{:S(2)}, u32[]{:S(2)}) collective-permute-start(bf16[3,96,1024]{2,1,0:T(8,128)(2,1)S(1)} %get-tuple-element.170), channel_id=1, source_target_pairs={{0,18},{1,19},{2,16},{3,17},{16,2},{17,3},{18,0},{19,1},{4,22},{5,... | collective-permute-start | bytes 1769480 | tf_op jit(solution)/shard_map/ppermute | solution.py:515
  142.5 11.2 %collective-permute-start.43 = (bf16[2,128,768]{2,1,0:T(8,128)(2,1)S(1)}, bf16[2,128,768]{2,1,0:T(8,128)(2,1)S(1)}, u32[]{:S(2)}, u32[]{:S(2)}) collective-permute-start(bf16[2,128,768]{2,1,0:T(8,128)(2,1)S(1)} %get-tuple-element.197), channel_id=1, source_target_pairs={{0,2},{1,3},{2,0},{3,1},{16,18},{17,19},{18,16},{19,17},{4,6},{5,7... | collective-permute-start | bytes 1179656 | tf_op jit(solution)/shard_map/ppermute | solution.py:515
  146.9 16.5 %collective-permute-start.33 = (bf16[560,256]{1,0:T(8,128)(2,1)S(1)}, bf16[560,256]{1,0:T(8,128)(2,1)S(1)}, u32[]{:S(2)}, u32[]{:S(2)}) collective-permute-start(bf16[560,256]{1,0:T(8,128)(2,1)S(1)} %get-tuple-element.175), channel_id=1, source_target_pairs={{0,4},{4,0},{8,12},{12,8},{1,5},{5,1},{9,13},{13,9},{2,6},{6,2},{1... | collective-permute-start | bytes 860168 | tf_op jit(solution)/shard_map/ppermute | solution.py:512
  148.6 23.0 %collective-permute-start.34 = (bf16[560,256]{1,0:T(8,128)(2,1)S(1)}, bf16[560,256]{1,0:T(8,128)(2,1)S(1)}, u32[]{:S(2)}, u32[]{:S(2)}) collective-permute-start(bf16[560,256]{1,0:T(8,128)(2,1)S(1)} %get-tuple-element.176), channel_id=1, source_target_pairs={{0,8},{4,12},{8,0},{12,4},{1,9},{5,13},{9,1},{13,5},{2,10},{6,14},... | collective-permute-start | bytes 860168 | tf_op jit(solution)/shard_map/ppermute | solution.py:512
  149.0 22.6 %collective-permute-start.35 = (bf16[560,256]{1,0:T(8,128)(2,1)S(1)}, bf16[560,256]{1,0:T(8,128)(2,1)S(1)}, u32[]{:S(2)}, u32[]{:S(2)}) collective-permute-start(bf16[560,256]{1,0:T(8,128)(2,1)S(1)} %get-tuple-element.177), channel_id=1, source_target_pairs={{0,12},{4,8},{8,4},{12,0},{1,13},{5,9},{9,5},{13,1},{2,14},{6,10},... | collective-permute-start | bytes 860168 | tf_op jit(solution)/shard_map/ppermute | solution.py:512
  (60 other events, 578.9 us)

commit v5 on v4

--- a/solution.py
+++ b/solution.py
@@ -78,11 +78,9 @@
 def adamw(weight, first, second, grad, rate, decay):
     first_new = BETA_FIRST * first + (1.0 - BETA_FIRST) * grad
     second_new = BETA_SECOND * second + (1.0 - BETA_SECOND) * grad * grad
-    first_hat = first_new * (1.0 / (1.0 - BETA_FIRST**STEP))
-    second_hat = second_new * (1.0 / (1.0 - BETA_SECOND**STEP))
-    weight_new = weight - rate * (
-        first_hat / (jnp.sqrt(second_hat) + ADAM_EPSILON) + decay * weight
-    )
+    step = first_new * (rate / (1.0 - BETA_FIRST**STEP))
+    scale = jnp.sqrt(second_new * (1.0 / (1.0 - BETA_SECOND**STEP))) + ADAM_EPSILON
+    weight_new = weight * (1.0 - rate * decay) - step / scale
     return (weight_new, first_new, second_new)
 
 

time: 183 us -> 183 us (level)
  no operation moved by 1% of the time
where the time goes in v5:
time: 183 us; the launch traced here: 180 us
  waiting for transfers between devices  84.7 us (46%)
  starting transfers between devices  56.9 us (31%)
  Pallas kernels  29.7 us (16%)
  local copies, waits for them, and re-layouts  6.78 us (4%)
    ppermute x24, waiting for transfers between devices, over_row(): return lax.ppermute(value, 'row', [(i, i ^ k) for i in range(n_row)])  70.3 us
    ppermute x24, starting transfers between devices, over_row(): return lax.ppermute(value, 'row', [(i, i ^ k) for i in range(n_row)])  37.3 us
    pallas_call x20, Pallas kernels, call(): pl.pallas_call(kernel, out_shape=list(outs), in_specs=[smem] * scalars +...  29.7 us
    ppermute x27, starting transfers between devices, over_plane(): return lax.ppermute(value, PLANE, [(i, i ^ k) for i in range(n_plane)])  19.6 us
    ppermute x27, waiting for transfers between devices, over_plane(): return lax.ppermute(value, PLANE, [(i, i ^ k) for i in range(n_plane)])  14.4 us
    unnamed x66, local copies, waits for them, and re-layouts  6.06 us
  transfers between devices with their start and end apart: 51, of which 28 were waited for; matrix products, arithmetic and copies ran while one was open for 1% of the time, Pallas kernels for 11%

profile of v5, /device:TPU:0, one launch (start us, length us, event | category | flops | bytes accessed | tf_op | source)
XLA Modules:
  0.0 180.3 jit_solution(12708260408068902392)
XLA Ops:
  0.7 2.8 %pack_kernel.1 = (bf16[1,128,1536]{2,1,0:T(8,128)(2,1)}, bf16[544,256]{1,0:T(8,128)(2,1)}, bf16[544,256]{1,0:T(8,128)(2,1)}, bf16[544,256]{1,0:T(8,128)(2,1)}, bf16[544,256]{1,0:T(8,128)(2,1)}) custom-call(f32[128,512]{1,0:T(8,128)} %rest_5_.4, f32[128,256]{1,0:T(8,128)} %rest_8_.2, f32[128,256]{1,0:T(8,128)} %rest_11_.2, f32[128,512]{1,0:T(8,128)} %rest_14_.1, ...), custom_call_target="tpu_custom_call" | custom-call | flops 1 | bytes 1 | tf_op jit(solution)/shard_map/pack_kernel/pallas_call | solution.py:57
  3.5 4.0 %collective-permute-start.5 = (bf16[1,128,1536]{2,1,0:T(8,128)(2,1)}, bf16[1,128,1536]{2,1,0:T(8,128)(2,1)S(1)}, u32[]{:S(2)}, u32[]{:S(2)}) collective-permute-start(bf16[1,128,1536]{2,1,0:T(8,128)(2,1)} %get-tuple-element.130.rest_4_), channel_id=1, source_target_pairs={{0,18},{1,19},{2,16},{3,17},{16,2},{17,3},{18,0},{19,1},{4,22},{5,... | collective-permute-start | bytes 1179656 | tf_op jit(solution)/shard_map/ppermute | solution.py:513
  9.1 2.6 %collective-permute-start.1 = (bf16[544,256]{1,0:T(8,128)(2,1)}, bf16[544,256]{1,0:T(8,128)(2,1)S(1)}, u32[]{:S(2)}, u32[]{:S(2)}) collective-permute-start(bf16[544,256]{1,0:T(8,128)(2,1)} %get-tuple-element.128), channel_id=1, source_target_pairs={{0,8},{4,12},{8,0},{12,4},{1,9},{5,13},{9,1},{13,5},{2,10},{6,14},... | collective-permute-start | bytes 835592 | tf_op jit(solution)/shard_map/ppermute | solution.py:510
  17.7 4.0 %collective-permute-done.rest_1_ = bf16[544,256]{1,0:T(8,128)(2,1)S(1)} collective-permute-done((bf16[544,256]{1,0:T(8,128)(2,1)}, bf16[544,256]{1,0:T(8,128)(2,1)S(1)}, u32[]{:S(2)}, u32[]{:S(2)}) %collective-permute-start) | collective-permute-done | bytes 278560 | tf_op jit(solution)/shard_map/ppermute | solution.py:510
  24.0 2.5 %collective-permute-start.2 = (bf16[544,256]{1,0:T(8,128)(2,1)}, bf16[544,256]{1,0:T(8,128)(2,1)S(1)}, u32[]{:S(2)}, u32[]{:S(2)}) collective-permute-start(bf16[544,256]{1,0:T(8,128)(2,1)} %get-tuple-element.129), channel_id=1, source_target_pairs={{0,12},{4,8},{8,4},{12,0},{1,13},{5,9},{9,5},{13,1},{2,14},{6,10},... | collective-permute-start | bytes 835592 | tf_op jit(solution)/shard_map/ppermute | solution.py:510
  27.8 5.1 %collective-permute-done.2.rest_3_ = bf16[544,256]{1,0:T(8,128)(2,1)S(1)} collective-permute-done((bf16[544,256]{1,0:T(8,128)(2,1)}, bf16[544,256]{1,0:T(8,128)(2,1)S(1)}, u32[]{:S(2)}, u32[]{:S(2)}) %collective-permute-start.2) | collective-permute-done | bytes 278560 | tf_op jit(solution)/shard_map/ppermute | solution.py:510
  40.5 3.7 %attend_kernel.1 = (bf16[256,512]{1,0:T(8,128)(2,1)S(1)}, f32[1024,256]{1,0:T(8,128)S(1)}, bf16[256,512]{1,0:T(8,128)(2,1)S(1)}, bf16[256,256]{1,0:T(8,128)(2,1)...) custom-call(s32[9]{0:T(128)S(1)} %pad_add_fusion.place, ...), custom_call_target="tpu_custom_call" | custom-call | flops 1 | bytes 1 | tf_op jit(solution)/shard_map/attend_kernel/pallas_call | solution.py:57
  45.3 5.0 %collective-permute-start.10 = (bf16[64,1024]{1,0:T(8,128)(2,1)S(1)}, bf16[64,1024]{1,0:T(8,128)(2,1)S(1)}, u32[]{:S(2)}, u32[]{:S(2)}) collective-permute-start(bf16[64,1024]{1,0:T(8,128)(2,1)S(1)} %get-tuple-element.139), channel_id=1, source_target_pairs={{0,4},{4,0},{8,12},{12,8},{1,5},{5,1},{9,13},{13,9},{2,6},{6,2},{1... | collective-permute-start | bytes 393224 | tf_op jit(solution)/shard_map/ppermute | solution.py:510
  50.3 4.3 %collective-permute-done.10.rest_1_ = bf16[64,1024]{1,0:T(8,128)(2,1)S(1)} collective-permute-done((bf16[64,1024]{1,0:T(8,128)(2,1)S(1)}, bf16[64,1024]{1,0:T(8,128)(2,1)S(1)}, u32[]{:S(2)}, u32[]{:S(2)}) %collective-permute-start.10) | collective-permute-done | bytes 131104 | tf_op jit(solution)/shard_map/ppermute | solution.py:510
  54.6 5.1 %collective-permute-done.11.rest_2_ = bf16[64,1024]{1,0:T(8,128)(2,1)S(1)} collective-permute-done((bf16[64,1024]{1,0:T(8,128)(2,1)S(1)}, bf16[64,1024]{1,0:T(8,128)(2,1)S(1)}, u32[]{:S(2)}, u32[]{:S(2)}) %collective-permute-start.11) | collective-permute-done | bytes 131104 | tf_op jit(solution)/shard_map/ppermute | solution.py:510
  66.9 2.8 %collective-permute-done.18.rest_7_ = bf16[64,1024]{1,0:T(8,128)(2,1)S(1)} collective-permute-done((bf16[64,1024]{1,0:T(8,128)(2,1)S(1)}, bf16[64,1024]{1,0:T(8,128)(2,1)S(1)}, u32[]{:S(2)}, u32[]{:S(2)}) %collective-permute-start.18) | collective-permute-done | bytes 131104 | tf_op jit(solution)/shard_map/ppermute | solution.py:510
  69.7 4.1 %collective-permute-done.17.rest_6_ = bf16[64,1024]{1,0:T(8,128)(2,1)S(1)} collective-permute-done((bf16[64,1024]{1,0:T(8,128)(2,1)S(1)}, bf16[64,1024]{1,0:T(8,128)(2,1)S(1)}, u32[]{:S(2)}, u32[]{:S(2)}) %collective-permute-start.17) | collective-permute-done | bytes 131104 | tf_op jit(solution)/shard_map/ppermute | solution.py:510
  75.4 2.8 %collective-permute-start.20 = (bf16[256,256]{1,0:T(8,128)(2,1)S(1)}, bf16[256,256]{1,0:T(8,128)(2,1)S(1)}, u32[]{:S(2)}, u32[]{:S(2)}) collective-permute-start(bf16[256,256]{1,0:T(8,128)(2,1)S(1)} %copy-done.22), channel_id=1, source_target_pairs={{0,4},{4,0},{8,12},{12,8},{1,5},{5,1},{9,13},{13,9},{2,6},{6,2},{1... | collective-permute-start | bytes 393224 | tf_op jit(solution)/shard_map/ppermute | solution.py:510
  78.2 3.9 %collective-permute-done.22.rest_3_ = bf16[256,256]{1,0:T(8,128)(2,1)S(1)} collective-permute-done((bf16[256,256]{1,0:T(8,128)(2,1)S(1)}, bf16[256,256]{1,0:T(8,128)(2,1)S(1)}, u32[]{:S(2)}, u32[]{:S(2)}) %collective-permute-start.22) | collective-permute-done | bytes 131104 | tf_op jit(solution)/shard_map/ppermute | solution.py:510
  82.0 5.1 %collective-permute-done.21.rest_2_ = bf16[256,256]{1,0:T(8,128)(2,1)S(1)} collective-permute-done((bf16[256,256]{1,0:T(8,128)(2,1)S(1)}, bf16[256,256]{1,0:T(8,128)(2,1)S(1)}, u32[]{:S(2)}, u32[]{:S(2)}) %collective-permute-start.21) | collective-permute-done | bytes 131104 | tf_op jit(solution)/shard_map/ppermute | solution.py:510
  87.1 3.8 %units_kernel.1 = (f32[64,1024]{1,0:T(8,128)S(1)}, bf16[64,1024]{1,0:T(8,128)(2,1)S(1)}, bf16[64,1024]{1,0:T(8,128)(2,1)S(1)}, bf16[64,1024]{1,0:T(8,128)(2,1)S(...) custom-call(s32[9]{0:T(128)S(1)} %pad_add_fusion.place, ...), custom_call_target="tpu_custom_call" | custom-call | flops 1 | bytes 1 | tf_op jit(solution)/shard_map/units_kernel/pallas_call | solution.py:57
  97.5 2.9 %collective-permute-done.24.rest_1_ = bf16[64,1024]{1,0:T(8,128)(2,1)S(1)} collective-permute-done((bf16[64,1024]{1,0:T(8,128)(2,1)S(1)}, bf16[64,1024]{1,0:T(8,128)(2,1)S(1)}, u32[]{:S(2)}, u32[]{:S(2)}) %collective-permute-start.24) | collective-permute-done | bytes 131104 | tf_op jit(solution)/shard_map/ppermute | solution.py:510
  100.4 5.1 %collective-permute-done.25.rest_2_ = bf16[64,1024]{1,0:T(8,128)(2,1)S(1)} collective-permute-done((bf16[64,1024]{1,0:T(8,128)(2,1)S(1)}, bf16[64,1024]{1,0:T(8,128)(2,1)S(1)}, u32[]{:S(2)}, u32[]{:S(2)}) %collective-permute-start.25) | collective-permute-done | bytes 131104 | tf_op jit(solution)/shard_map/ppermute | solution.py:510
  114.2 6.7 %collective-permute-done.28.rest_2_ = bf16[64,1024]{1,0:T(8,128)(2,1)S(1)} collective-permute-done((bf16[64,1024]{1,0:T(8,128)(2,1)S(1)}, bf16[64,1024]{1,0:T(8,128)(2,1)S(1)}, u32[]{:S(2)}, u32[]{:S(2)}) %collective-permute-start.28) | collective-permute-done | bytes 131104 | tf_op jit(solution)/shard_map/ppermute | solution.py:510
  125.1 4.3 %collective-permute-done.36.rest_9_ = bf16[256,256]{1,0:T(8,128)(2,1)S(1)} collective-permute-done((bf16[256,256]{1,0:T(8,128)(2,1)S(1)}, bf16[256,256]{1,0:T(8,128)(2,1)S(1)}, u32[]{:S(2)}, u32[]{:S(2)}) %collective-permute-start.36) | collective-permute-done | bytes 131104 | tf_op jit(solution)/shard_map/ppermute | solution.py:510
  130.8 3.1 %attend_back_kernel.1 = (bf16[256,1024]{1,0:T(8,128)(2,1)S(1)}, f32[1,128]{1,0:T(1,128)S(1)}, f32[1,128]{1,0:T(1,128)S(1)}, bf16[256,1024]{1,0:T(8,128)(2,1)S(1)}) custom-call(s32[9]{0:T(128)S(1)} %pad_add_fusion.place, bf16[64,1024]{1,0:T(8,128)(2,1)S(1)} %get-tuple-element.158.rest_0_, bf16[64,1024]{1,0:T(8,128)(2,1)S(1)} %collective-permute-done.27.rest_1_, ...), custom_call_target="tpu_custom_call" | custom-call | flops 1 | bytes 1 | tf_op jit(solution)/shard_map/attend_back_kernel/pallas_call | solution.py:57
  156.8 4.1 %collective-permute-done.45.rest_3_ = bf16[1,128,768]{2,1,0:T(8,128)(2,1)S(1)} collective-permute-done((bf16[1,128,768]{2,1,0:T(8,128)(2,1)S(1)}, bf16[1,128,768]{2,1,0:T(8,128)(2,1)S(1)}, u32[]{:S(2)}, u32[]{:S(2)}) %collective-permute-start.45) | collective-permute-done | bytes 196640 | tf_op jit(solution)/shard_map/ppermute | solution.py:513
  163.4 8.2 %collective-permute-done.34.rest_6_.rest_2_ = bf16[560,256]{1,0:T(8,128)(2,1)S(1)} collective-permute-done((bf16[560,256]{1,0:T(8,128)(2,1)S(1)}, bf16[560,256]{1,0:T(8,128)(2,1)S(1)}, u32[]{:S(2)}, u32[]{:S(2)}) %collective-permute-start.34) | collective-permute-done | bytes 286752 | tf_op jit(solution)/shard_map/ppermute | solution.py:510
  176.7 2.9 %units_update_kernel.1 = (f32[256,384]{1,0:T(8,128)}, f32[256,384]{1,0:T(8,128)}, f32[256,384]{1,0:T(8,128)}, f32[256,384]{1,0:T(8,128)}, f32[256,384]{1,0:T(8,1...) custom-call(s32[9]{0:T(128)S(1)} %pad_add_fusion.place, ...), custom_call_target="tpu_custom_call" | custom-call | flops 1 | bytes 1 | tf_op jit(solution)/shard_map/units_update_kernel/pallas_call | solution.py:57
  (172 shorter events, 80.5 us)
Async XLA Ops:
  3.5 14.2 %collective-permute-start.5 = (bf16[1,128,1536]{2,1,0:T(8,128)(2,1)}, bf16[1,128,1536]{2,1,0:T(8,128)(2,1)S(1)}, u32[]{:S(2)}, u32[]{:S(2)}) collective-permute-start(bf16[1,128,1536]{2,1,0:T(8,128)(2,1)} %get-tuple-element.130.rest_4_), channel_id=1, source_target_pairs={{0,18},{1,19},{2,16},{3,17},{16,2},{17,3},{18,0},{19,1},{4,22},{5,... | collective-permute-start | bytes 1179656 | tf_op jit(solution)/shard_map/ppermute | solution.py:513
  7.5 14.2 %collective-permute-start = (bf16[544,256]{1,0:T(8,128)(2,1)}, bf16[544,256]{1,0:T(8,128)(2,1)S(1)}, u32[]{:S(2)}, u32[]{:S(2)}) collective-permute-start(bf16[544,256]{1,0:T(8,128)(2,1)} %get-tuple-element.127), channel_id=1, source_target_pairs={{0,4},{4,0},{8,12},{12,8},{1,5},{5,1},{9,13},{13,9},{2,6},{6,2},{1... | collective-permute-start | bytes 835592 | tf_op jit(solution)/shard_map/ppermute | solution.py:510
  9.1 15.0 %collective-permute-start.1 = (bf16[544,256]{1,0:T(8,128)(2,1)}, bf16[544,256]{1,0:T(8,128)(2,1)S(1)}, u32[]{:S(2)}, u32[]{:S(2)}) collective-permute-start(bf16[544,256]{1,0:T(8,128)(2,1)} %get-tuple-element.128), channel_id=1, source_target_pairs={{0,8},{4,12},{8,0},{12,4},{1,9},{5,13},{9,1},{13,5},{2,10},{6,14},... | collective-permute-start | bytes 835592 | tf_op jit(solution)/shard_map/ppermute | solution.py:510
  11.7 14.9 %collective-permute-start.4 = (bf16[1,128,1536]{2,1,0:T(8,128)(2,1)}, bf16[1,128,1536]{2,1,0:T(8,128)(2,1)S(1)}, u32[]{:S(2)}, u32[]{:S(2)}) collective-permute-start(bf16[1,128,1536]{2,1,0:T(8,128)(2,1)} %get-tuple-element.130.rest_4_), channel_id=1, source_target_pairs={{0,16},{1,17},{2,18},{3,19},{16,0},{17,1},{18,2},{19,3},{4,20},{5,... | collective-permute-start | bytes 1179656 | tf_op jit(solution)/shard_map/ppermute | solution.py:513
  12.2 14.4 %collective-permute-start.3 = (bf16[1,128,1536]{2,1,0:T(8,128)(2,1)}, bf16[1,128,1536]{2,1,0:T(8,128)(2,1)S(1)}, u32[]{:S(2)}, u32[]{:S(2)}) collective-permute-start(bf16[1,128,1536]{2,1,0:T(8,128)(2,1)} %get-tuple-element.130.rest_4_), channel_id=1, source_target_pairs={{0,2},{1,3},{2,0},{3,1},{16,18},{17,19},{18,16},{19,17},{4,6},{5,7... | collective-permute-start | bytes 1179656 | tf_op jit(solution)/shard_map/ppermute | solution.py:513
  17.7 16.7 %collective-permute-start.6 = (bf16[1,128,1536]{2,1,0:T(8,128)(2,1)}, bf16[1,128,1536]{2,1,0:T(8,128)(2,1)S(1)}, u32[]{:S(2)}, u32[]{:S(2)}) collective-permute-start(bf16[1,128,1536]{2,1,0:T(8,128)(2,1)} %get-tuple-element.130.rest_4_), channel_id=1, source_target_pairs={{0,1},{1,0},{2,3},{3,2},{16,17},{17,16},{18,19},{19,18},{4,5},{5,4... | collective-permute-start | bytes 1179656 | tf_op jit(solution)/shard_map/ppermute | solution.py:513
  21.7 14.3 %collective-permute-start.9 = (bf16[1,128,1536]{2,1,0:T(8,128)(2,1)S(1)}, bf16[1,128,1536]{2,1,0:T(8,128)(2,1)S(1)}, u32[]{:S(2)}, u32[]{:S(2)}) collective-permute-start(bf16[1,128,1536]{2,1,0:T(8,128)(2,1)S(1)} %collective-permute-done.5.rest_7_), channel_id=1, source_target_pairs={{0,1},{1,0},{2,3},{3,2},{16,17},{17,16},{18,19},{19,18},{4,5},{5,4... | collective-permute-start | bytes 1179656 | tf_op jit(solution)/shard_map/ppermute | solution.py:513
  26.5 11.0 %collective-permute-start.8 = (bf16[1,128,1536]{2,1,0:T(8,128)(2,1)S(1)}, bf16[1,128,1536]{2,1,0:T(8,128)(2,1)S(1)}, u32[]{:S(2)}, u32[]{:S(2)}) collective-permute-start(bf16[1,128,1536]{2,1,0:T(8,128)(2,1)S(1)} %collective-permute-done.4.rest_6_), channel_id=1, source_target_pairs={{0,1},{1,0},{2,3},{3,2},{16,17},{17,16},{18,19},{19,18},{4,5},{5,4... | collective-permute-start | bytes 1179656 | tf_op jit(solution)/shard_map/ppermute | solution.py:513
  26.5 11.0 %collective-permute-start.7 = (bf16[1,128,1536]{2,1,0:T(8,128)(2,1)S(1)}, bf16[1,128,1536]{2,1,0:T(8,128)(2,1)}, u32[]{:S(2)}, u32[]{:S(2)}) collective-permute-start(bf16[1,128,1536]{2,1,0:T(8,128)(2,1)S(1)} %collective-permute-done.3.rest_5_), channel_id=1, source_target_pairs={{0,1},{1,0},{2,3},{3,2},{16,17},{17,16},{18,19},{19,18},{4,5},{5,4... | collective-permute-start | bytes 1179656 | tf_op jit(solution)/shard_map/ppermute | solution.py:513
  33.9 31.4 %collective-permute-start.15 = (bf16[3,96,1024]{2,1,0:T(8,128)(2,1)S(1)}, bf16[3,96,1024]{2,1,0:T(8,128)(2,1)S(1)}, u32[]{:S(2)}, u32[]{:S(2)}) collective-permute-start(bf16[3,96,1024]{2,1,0:T(8,128)(2,1)S(1)} %join_kernel.1), channel_id=1, source_target_pairs={{0,18},{1,19},{2,16},{3,17},{16,2},{17,3},{18,0},{19,1},{4,22},{5,... | collective-permute-start | bytes 1769480 | tf_op jit(solution)/shard_map/ppermute | solution.py:513
  34.3 32.3 %collective-permute-start.14 = (bf16[3,96,1024]{2,1,0:T(8,128)(2,1)S(1)}, bf16[3,96,1024]{2,1,0:T(8,128)(2,1)S(1)}, u32[]{:S(2)}, u32[]{:S(2)}) collective-permute-start(bf16[3,96,1024]{2,1,0:T(8,128)(2,1)S(1)} %join_kernel.1), channel_id=1, source_target_pairs={{0,16},{1,17},{2,18},{3,19},{16,0},{17,1},{18,2},{19,3},{4,20},{5,... | collective-permute-start | bytes 1769480 | tf_op jit(solution)/shard_map/ppermute | solution.py:513
  36.0 30.7 %collective-permute-start.13 = (bf16[3,96,1024]{2,1,0:T(8,128)(2,1)S(1)}, bf16[3,96,1024]{2,1,0:T(8,128)(2,1)S(1)}, u32[]{:S(2)}, u32[]{:S(2)}) collective-permute-start(bf16[3,96,1024]{2,1,0:T(8,128)(2,1)S(1)} %join_kernel.1), channel_id=1, source_target_pairs={{0,2},{1,3},{2,0},{3,1},{16,18},{17,19},{18,16},{19,17},{4,6},{5,7... | collective-permute-start | bytes 1769480 | tf_op jit(solution)/shard_map/ppermute | solution.py:513
  73.7 13.4 %collective-permute-start.19 = (bf16[3,384,1024]{2,1,0:T(8,128)(2,1)S(1)}, bf16[3,384,1024]{2,1,0:T(8,128)(2,1)S(1)}, u32[]{:S(2)}, u32[]{:S(2)}) collective-permute-start(bf16[3,384,1024]{2,1,0:T(8,128)(2,1)S(1)} %pad_maximum_fusion.wz_ref), channel_id=1, source_target_pairs={{0,1},{1,0},{2,3},{3,2},{16,17},{17,16},{18,19},{19,18},{4,5},{5,4... | collective-permute-start | bytes 7077896 | tf_op jit(solution)/shard_map/ppermute | solution.py:513
  75.4 11.7 %collective-permute-start.21 = (bf16[256,256]{1,0:T(8,128)(2,1)S(1)}, bf16[256,256]{1,0:T(8,128)(2,1)S(1)}, u32[]{:S(2)}, u32[]{:S(2)}) collective-permute-start(bf16[256,256]{1,0:T(8,128)(2,1)S(1)} %copy-done.22), channel_id=1, source_target_pairs={{0,8},{4,12},{8,0},{12,4},{1,9},{5,13},{9,1},{13,5},{2,10},{6,14},... | collective-permute-start | bytes 393224 | tf_op jit(solution)/shard_map/ppermute | solution.py:510
  75.4 11.7 %collective-permute-start.20 = (bf16[256,256]{1,0:T(8,128)(2,1)S(1)}, bf16[256,256]{1,0:T(8,128)(2,1)S(1)}, u32[]{:S(2)}, u32[]{:S(2)}) collective-permute-start(bf16[256,256]{1,0:T(8,128)(2,1)S(1)} %copy-done.22), channel_id=1, source_target_pairs={{0,4},{4,0},{8,12},{12,8},{1,5},{5,1},{9,13},{13,9},{2,6},{6,2},{1... | collective-permute-start | bytes 393224 | tf_op jit(solution)/shard_map/ppermute | solution.py:510
  92.5 12.9 %collective-permute-start.25 = (bf16[64,1024]{1,0:T(8,128)(2,1)S(1)}, bf16[64,1024]{1,0:T(8,128)(2,1)S(1)}, u32[]{:S(2)}, u32[]{:S(2)}) collective-permute-start(bf16[64,1024]{1,0:T(8,128)(2,1)S(1)} %get-tuple-element.156), channel_id=1, source_target_pairs={{0,8},{4,12},{8,0},{12,4},{1,9},{5,13},{9,1},{13,5},{2,10},{6,14},... | collective-permute-start | bytes 393224 | tf_op jit(solution)/shard_map/ppermute | solution.py:510
  108.3 12.6 %collective-permute-start.28 = (bf16[64,1024]{1,0:T(8,128)(2,1)S(1)}, bf16[64,1024]{1,0:T(8,128)(2,1)S(1)}, u32[]{:S(2)}, u32[]{:S(2)}) collective-permute-start(bf16[64,1024]{1,0:T(8,128)(2,1)S(1)} %get-tuple-element.158.rest_0_), channel_id=1, source_target_pairs={{0,8},{4,12},{8,0},{12,4},{1,9},{5,13},{9,1},{13,5},{2,10},{6,14},... | collective-permute-start | bytes 393224 | tf_op jit(solution)/shard_map/ppermute | solution.py:510
  110.7 25.6 %collective-permute-start.30 = (bf16[3,96,1024]{2,1,0:T(8,128)(2,1)S(1)}, bf16[3,96,1024]{2,1,0:T(8,128)(2,1)S(1)}, u32[]{:S(2)}, u32[]{:S(2)}) collective-permute-start(bf16[3,96,1024]{2,1,0:T(8,128)(2,1)S(1)} %get-tuple-element.166), channel_id=1, source_target_pairs={{0,2},{1,3},{2,0},{3,1},{16,18},{17,19},{18,16},{19,17},{4,6},{5,7... | collective-permute-start | bytes 1769480 | tf_op jit(solution)/shard_map/ppermute | solution.py:513
  111.2 26.5 %collective-permute-start.31 = (bf16[3,96,1024]{2,1,0:T(8,128)(2,1)S(1)}, bf16[3,96,1024]{2,1,0:T(8,128)(2,1)S(1)}, u32[]{:S(2)}, u32[]{:S(2)}) collective-permute-start(bf16[3,96,1024]{2,1,0:T(8,128)(2,1)S(1)} %get-tuple-element.168), channel_id=1, source_target_pairs={{0,16},{1,17},{2,18},{3,19},{16,0},{17,1},{18,2},{19,3},{4,20},{5,... | collective-permute-start | bytes 1769480 | tf_op jit(solution)/shard_map/ppermute | solution.py:513
  120.9 16.8 %collective-permute-start.32 = (bf16[3,96,1024]{2,1,0:T(8,128)(2,1)S(1)}, bf16[3,96,1024]{2,1,0:T(8,128)(2,1)S(1)}, u32[]{:S(2)}, u32[]{:S(2)}) collective-permute-start(bf16[3,96,1024]{2,1,0:T(8,128)(2,1)S(1)} %get-tuple-element.170), channel_id=1, source_target_pairs={{0,18},{1,19},{2,16},{3,17},{16,2},{17,3},{18,0},{19,1},{4,22},{5,... | collective-permute-start | bytes 1769480 | tf_op jit(solution)/shard_map/ppermute | solution.py:513
  142.5 11.2 %collective-permute-start.43 = (bf16[2,128,768]{2,1,0:T(8,128)(2,1)S(1)}, bf16[2,128,768]{2,1,0:T(8,128)(2,1)S(1)}, u32[]{:S(2)}, u32[]{:S(2)}) collective-permute-start(bf16[2,128,768]{2,1,0:T(8,128)(2,1)S(1)} %get-tuple-element.197), channel_id=1, source_target_pairs={{0,2},{1,3},{2,0},{3,1},{16,18},{17,19},{18,16},{19,17},{4,6},{5,7... | collective-permute-start | bytes 1179656 | tf_op jit(solution)/shard_map/ppermute | solution.py:513
  146.9 16.5 %collective-permute-start.33 = (bf16[560,256]{1,0:T(8,128)(2,1)S(1)}, bf16[560,256]{1,0:T(8,128)(2,1)S(1)}, u32[]{:S(2)}, u32[]{:S(2)}) collective-permute-start(bf16[560,256]{1,0:T(8,128)(2,1)S(1)} %get-tuple-element.175), channel_id=1, source_target_pairs={{0,4},{4,0},{8,12},{12,8},{1,5},{5,1},{9,13},{13,9},{2,6},{6,2},{1... | collective-permute-start | bytes 860168 | tf_op jit(solution)/shard_map/ppermute | solution.py:510
  148.6 23.0 %collective-permute-start.34 = (bf16[560,256]{1,0:T(8,128)(2,1)S(1)}, bf16[560,256]{1,0:T(8,128)(2,1)S(1)}, u32[]{:S(2)}, u32[]{:S(2)}) collective-permute-start(bf16[560,256]{1,0:T(8,128)(2,1)S(1)} %get-tuple-element.176), channel_id=1, source_target_pairs={{0,8},{4,12},{8,0},{12,4},{1,9},{5,13},{9,1},{13,5},{2,10},{6,14},... | collective-permute-start | bytes 860168 | tf_op jit(solution)/shard_map/ppermute | solution.py:510
  149.0 22.6 %collective-permute-start.35 = (bf16[560,256]{1,0:T(8,128)(2,1)S(1)}, bf16[560,256]{1,0:T(8,128)(2,1)S(1)}, u32[]{:S(2)}, u32[]{:S(2)}) collective-permute-start(bf16[560,256]{1,0:T(8,128)(2,1)S(1)} %get-tuple-element.177), channel_id=1, source_target_pairs={{0,12},{4,8},{8,4},{12,0},{1,13},{5,9},{9,5},{13,1},{2,14},{6,10},... | collective-permute-start | bytes 860168 | tf_op jit(solution)/shard_map/ppermute | solution.py:510
  (60 other events, 578.4 us)
